TPU v7x, 1024 devices: a whole 4x4x32 slice. The times are simulated.
1024 devices in a mesh: dp: 128 (over y, z), tensor: 8 (over x, core).
Axes of the slice: x: 4, y: 4, z: 32, core: 2. Of those that a mesh axis runs over, the one named last changes fastest.
Arguments:
- hidden_states: bfloat16 [32768, 4096], P('dp'), may hold values from -120 to 120
- key_cotangent: bfloat16 [32768, 1024], P('dp', 'tensor'), may hold values from -0.04 to 0.04
- norm_gain: float32 [4096], replicated, may hold values from 0.1 to 1.9
- key_weight: bfloat16 [4096, 1024], P(None, 'tensor'), may hold values from -0.09375 to 0.09375
Outputs:
- merged_key_grad: bfloat16 [4096, 1024], P('dp', 'tensor')
- merged_gain_grad: bfloat16 [4096], P('dp')
All inputs are finite; a program needn't handle non-finite values.
Results may differ from a plain program's by a relative error of at most 0.0065.
Values may be sent and summed in bfloat16 or wider, within the bound.
No kernel may reach another device: no remote copies, remote signals or barrier semaphores. Data moves between devices by JAX's collectives and lax.ppermute only.
A program may use at most 32 MiB of HBM per device.

v0:
```python
import jax
import jax.numpy as jnp
from jax import lax
from jax.sharding import PartitionSpec as P

eps_norm = 1e-05
eps_merge = 1e-06


def swapped(x, axis, apart):
    return lax.ppermute(x, axis, [(i, i ^ 1 << apart) for i in range(lax.axis_size(axis))])


def stat_terms(low_key, high_key, low_gain, high_gain, weight):
    low_wide = low_key.astype(jnp.float32)
    high_wide = high_key.astype(jnp.float32)
    low_gw = low_gain.astype(jnp.float32)
    high_gw = high_gain.astype(jnp.float32)
    return jnp.stack(
        [
            jnp.sum(low_wide * high_wide),
            jnp.sum(low_wide * low_wide),
            jnp.sum(high_wide * high_wide),
            weight * jnp.sum(low_gw * high_gw),
            weight * jnp.sum(low_gw * low_gw),
            weight * jnp.sum(high_gw * high_gw),
        ]
    )


def combine_pair(low_key, high_key, low_gain, high_gain, totals):
    low_wide = low_key.astype(jnp.float32)
    high_wide = high_key.astype(jnp.float32)
    low_gw = low_gain.astype(jnp.float32)
    high_gw = high_gain.astype(jnp.float32)
    new_key = (1.0 - totals[0] / (2.0 * (totals[1] + eps_merge))) * low_wide + (
        1.0 - totals[0] / (2.0 * (totals[2] + eps_merge))
    ) * high_wide
    new_gain = (1.0 - totals[3] / (2.0 * (totals[4] + eps_merge))) * low_gw + (
        1.0 - totals[3] / (2.0 * (totals[5] + eps_merge))
    ) * high_gw
    return (new_key.astype(jnp.bfloat16), new_gain.astype(jnp.bfloat16))


def body(hidden_states, key_cotangent, norm_gain, key_weight):
    wide_rows = hidden_states.astype(jnp.float32)
    inv_rms = lax.rsqrt(jnp.mean(wide_rows * wide_rows, axis=1, keepdims=True) + eps_norm)
    normed = wide_rows * inv_rms
    inputs = (normed * norm_gain).astype(jnp.bfloat16)
    grad_key = lax.dot_general(
        inputs, key_cotangent, (((0,), (0,)), ((), ())), preferred_element_type=jnp.float32
    ).astype(jnp.bfloat16)
    input_grad = lax.dot_general(
        key_cotangent, key_weight, (((1,), (1,)), ((), ())), preferred_element_type=jnp.float32
    )
    partial_gain = jnp.sum(input_grad * normed, axis=0)
    grad_gain = lax.psum(partial_gain, "tensor").astype(jnp.bfloat16)
    replicas = lax.axis_size("dp")
    section_count = replicas.bit_length() - 1
    replica = lax.axis_index("dp")
    leader = (lax.axis_index("tensor") == 0).astype(jnp.float32)
    width_all = grad_key.shape[0]
    own_rows = width_all // replicas
    for section_bit in range(section_count):
        other_key, other_gain = swapped((grad_key, grad_gain), "dp", section_bit)
        upper = replica >> section_bit & 1 == 1
        low_key = jnp.where(upper, other_key, grad_key)
        high_key = jnp.where(upper, grad_key, other_key)
        low_gain = jnp.where(upper, other_gain, grad_gain)
        high_gain = jnp.where(upper, grad_gain, other_gain)
        local_terms = stat_terms(low_key, high_key, low_gain, high_gain, leader)
        totals = lax.psum(local_terms, "tensor")
        grad_key, grad_gain = combine_pair(low_key, high_key, low_gain, high_gain, totals)
    merged_key = lax.dynamic_slice_in_dim(grad_key, replica * own_rows, own_rows, 0)
    merged_gain = lax.dynamic_slice_in_dim(grad_gain, replica * own_rows, own_rows, 0)
    return (merged_key, merged_gain)


def solution(mesh):
    return jax.shard_map(
        body,
        mesh=mesh,
        in_specs=(P("dp", None), P("dp", "tensor"), P(), P(None, "tensor")),
        out_specs=(P("dp", "tensor"), P("dp")),
        check_vma=False,
    )
```

profile of v0, /device:TPU:273, one launch (start us, length us, event | category | flops | bytes accessed | tf_op | source)
XLA Modules:
  0.0 766.3 jit_solution(844278539271346332)
XLA Ops:
  0.7 2.2 fusion.2
  4.8 3.5 collective-permute-start
  9.2 22.7 %psum.56 = bf16[4096]{0:T(1024)(128)(2,1)S(1)} all-reduce(f32[4096]{0:T(1024)S(1)} %fusion.36), channel_id=1, replica_groups=mesh['dp'=128,'tensor'=8] {'tensor'}, use_global_device_ids=true, to_apply=%region_5.6 | all-reduce | flops 4096 | bytes 24576 | tf_op jit(solution)/shard_map/psum | solution.py:57
  33.9 2.5 collective-permute-done.1
  39.0 3.7 fusion.7
  44.7 16.5 %psum.57 = f32[6]{0:T(128)S(1)} all-reduce(f32[6]{0:T(128)S(1)} %stack.153), channel_id=1, replica_groups=mesh['dp'=128,'tensor'=8] {'tensor'}, use_global_device_ids=true, to_apply=%region_9.10 | all-reduce | flops 6 | bytes 48 | tf_op jit(solution)/shard_map/psum | solution.py:72
  66.0 4.9 collective-permute-start.2
  75.4 41.8 %collective-permute-done.3 = bf16[4096]{0:T(1024)(128)(2,1)S(1)} collective-permute-done((bf16[4096]{0:T(1024)(128)(2,1)S(1)}, bf16[4096]{0:T(1024)(128)(2,1)S(1)}, u32[]{:S(2)}, u32[]{:S(2)}) %collective-permute-start.3) | collective-permute-done | bytes 8224 | tf_op jit(solution)/shard_map/ppermute | solution.py:11
  119.8 3.7 fusion.12
  123.5 2.0 stack.160
  125.5 12.2 %psum.58 = f32[6]{0:T(128)S(1)} all-reduce(f32[6]{0:T(128)S(1)} %stack.160), channel_id=1, replica_groups=mesh['dp'=128,'tensor'=8] {'tensor'}, use_global_device_ids=true, to_apply=%region_16.17 | all-reduce | flops 6 | bytes 48 | tf_op jit(solution)/shard_map/psum | solution.py:72
  142.4 8.8 %collective-permute-start.4 = (bf16[4096,128]{1,0:T(8,128)(2,1)S(1)}, bf16[4096,128]{1,0:T(8,128)(2,1)}, u32[]{:S(2)}, u32[]{:S(2)}) collective-permute-start(bf16[4096,128]{1,0:T(8,128)(2,1)S(1)} %fusion.10), channel_id=1, source_target_pairs={{0,32},{8,40},{16,48},{24,56},{32,0},{40,8},{48,16},{56,24},{64,96... | collective-permute-start | bytes 3145736 | tf_op jit(solution)/shard_map/ppermute | solution.py:11
  155.7 86.3 %collective-permute-done.5 = bf16[4096]{0:T(1024)(128)(2,1)S(1)} collective-permute-done((bf16[4096]{0:T(1024)(128)(2,1)S(1)}, bf16[4096]{0:T(1024)(128)(2,1)S(1)}, u32[]{:S(2)}, u32[]{:S(2)}) %collective-permute-start.5) | collective-permute-done | bytes 8224 | tf_op jit(solution)/shard_map/ppermute | solution.py:11
  244.7 3.7 fusion.17
  250.4 12.2 %psum.59 = f32[6]{0:T(128)S(1)} all-reduce(f32[6]{0:T(128)S(1)} %stack.167), channel_id=1, replica_groups=mesh['dp'=128,'tensor'=8] {'tensor'}, use_global_device_ids=true, to_apply=%region_23.24 | all-reduce | flops 6 | bytes 48 | tf_op jit(solution)/shard_map/psum | solution.py:72
  271.8 12.1 %collective-permute-start.7 = (bf16[4096]{0:T(1024)(128)(2,1)S(1)}, bf16[4096]{0:T(1024)(128)(2,1)S(1)}, u32[]{:S(2)}, u32[]{:S(2)}) collective-permute-start(bf16[4096]{0:T(1024)(128)(2,1)S(1)} %fusion.49), channel_id=1, source_target_pairs={{0,64},{8,72},{16,80},{24,88},{32,96},{40,104},{48,112},{56,120},{... | collective-permute-start | bytes 24584 | tf_op jit(solution)/shard_map/ppermute | solution.py:11
  283.9 189.1 %collective-permute-done.7 = bf16[4096]{0:T(1024)(128)(2,1)S(1)} collective-permute-done((bf16[4096]{0:T(1024)(128)(2,1)S(1)}, bf16[4096]{0:T(1024)(128)(2,1)S(1)}, u32[]{:S(2)}, u32[]{:S(2)}) %collective-permute-start.7) | collective-permute-done | bytes 8224 | tf_op jit(solution)/shard_map/ppermute | solution.py:11
  475.6 3.7 fusion.22
  481.3 12.3 %psum.60 = f32[6]{0:T(128)S(1)} all-reduce(f32[6]{0:T(128)S(1)} %stack.174), channel_id=1, replica_groups=mesh['dp'=128,'tensor'=8] {'tensor'}, use_global_device_ids=true, to_apply=%region_30.31 | all-reduce | flops 6 | bytes 48 | tf_op jit(solution)/shard_map/psum | solution.py:72
  498.3 42.4 %collective-permute-start.8 = (bf16[4096,128]{1,0:T(8,128)(2,1)S(1)}, bf16[4096,128]{1,0:T(8,128)(2,1)}, u32[]{:S(2)}, u32[]{:S(2)}) collective-permute-start(bf16[4096,128]{1,0:T(8,128)(2,1)S(1)} %fusion.20), channel_id=1, source_target_pairs={{0,128},{8,136},{16,144},{24,152},{32,160},{40,168},{48,176},{56,1... | collective-permute-start | bytes 3145736 | tf_op jit(solution)/shard_map/ppermute | solution.py:11
  545.2 87.6 %collective-permute-done.9 = bf16[4096]{0:T(1024)(128)(2,1)S(1)} collective-permute-done((bf16[4096]{0:T(1024)(128)(2,1)S(1)}, bf16[4096]{0:T(1024)(128)(2,1)S(1)}, u32[]{:S(2)}, u32[]{:S(2)}) %collective-permute-start.9) | collective-permute-done | bytes 8224 | tf_op jit(solution)/shard_map/ppermute | solution.py:11
  635.5 3.7 fusion.27
  641.2 12.2 %psum.61 = f32[6]{0:T(128)S(1)} all-reduce(f32[6]{0:T(128)S(1)} %stack.181), channel_id=1, replica_groups=mesh['dp'=128,'tensor'=8] {'tensor'}, use_global_device_ids=true, to_apply=%region_37.38 | all-reduce | flops 6 | bytes 48 | tf_op jit(solution)/shard_map/psum | solution.py:72
  658.1 2.9 collective-permute-start.10
  663.6 2.6 collective-permute-start.11
  666.2 18.1 %collective-permute-done.11 = bf16[4096]{0:T(1024)(128)(2,1)S(1)} collective-permute-done((bf16[4096]{0:T(1024)(128)(2,1)S(1)}, bf16[4096]{0:T(1024)(128)(2,1)S(1)}, u32[]{:S(2)}, u32[]{:S(2)}) %collective-permute-start.11) | collective-permute-done | bytes 8224 | tf_op jit(solution)/shard_map/ppermute | solution.py:11
  686.9 3.7 fusion.32
  692.6 13.3 %psum.62 = f32[6]{0:T(128)S(1)} all-reduce(f32[6]{0:T(128)S(1)} %stack.188), channel_id=1, replica_groups=mesh['dp'=128,'tensor'=8] {'tensor'}, use_global_device_ids=true, to_apply=%region_44.45 | all-reduce | flops 6 | bytes 48 | tf_op jit(solution)/shard_map/psum | solution.py:72
  715.2 4.8 collective-permute-start.13
  720.0 18.4 %collective-permute-done.13 = bf16[4096]{0:T(1024)(128)(2,1)S(1)} collective-permute-done((bf16[4096]{0:T(1024)(128)(2,1)S(1)}, bf16[4096]{0:T(1024)(128)(2,1)S(1)}, u32[]{:S(2)}, u32[]{:S(2)}) %collective-permute-start.13) | collective-permute-done | bytes 8224 | tf_op jit(solution)/shard_map/ppermute | solution.py:11
  741.0 3.0 multiply_reduce_fusion
  745.9 13.2 %psum.63 = f32[6]{0:T(128)S(1)} all-reduce(f32[6]{0:T(128)S(1)} %stack.195), channel_id=1, replica_groups=mesh['dp'=128,'tensor'=8] {'tensor'}, use_global_device_ids=true, to_apply=%region_51.52 | all-reduce | flops 6 | bytes 48 | tf_op jit(solution)/shard_map/psum | solution.py:72
  (61 shorter events, 47.1 us)
Async XLA Ops:
  0.6 7.8 %copy-start = (bf16[4096,128]{1,0:T(8,128)(2,1)S(1)}, bf16[4096,128]{1,0:T(8,128)(2,1)}, u32[]{:S(2)}) copy-start(bf16[4096,128]{1,0:T(8,128)(2,1)} %param.7) | copy-start | bytes 3145732
  0.6 2.3 copy-start.2
  3.0 5.5 copy-start.3
  4.8 34.2 %collective-permute-start = (bf16[4096,128]{1,0:T(8,128)(2,1)S(1)}, bf16[4096,128]{1,0:T(8,128)(2,1)}, u32[]{:S(2)}, u32[]{:S(2)}) collective-permute-start(bf16[4096,128]{1,0:T(8,128)(2,1)S(1)} %convolution_convert_fusion), channel_id=1, source_target_pairs={{0,8},{8,0},{16,24},{24,16},{32,40},{40,32},{48,56},{56,48},{64,72... | collective-permute-start | bytes 3145736 | tf_op jit(solution)/shard_map/ppermute | solution.py:11
  32.0 4.4 collective-permute-start.1
  66.0 53.9 %collective-permute-start.2 = (bf16[4096,128]{1,0:T(8,128)(2,1)S(1)}, bf16[4096,128]{1,0:T(8,128)(2,1)}, u32[]{:S(2)}, u32[]{:S(2)}) collective-permute-start(bf16[4096,128]{1,0:T(8,128)(2,1)S(1)} %fusion.5), channel_id=1, source_target_pairs={{0,16},{8,24},{16,0},{24,8},{32,48},{40,56},{48,32},{56,40},{64,80... | collective-permute-start | bytes 3145736 | tf_op jit(solution)/shard_map/ppermute | solution.py:11
  73.5 43.7 %collective-permute-start.3 = (bf16[4096]{0:T(1024)(128)(2,1)S(1)}, bf16[4096]{0:T(1024)(128)(2,1)S(1)}, u32[]{:S(2)}, u32[]{:S(2)}) collective-permute-start(bf16[4096]{0:T(1024)(128)(2,1)S(1)} %fusion.39), channel_id=1, source_target_pairs={{0,16},{8,24},{16,0},{24,8},{32,48},{40,56},{48,32},{56,40},{64,80... | collective-permute-start | bytes 24584 | tf_op jit(solution)/shard_map/ppermute | solution.py:11
  142.4 102.3 %collective-permute-start.4 = (bf16[4096,128]{1,0:T(8,128)(2,1)S(1)}, bf16[4096,128]{1,0:T(8,128)(2,1)}, u32[]{:S(2)}, u32[]{:S(2)}) collective-permute-start(bf16[4096,128]{1,0:T(8,128)(2,1)S(1)} %fusion.10), channel_id=1, source_target_pairs={{0,32},{8,40},{16,48},{24,56},{32,0},{40,8},{48,16},{56,24},{64,96... | collective-permute-start | bytes 3145736 | tf_op jit(solution)/shard_map/ppermute | solution.py:11
  153.8 88.2 %collective-permute-start.5 = (bf16[4096]{0:T(1024)(128)(2,1)S(1)}, bf16[4096]{0:T(1024)(128)(2,1)S(1)}, u32[]{:S(2)}, u32[]{:S(2)}) collective-permute-start(bf16[4096]{0:T(1024)(128)(2,1)S(1)} %fusion.44), channel_id=1, source_target_pairs={{0,32},{8,40},{16,48},{24,56},{32,0},{40,8},{48,16},{56,24},{64,96... | collective-permute-start | bytes 24584 | tf_op jit(solution)/shard_map/ppermute | solution.py:11
  267.3 208.3 %collective-permute-start.6 = (bf16[4096,128]{1,0:T(8,128)(2,1)S(1)}, bf16[4096,128]{1,0:T(8,128)(2,1)}, u32[]{:S(2)}, u32[]{:S(2)}) collective-permute-start(bf16[4096,128]{1,0:T(8,128)(2,1)S(1)} %fusion.15), channel_id=1, source_target_pairs={{0,64},{8,72},{16,80},{24,88},{32,96},{40,104},{48,112},{56,120},{... | collective-permute-start | bytes 3145736 | tf_op jit(solution)/shard_map/ppermute | solution.py:11
  271.8 201.2 %collective-permute-start.7 = (bf16[4096]{0:T(1024)(128)(2,1)S(1)}, bf16[4096]{0:T(1024)(128)(2,1)S(1)}, u32[]{:S(2)}, u32[]{:S(2)}) collective-permute-start(bf16[4096]{0:T(1024)(128)(2,1)S(1)} %fusion.49), channel_id=1, source_target_pairs={{0,64},{8,72},{16,80},{24,88},{32,96},{40,104},{48,112},{56,120},{... | collective-permute-start | bytes 24584 | tf_op jit(solution)/shard_map/ppermute | solution.py:11
  498.3 137.2 %collective-permute-start.8 = (bf16[4096,128]{1,0:T(8,128)(2,1)S(1)}, bf16[4096,128]{1,0:T(8,128)(2,1)}, u32[]{:S(2)}, u32[]{:S(2)}) collective-permute-start(bf16[4096,128]{1,0:T(8,128)(2,1)S(1)} %fusion.20), channel_id=1, source_target_pairs={{0,128},{8,136},{16,144},{24,152},{32,160},{40,168},{48,176},{56,1... | collective-permute-start | bytes 3145736 | tf_op jit(solution)/shard_map/ppermute | solution.py:11
  543.3 89.6 %collective-permute-start.9 = (bf16[4096]{0:T(1024)(128)(2,1)S(1)}, bf16[4096]{0:T(1024)(128)(2,1)S(1)}, u32[]{:S(2)}, u32[]{:S(2)}) collective-permute-start(bf16[4096]{0:T(1024)(128)(2,1)S(1)} %fusion.54), channel_id=1, source_target_pairs={{0,128},{8,136},{16,144},{24,152},{32,160},{40,168},{48,176},{56,1... | collective-permute-start | bytes 24584 | tf_op jit(solution)/shard_map/ppermute | solution.py:11
  658.1 28.8 %collective-permute-start.10 = (bf16[4096,128]{1,0:T(8,128)(2,1)S(1)}, bf16[4096,128]{1,0:T(8,128)(2,1)}, u32[]{:S(2)}, u32[]{:S(2)}) collective-permute-start(bf16[4096,128]{1,0:T(8,128)(2,1)S(1)} %fusion.25), channel_id=1, source_target_pairs={{0,256},{8,264},{16,272},{24,280},{32,288},{40,296},{48,304},{56,3... | collective-permute-start | bytes 3145736 | tf_op jit(solution)/shard_map/ppermute | solution.py:11
  663.6 20.6 %collective-permute-start.11 = (bf16[4096]{0:T(1024)(128)(2,1)S(1)}, bf16[4096]{0:T(1024)(128)(2,1)S(1)}, u32[]{:S(2)}, u32[]{:S(2)}) collective-permute-start(bf16[4096]{0:T(1024)(128)(2,1)S(1)} %fusion.59), channel_id=1, source_target_pairs={{0,256},{8,264},{16,272},{24,280},{32,288},{40,296},{48,304},{56,3... | collective-permute-start | bytes 24584 | tf_op jit(solution)/shard_map/ppermute | solution.py:11
  710.6 30.3 %copy-start.1 = (bf16[4096,128]{1,0:T(8,128)(2,1)}, bf16[4096,128]{1,0:T(8,128)(2,1)S(1)}, u32[]{:S(2)}) copy-start(bf16[4096,128]{1,0:T(8,128)(2,1)S(1)} %fusion.30) | copy-start | bytes 3145732
  710.6 30.3 %collective-permute-start.12 = (bf16[4096,128]{1,0:T(8,128)(2,1)S(1)}, bf16[4096,128]{1,0:T(8,128)(2,1)}, u32[]{:S(2)}, u32[]{:S(2)}) collective-permute-start(bf16[4096,128]{1,0:T(8,128)(2,1)S(1)} %fusion.30), channel_id=1, source_target_pairs={{0,512},{8,520},{16,528},{24,536},{32,544},{40,552},{48,560},{56,5... | collective-permute-start | bytes 3145736 | tf_op jit(solution)/shard_map/ppermute | solution.py:11
  715.2 23.2 %collective-permute-start.13 = (bf16[4096]{0:T(1024)(128)(2,1)S(1)}, bf16[4096]{0:T(1024)(128)(2,1)S(1)}, u32[]{:S(2)}, u32[]{:S(2)}) collective-permute-start(bf16[4096]{0:T(1024)(128)(2,1)S(1)} %fusion.64), channel_id=1, source_target_pairs={{0,512},{8,520},{16,528},{24,536},{32,544},{40,552},{48,560},{56,5... | collective-permute-start | bytes 24584 | tf_op jit(solution)/shard_map/ppermute | solution.py:11
where the time goes:
time: 768 us; the launch traced here: 766 us
  waiting for transfers between devices  444 us (58%)
  blocking collectives  114 us (15%)
  starting transfers between devices  93.6 us (12%)
  between operations  50 us (7%)
  other arithmetic  43.3 us (6%)
  local copies, waits for them, and re-layouts  18.6 us (2%)
    ppermute x14, waiting for transfers between devices, swapped(): lax.ppermute(x, axis, [(i, i ^ 1 << apart) for i in range(lax.axis_size(a...  444 us
    ppermute x14, starting transfers between devices, swapped(): lax.ppermute(x, axis, [(i, i ^ 1 << apart) for i in range(lax.axis_size(a...  93.6 us
    psum x7, blocking collectives, body(): totals = lax.psum(local_terms, 'tensor')  91.7 us
    reduce_sum x7, other arithmetic, stat_terms(): jnp.sum(high_wide * high_wide)  25 us
    psum x1, blocking collectives, body(): grad_gain = lax.psum(partial_gain, 'tensor').astype(jnp.bfloat16)  22.7 us
  transfers between devices with their start and end apart: 14, of which 7 were waited for; matrix products, arithmetic and copies ran while one was open for 1% of the time, Pallas kernels for 0%

commit v1 on v0

v1 whole, which is shorter than its diff:
```python
import jax
import jax.numpy as jnp
from jax import lax
from jax.experimental import pallas as pl
from jax.experimental.pallas import tpu as pltpu
from jax.sharding import Mesh
from jax.sharding import PartitionSpec as P

eps_norm = 1e-05
eps_merge = 1e-06

f32 = jnp.float32
bf16 = jnp.bfloat16

NEAR = 4
FAR = 32
FAR_Z = 8
WIDTH = 8
PIECE = 32
LANES = 128
VMEM_SPEC = pl.BlockSpec(memory_space=pltpu.VMEM)
SMEM_SPEC = pl.BlockSpec(memory_space=pltpu.SMEM)


def factor(cross, own_sq):
    return 1.0 - cross / (2.0 * (jnp.maximum(own_sq, 0.0) + eps_merge))


def grads_kernel(place, hidden, cot, gain, weight, p0, p1, p2, p3, gain_out, inv_wide, pieces):
    tokens, width = hidden.shape
    blocks = width // LANES
    half = tokens // 2
    for part in range(2):
        rows = pl.ds(part * half, half)
        total = jnp.zeros((half, LANES), f32)
        for block in range(blocks):
            x = hidden[rows, pl.ds(block * LANES, LANES)].astype(f32)
            total = total + x * x
        mean = jnp.sum(total, axis=1, keepdims=True) * (1.0 / width)
        inv_wide[rows, :] = jnp.broadcast_to(lax.rsqrt(mean + eps_norm), (half, LANES))
    step = 4 * LANES
    for chunk in range(width // step):
        inv = inv_wide[...]
        normed = []
        inputs = []
        for sub in range(4):
            block = 4 * chunk + sub
            x = hidden[:, pl.ds(block * LANES, LANES)].astype(f32) * inv
            normed.append(x)
            inputs.append((x * gain[pl.ds(block, 1), :]).astype(bf16))
        grad = lax.dot_general(
            jnp.concatenate(inputs, axis=1),
            cot[...],
            (((0,), (0,)), ((), ())),
            preferred_element_type=f32,
        ).astype(bf16)
        back = lax.dot_general(
            cot[...],
            weight[pl.ds(chunk * step, step), :],
            (((1,), (1,)), ((), ())),
            preferred_element_type=f32,
        )
        for sub in range(4):
            block = 4 * chunk + sub
            for near in range(NEAR):
                at = sub * LANES + near * PIECE
                pieces[near, pl.ds(block * PIECE, PIECE), :] = grad[at : at + PIECE]
            row = jnp.sum(
                back[:, sub * LANES : (sub + 1) * LANES] * normed[sub], axis=0, keepdims=True
            )
            for other in range(WIDTH):
                gain_out[other, pl.ds(block, 1), :] = row
    here = place[0]
    for apart, out in enumerate((p0, p1, p2, p3)):
        out[...] = pieces[here ^ apart]


def local_grads(place, hidden, cot, gain, weight):
    piece = jax.ShapeDtypeStruct((FAR * PIECE, LANES), bf16)
    return pl.pallas_call(
        grads_kernel,
        out_shape=[piece] * NEAR + [jax.ShapeDtypeStruct((WIDTH, FAR, LANES), f32)],
        in_specs=[SMEM_SPEC] + [VMEM_SPEC] * 4,
        out_specs=[VMEM_SPEC] * (NEAR + 1),
        scratch_shapes=[
            pltpu.VMEM((hidden.shape[0], LANES), f32),
            pltpu.VMEM((NEAR, FAR * PIECE, LANES), bf16),
        ],
        compiler_params=pltpu.CompilerParams(vmem_limit_bytes=32 << 20),
        name="local_grads",
    )(place, hidden, cot, gain, weight)


def all_sum(x):
    return jnp.sum(jnp.sum(x, axis=0, keepdims=True), axis=1, keepdims=True)


def near_dots_kernel(place, p0, p1, p2, p3, out):
    refs = (p0, p1, p2, p3)
    pairs = [(a, b) for a in range(NEAR) for b in range(a, NEAR)]
    rows = 64

    def add(step, totals):
        values = [ref[pl.ds(step * rows, rows), :].astype(f32) for ref in refs]
        return tuple(
            total + jnp.sum((values[a] * values[b]).reshape(rows // 8, 8, LANES), axis=0)
            for total, (a, b) in zip(totals, pairs)
        )

    totals = lax.fori_loop(
        0, p0.shape[0] // rows, add, tuple(jnp.zeros((8, LANES), f32) for _ in pairs)
    )
    here = place[0]
    lane = lax.broadcasted_iota(jnp.int32, (1, LANES), 1)
    row = jnp.zeros((1, LANES), f32)
    for total, (a, b) in zip(totals, pairs):
        dot = all_sum(total)
        row = jnp.where(lane == ((NEAR * a + b) ^ (5 * here)), dot, row)
        row = jnp.where(lane == ((NEAR * b + a) ^ (5 * here)), dot, row)
    out[...] = jnp.broadcast_to(row.reshape(1, 1, LANES), out.shape)


def near_dots(place, pieces):
    return pl.pallas_call(
        near_dots_kernel,
        out_shape=jax.ShapeDtypeStruct((NEAR * WIDTH, 1, LANES), f32),
        in_specs=[SMEM_SPEC] + [VMEM_SPEC] * NEAR,
        out_specs=VMEM_SPEC,
        name="near_dots",
    )(place, *pieces)


def near_shares(dots):
    low = (factor(dots[0][1], dots[0][0]), factor(dots[0][1], dots[1][1]))
    high = (factor(dots[2][3], dots[2][2]), factor(dots[2][3], dots[3][3]))
    low_sq = (
        low[0] * low[0] * dots[0][0]
        + 2.0 * (low[0] * low[1] * dots[0][1])
        + low[1] * low[1] * dots[1][1]
    )
    high_sq = (
        high[0] * high[0] * dots[2][2]
        + 2.0 * (high[0] * high[1] * dots[2][3])
        + high[1] * high[1] * dots[3][3]
    )
    cross = low[0] * (high[0] * dots[0][2] + high[1] * dots[0][3]) + low[1] * (
        high[0] * dots[1][2] + high[1] * dots[1][3]
    )
    of_low = factor(cross, low_sq)
    of_high = factor(cross, high_sq)
    return (of_low * low[0], of_low * low[1], of_high * high[0], of_high * high[1])


def near_merge_kernel(place, dots, gains, p0, p1, p2, p3, out):
    here = place[0]
    row = jnp.sum(dots[...], axis=0)
    lane = lax.broadcasted_iota(jnp.int32, (1, LANES), 1)

    def entry(a, b):
        return jnp.sum(jnp.where(lane == NEAR * a + b, row, 0.0), axis=1, keepdims=True)

    shares = near_shares([[entry(a, b) if a <= b else None for b in range(NEAR)] for a in range(NEAR)])
    by_apart = []
    for apart in range(NEAR):
        share = shares[apart]
        for other in range(1, NEAR):
            share = jnp.where(here == other, shares[other ^ apart], share)
        by_apart.append(share)
    for far in range(FAR):
        rows = pl.ds(far * PIECE, PIECE)
        total = by_apart[0] * p0[rows, :].astype(f32)
        for share, ref in zip(by_apart[1:], (p1, p2, p3)):
            total = total + share * ref[rows, :].astype(f32)
        out[far, pl.ds(0, PIECE), :] = total.astype(bf16)

    gain = [gains[near] for near in range(NEAR)]
    gain_shares = near_shares(
        [[all_sum(gain[a] * gain[b]) if a <= b else None for b in range(NEAR)] for a in range(NEAR)]
    )
    merged = gain_shares[0] * gain[0]
    for near in range(1, NEAR):
        merged = merged + gain_shares[near] * gain[near]
    for far in range(FAR):
        out[far, pl.ds(PIECE, 8), :] = jnp.broadcast_to(merged[far : far + 1], (8, LANES)).astype(bf16)


def near_merge(place, dots, gains, pieces):
    return pl.pallas_call(
        near_merge_kernel,
        out_shape=jax.ShapeDtypeStruct((FAR, PIECE + 8, LANES), bf16),
        in_specs=[SMEM_SPEC] + [VMEM_SPEC] * (2 + NEAR),
        out_specs=VMEM_SPEC,
        name="near_merge",
    )(place, dots, gains, *pieces)


def packed(dots):
    total = dots[0:8]
    for block in range(1, 4):
        total = total + pltpu.roll(dots[8 * block : 8 * block + 8], 32 * block, 1)
    return total


def unpacked(rows):
    lane = lax.broadcasted_iota(jnp.int32, (8, LANES), 1)
    blocks = []
    for block in range(4):
        moved = rows if block == 0 else pltpu.roll(rows, LANES - 32 * block, 1)
        blocks.append(jnp.where(lane < FAR, moved, 0.0))
    return jnp.concatenate(blocks, axis=0)


def far_dots_kernel(values, key_out, gain_out, by_row, wide):
    for far in range(FAR):
        wide[pl.ds(far * (PIECE + 8), PIECE + 8), :] = values[far].astype(f32)
    columns = []
    for row in range(PIECE + 1):
        block = wide[pl.ds(row, FAR, stride=PIECE + 8), :]
        by_row[pl.ds(row * FAR, FAR), :] = block
        columns.append(block.astype(bf16))

    def dots(matrix):
        padded = jnp.concatenate(
            [matrix, jnp.zeros((LANES - FAR, matrix.shape[1]), bf16)], axis=0
        )
        return lax.dot_general(
            matrix, padded, (((1,), (1,)), ((), ())), preferred_element_type=f32
        )

    key_rows = packed(dots(jnp.concatenate(columns[:PIECE], axis=1)))
    key_out[...] = jnp.broadcast_to(key_rows[None], key_out.shape)
    gain_out[...] = packed(dots(columns[PIECE]))


def far_dots(values):
    return pl.pallas_call(
        far_dots_kernel,
        out_shape=[
            jax.ShapeDtypeStruct((NEAR * WIDTH, 8, LANES), f32),
            jax.ShapeDtypeStruct((8, LANES), f32),
            jax.ShapeDtypeStruct(((PIECE + 1) * FAR, LANES), f32),
        ],
        in_specs=[VMEM_SPEC],
        out_specs=[VMEM_SPEC] * 3,
        scratch_shapes=[pltpu.VMEM((FAR * (PIECE + 8), LANES), f32)],
        name="far_dots",
    )(values)


def far_shares(dots):
    shape = dots.shape
    row = lax.broadcasted_iota(jnp.int32, shape, 0)
    lane = lax.broadcasted_iota(jnp.int32, shape, 1)
    share = jnp.ones((shape[0], 1), f32)
    for level in range(5):
        same = (row >> level) == (lane >> level)
        across = ((row >> level) ^ 1) == (lane >> level)
        own_part = jnp.sum(jnp.where(same, dots, 0.0), axis=0, keepdims=True)
        cross_part = jnp.sum(jnp.where(across, dots, 0.0), axis=0, keepdims=True)
        own_sq = jnp.sum(jnp.where(same, own_part, 0.0), axis=1, keepdims=True)
        cross = jnp.sum(jnp.where(same, cross_part, 0.0), axis=1, keepdims=True)
        scale = factor(cross, own_sq)
        share = share * scale
        if level < 4:
            scale_row = jnp.sum(jnp.where(row == lane, scale, 0.0), axis=0, keepdims=True)
            dots = dots * scale * scale_row
    return share


def far_merge_kernel(place, dots, by_row, key_out, gain_out):
    key_share = far_shares(unpacked(dots[pl.ds(0, 8), :]))
    gain_share = far_shares(unpacked(dots[pl.ds(8, 8), :]))
    key_wide = jnp.broadcast_to(key_share, (FAR, LANES))
    rows = []
    for row in range(PIECE):
        rows.append(
            jnp.sum(key_wide * by_row[pl.ds(row * FAR, FAR), :], axis=0, keepdims=True)
        )
    key_out[...] = jnp.concatenate(rows, axis=0).astype(bf16)
    gain = jnp.sum(gain_share * by_row[pl.ds(PIECE * FAR, FAR), :], axis=0, keepdims=True)
    wide = jnp.broadcast_to(gain, (8, LANES))
    moved = wide
    for near in range(1, NEAR):
        moved = jnp.where(place[0] == near, pltpu.roll(wide, LANES - PIECE * near, 1), moved)
    gain_out[...] = moved[0:1].astype(bf16)


def far_merge(place, dots, by_row):
    return pl.pallas_call(
        far_merge_kernel,
        out_shape=[
            jax.ShapeDtypeStruct((PIECE, LANES), bf16),
            jax.ShapeDtypeStruct((1, LANES), bf16),
        ],
        in_specs=[SMEM_SPEC] + [VMEM_SPEC] * 2,
        out_specs=[VMEM_SPEC] * 2,
        name="far_merge",
    )(place, dots, by_row)


def paired(x, axis, apart):
    return lax.ppermute(x, axis, [(i, i ^ apart) for i in range(lax.axis_size(axis))])


def exchanged(x, axes):
    return lax.all_to_all(x, axes, 0, 0)


def body(hidden_states, key_cotangent, norm_gain, key_weight):
    place = lax.axis_index("zl").astype(jnp.int32).reshape(1)
    *pieces, gain_parts = local_grads(
        place, hidden_states, key_cotangent, norm_gain.reshape(FAR, LANES), key_weight
    )
    with jax.named_scope("near_exchange"):
        arrived = {apart: paired(pieces[apart], "zl", apart) for apart in (2, 3, 1)}
    with jax.named_scope("gain_sum"):
        gain = jnp.sum(exchanged(gain_parts, ("x", "core")), axis=0)
        gain = lax.reduce_precision(gain, 8, 7)
        gains = exchanged(jnp.broadcast_to(gain[None], (NEAR, FAR, LANES)), "zl")
    pieces = [pieces[0]] + [arrived[apart] for apart in range(1, NEAR)]
    with jax.named_scope("near_dots_sum"):
        dots = exchanged(near_dots(place, pieces), ("zl", "x", "core"))
    values = near_merge(place, dots, gains, pieces)
    with jax.named_scope("far_exchange"):
        values = exchanged(values, ("y", "zh"))
    key_dots, gain_dots, by_row = far_dots(values)
    with jax.named_scope("far_dots_sum"):
        key_dots = jnp.sum(exchanged(key_dots, ("zl", "x", "core")), axis=0)
        dots = jnp.concatenate([key_dots, gain_dots], axis=0)
        dots = jnp.sum(exchanged(jnp.broadcast_to(dots[None], (4, 16, LANES)), "y"), axis=0)
        for apart in (1, 2, 4):
            dots = dots + paired(dots, "zh", apart)
    merged_key, merged_gain = far_merge(place, dots, by_row)
    return (merged_key, merged_gain[0, :PIECE])


def solution(mesh):
    split = Mesh(mesh.devices.reshape(4, FAR_Z, NEAR, 4, 2), ("y", "zh", "zl", "x", "core"))
    rows = ("y", "zh", "zl")
    columns = ("x", "core")
    return jax.shard_map(
        body,
        mesh=split,
        in_specs=(P(rows, None), P(rows, columns), P(), P(None, columns)),
        out_specs=(P(rows, columns), P(rows)),
        check_vma=False,
    )
```

time: 768 us -> 218 us (0.28)
  the two profiles are of different devices: /device:TPU:273 before, /device:TPU:2 now
where the time goes in v1:
time: 218 us; the launch traced here: 217 us
  blocking collectives  104 us (48%)
  starting transfers between devices  54.8 us (25%)
  waiting for transfers between devices  36.9 us (17%)
  Pallas kernels  11.7 us (5%)
  local copies, waits for them, and re-layouts  7.05 us (3%)
    all_to_all x4, blocking collectives, exchanged(): return lax.all_to_all(x, axes, 0, 0)  104 us
    ppermute x6, waiting for transfers between devices, paired(): lax.ppermute(x, axis, [(i, i ^ apart) for i in range(lax.axis_size(axis))])  29.7 us
    ppermute x6, starting transfers between devices, paired(): lax.ppermute(x, axis, [(i, i ^ apart) for i in range(lax.axis_size(axis))])  29.5 us
    all_to_all x2, starting transfers between devices, exchanged(): return lax.all_to_all(x, axes, 0, 0)  25.3 us
    all_to_all x2, waiting for transfers between devices, exchanged(): return lax.all_to_all(x, axes, 0, 0)  7.13 us
    unnamed x18, local copies, waits for them, and re-layouts  5.86 us
  transfers between devices with their start and end apart: 8, of which 6 were waited for; matrix products, arithmetic and copies ran while one was open for 0% of the time, Pallas kernels for 1%

profile of v1, /device:TPU:2, one launch (start us, length us, event | category | flops | bytes accessed | tf_op | source)
XLA Modules:
  0.0 216.7 jit_solution(18104511286640698754)
XLA Ops:
  0.6 1.6 copy-done
  2.2 1.2 copy-done.1
  3.5 0.8 copy-done.3
  4.3 0.7 copy-done.4
  5.0 2.5 %local_grads.1 = (bf16[1024,128]{1,0:T(8,128)(2,1)S(1)}, bf16[1024,128]{1,0:T(8,128)(2,1)S(1)}, bf16[1024,128]{1,0:T(8,128)(2,1)S(1)}, bf16[1024,128]{1,0:T(8,128)(2,1)S(1)}, f32[8,32,128]{2,1,0:T(8,128)}) custom-call(s32[1]{0:T(128)} %bitcast.place, bf16[256,4096]{1,0:T(8,128)(2,1)S(1)} %copy-done, bf16[256,128]{1,0:T(8,128)(2,1)S(1)} %copy-done.3, ...), custom_call_target="tpu_custom_call" | custom-call | tf_op jit(solution)/shard_map/local_grads/pallas_call | solution.py:80
  7.5 0.7 copy-done.2
  8.2 3.8 %collective-permute-start = (bf16[1024,128]{1,0:T(8,128)(2,1)S(1)}, bf16[1024,128]{1,0:T(8,128)(2,1)S(1)}, u32[]{:S(2)}, u32[]{:S(2)}) collective-permute-start(bf16[1024,128]{1,0:T(8,128)(2,1)S(1)} %get-tuple-element.13), channel_id=1, source_target_pairs={{0,8},{8,0},{16,24},{24,16},{1,9},{9,1},{17,25},{25,17},{2,10},{10... | collective-permute-start | bytes 786440 | tf_op jit(solution)/shard_map/near_exchange/ppermute | solution.py:302
  12.0 5.2 %collective-permute-start.1 = (bf16[1024,128]{1,0:T(8,128)(2,1)S(1)}, bf16[1024,128]{1,0:T(8,128)(2,1)S(1)}, u32[]{:S(2)}, u32[]{:S(2)}) collective-permute-start(bf16[1024,128]{1,0:T(8,128)(2,1)S(1)} %get-tuple-element.14), channel_id=1, source_target_pairs={{0,16},{8,24},{16,0},{24,8},{1,17},{9,25},{17,1},{25,9},{2,18},{10... | collective-permute-start | bytes 786440 | tf_op jit(solution)/shard_map/near_exchange/ppermute | solution.py:302
  17.2 1.9 collective-permute-start.2
  19.1 15.7 %all-to-all-start.1 = ((f32[8,32,128]{2,1,0:T(8,128)}), f32[8,32,128]{2,1,0:T(8,128)S(1)}, u32[]{:S(2)}, u32[]{:S(2)}) async-start(f32[8,32,128]{2,1,0:T(8,128)} %get-tuple-element.16), calls=%async_computation.1 | async-start | bytes 262144 | tf_op jit(solution)/shard_map/gain_sum/all_to_all | solution.py:306
  34.8 0.8 collective-permute-done.1.p2
  35.6 0.7 copy-done.6
  36.4 2.4 %near_dots.1 = f32[32,1,128]{2,1,0:T(1,128)} custom-call(s32[1]{0:T(128)} %bitcast.place, bf16[1024,128]{1,0:T(8,128)(2,1)} %copy-done.2, bf16[1024,128]{1,0:T(8,128)(2,1)} %copy-done.5, bf16[1024,128]{1,0:T(8,128)(2,1)} %copy-done.6, bf16[1024,128]{1,0:T(8,128)(2,1)} %copy-done.7), custom_call_target="tpu_custom_call" | custom-call | tf_op jit(solution)/shard_map/near_dots_sum/near_dots/pallas_call | solution.py:124
  38.8 0.7 all-to-all-done.1
  39.5 9.7 %all-to-all-start = ((f32[32,1,128]{2,1,0:T(1,128)}), f32[32,1,128]{2,1,0:T(1,128)S(1)}, u32[]{:S(2)}, u32[]{:S(2)}) async-start(f32[32,1,128]{2,1,0:T(1,128)} %near_dots.1), calls=%async_computation | async-start | bytes 32768 | tf_op jit(solution)/shard_map/near_dots_sum/all_to_all | solution.py:306
  49.2 6.5 %all-to-all-done.dots = f32[32,1,128]{2,1,0:T(1,128)S(1)} async-done(((f32[32,1,128]{2,1,0:T(1,128)}), f32[32,1,128]{2,1,0:T(1,128)S(1)}, u32[]{:S(2)}, u32[]{:S(2)}) %all-to-all-start) | async-done | bytes 16416 | tf_op jit(solution)/shard_map/near_dots_sum/all_to_all | solution.py:306
  55.6 8.8 %all_to_all.30.gains = f32[4,32,128]{2,1,0:T(8,128)} all-to-all(f32[4,32,128]{2,1,0:T(8,128)S(1)} %broadcast_in_dim.4), channel_id=1, replica_groups=mesh['y'=4,'zh'=8,'zl'=4,'x'=4,'core'=2] {'zl'}, dimensions={0} | all-to-all | bytes 131072 | tf_op jit(solution)/shard_map/gain_sum/all_to_all | solution.py:306
  64.4 2.3 %near_merge.1 = bf16[32,40,128]{2,1,0:T(8,128)(2,1)} custom-call(s32[1]{0:T(128)} %bitcast.place, f32[32,1,128]{2,1,0:T(1,128)} %copy-done.8, f32[4,32,128]{2,1,0:T(8,128)} %all_to_all.30.gains, bf16[1024,128]{1,0:T(8,128)(2,1)} %copy-done.2, bf16[1024,128]{1,0:T(8,128)(2,1)} %copy-done.5, bf16[1024,128]{1,0:T(8,128)(2,1)} %copy-done.6, ...), custom_call_target="tpu_custom_call" | custom-call | tf_op jit(solution)/shard_map/near_merge/pallas_call | solution.py:188
  66.7 68.6 %all_to_all.31.values = bf16[32,40,128]{2,1,0:T(8,128)(2,1)} all-to-all(bf16[32,40,128]{2,1,0:T(8,128)(2,1)} %near_merge.1), channel_id=1, replica_groups=mesh['y'=4,'zh'=8,'zl'=4,'x'=4,'core'=2] {'y','zh'}, dimensions={0} | all-to-all | bytes 655360 | tf_op jit(solution)/shard_map/far_exchange/all_to_all | solution.py:306
  135.3 2.2 far_dots.1
  137.5 17.5 %all_to_all.32 = f32[32,8,128]{2,1,0:T(8,128)S(1)} all-to-all(f32[32,8,128]{2,1,0:T(8,128)} %get-tuple-element.17), channel_id=1, replica_groups=mesh['y'=4,'zh'=8,'zl'=4,'x'=4,'core'=2] {'zl','x','core'}, dimensions={0} | all-to-all | bytes 262144 | tf_op jit(solution)/shard_map/far_dots_sum/all_to_all | solution.py:306
  155.0 0.7 pad_maximum_fusion
  155.7 9.3 %all_to_all.33 = f32[4,16,128]{2,1,0:T(8,128)S(1)} all-to-all(f32[4,16,128]{2,1,0:T(8,128)S(1)} %broadcast_in_dim.5), channel_id=1, replica_groups=mesh['y'=4,'zh'=8,'zl'=4,'x'=4,'core'=2] {'y'}, dimensions={0} | all-to-all | bytes 65536 | tf_op jit(solution)/shard_map/far_dots_sum/all_to_all | solution.py:306
  165.0 6.2 %collective-permute-start.3 = (f32[16,128]{1,0:T(8,128)S(1)}, f32[16,128]{1,0:T(8,128)S(1)}, u32[]{:S(2)}, u32[]{:S(2)}) collective-permute-start(f32[16,128]{1,0:T(8,128)S(1)} %reduce_sum.29), channel_id=1, source_target_pairs={{0,32},{32,0},{64,96},{96,64},{128,160},{160,128},{192,224},{224,1... | collective-permute-start | bytes 24584 | tf_op jit(solution)/shard_map/far_dots_sum/ppermute | solution.py:302
  171.2 3.3 %collective-permute-done.3 = f32[16,128]{1,0:T(8,128)S(1)} collective-permute-done((f32[16,128]{1,0:T(8,128)S(1)}, f32[16,128]{1,0:T(8,128)S(1)}, u32[]{:S(2)}, u32[]{:S(2)}) %collective-permute-start.3) | collective-permute-done | bytes 8224 | tf_op jit(solution)/shard_map/far_dots_sum/ppermute | solution.py:302
  174.5 6.2 %collective-permute-start.4 = (f32[16,128]{1,0:T(8,128)S(1)}, f32[16,128]{1,0:T(8,128)S(1)}, u32[]{:S(2)}, u32[]{:S(2)}) collective-permute-start(f32[16,128]{1,0:T(8,128)S(1)} %add.9), channel_id=1, source_target_pairs={{0,64},{32,96},{64,0},{96,32},{128,192},{160,224},{192,128},{224,1... | collective-permute-start | bytes 24584 | tf_op jit(solution)/shard_map/far_dots_sum/ppermute | solution.py:302
  180.7 8.0 %collective-permute-done.4 = f32[16,128]{1,0:T(8,128)S(1)} collective-permute-done((f32[16,128]{1,0:T(8,128)S(1)}, f32[16,128]{1,0:T(8,128)S(1)}, u32[]{:S(2)}, u32[]{:S(2)}) %collective-permute-start.4) | collective-permute-done | bytes 8224 | tf_op jit(solution)/shard_map/far_dots_sum/ppermute | solution.py:302
  188.8 6.2 %collective-permute-start.5 = (f32[16,128]{1,0:T(8,128)S(1)}, f32[16,128]{1,0:T(8,128)S(1)}, u32[]{:S(2)}, u32[]{:S(2)}) collective-permute-start(f32[16,128]{1,0:T(8,128)S(1)} %add.10), channel_id=1, source_target_pairs={{0,128},{32,160},{64,192},{96,224},{128,0},{160,32},{192,64},{224,... | collective-permute-start | bytes 24584 | tf_op jit(solution)/shard_map/far_dots_sum/ppermute | solution.py:302
  195.0 17.6 %collective-permute-done.5 = f32[16,128]{1,0:T(8,128)S(1)} collective-permute-done((f32[16,128]{1,0:T(8,128)S(1)}, f32[16,128]{1,0:T(8,128)S(1)}, u32[]{:S(2)}, u32[]{:S(2)}) %collective-permute-start.5) | collective-permute-done | bytes 8224 | tf_op jit(solution)/shard_map/far_dots_sum/ppermute | solution.py:302
  212.6 0.6 add.11.dots
  213.2 2.3 %far_merge.1 = (bf16[32,128]{1,0:T(8,128)(2,1)}, bf16[1,128]{1,0:T(2,128)(2,1)}) custom-call(s32[1]{0:T(128)} %bitcast.place, f32[16,128]{1,0:T(8,128)} %add.11.dots, f32[1056,128]{1,0:T(8,128)} %get-tuple-element.19.by_row), custom_call_target="tpu_custom_call" | custom-call | tf_op jit(solution)/shard_map/far_merge/pallas_call | solution.py:289
  215.6 1.2 slice_bitcast_fusion
  (22 shorter events, 0.2 us)
Async XLA Ops:
  0.6 1.6 copy-start
  2.2 1.2 copy-start.1
  3.5 0.8 copy-start.3
  4.3 0.7 copy-start.4
  7.5 0.7 copy-start.2
  8.2 26.6 %collective-permute-start = (bf16[1024,128]{1,0:T(8,128)(2,1)S(1)}, bf16[1024,128]{1,0:T(8,128)(2,1)S(1)}, u32[]{:S(2)}, u32[]{:S(2)}) collective-permute-start(bf16[1024,128]{1,0:T(8,128)(2,1)S(1)} %get-tuple-element.13), channel_id=1, source_target_pairs={{0,8},{8,0},{16,24},{24,16},{1,9},{9,1},{17,25},{25,17},{2,10},{10... | collective-permute-start | bytes 786440 | tf_op jit(solution)/shard_map/near_exchange/ppermute | solution.py:302
  12.0 23.6 %collective-permute-start.1 = (bf16[1024,128]{1,0:T(8,128)(2,1)S(1)}, bf16[1024,128]{1,0:T(8,128)(2,1)S(1)}, u32[]{:S(2)}, u32[]{:S(2)}) collective-permute-start(bf16[1024,128]{1,0:T(8,128)(2,1)S(1)} %get-tuple-element.14), channel_id=1, source_target_pairs={{0,16},{8,24},{16,0},{24,8},{1,17},{9,25},{17,1},{25,9},{2,18},{10... | collective-permute-start | bytes 786440 | tf_op jit(solution)/shard_map/near_exchange/ppermute | solution.py:302
  17.2 18.4 %collective-permute-start.2 = (bf16[1024,128]{1,0:T(8,128)(2,1)S(1)}, bf16[1024,128]{1,0:T(8,128)(2,1)S(1)}, u32[]{:S(2)}, u32[]{:S(2)}) collective-permute-start(bf16[1024,128]{1,0:T(8,128)(2,1)S(1)} %get-tuple-element.15), channel_id=1, source_target_pairs={{0,24},{8,16},{16,8},{24,0},{1,25},{9,17},{17,9},{25,1},{2,26},{10... | collective-permute-start | bytes 786440 | tf_op jit(solution)/shard_map/near_exchange/ppermute | solution.py:302
  19.1 20.4 %all-to-all-start.1 = ((f32[8,32,128]{2,1,0:T(8,128)}), f32[8,32,128]{2,1,0:T(8,128)S(1)}, u32[]{:S(2)}, u32[]{:S(2)}) async-start(f32[8,32,128]{2,1,0:T(8,128)} %get-tuple-element.16), calls=%async_computation.1 | async-start | bytes 262144 | tf_op jit(solution)/shard_map/gain_sum/all_to_all | solution.py:306
  34.8 0.8 copy-start.5
  35.6 0.7 copy-start.6
  35.6 0.8 copy-start.7
  39.5 16.2 %all-to-all-start = ((f32[32,1,128]{2,1,0:T(1,128)}), f32[32,1,128]{2,1,0:T(1,128)S(1)}, u32[]{:S(2)}, u32[]{:S(2)}) async-start(f32[32,1,128]{2,1,0:T(1,128)} %near_dots.1), calls=%async_computation | async-start | bytes 32768 | tf_op jit(solution)/shard_map/near_dots_sum/all_to_all | solution.py:306
  55.6 8.8 %copy-start.8 = (f32[32,1,128]{2,1,0:T(1,128)}, f32[32,1,128]{2,1,0:T(1,128)S(1)}, u32[]{:S(2)}) copy-start(f32[32,1,128]{2,1,0:T(1,128)S(1)} %all-to-all-done.dots) | copy-start | bytes 49156
  165.0 9.5 %collective-permute-start.3 = (f32[16,128]{1,0:T(8,128)S(1)}, f32[16,128]{1,0:T(8,128)S(1)}, u32[]{:S(2)}, u32[]{:S(2)}) collective-permute-start(f32[16,128]{1,0:T(8,128)S(1)} %reduce_sum.29), channel_id=1, source_target_pairs={{0,32},{32,0},{64,96},{96,64},{128,160},{160,128},{192,224},{224,1... | collective-permute-start | bytes 24584 | tf_op jit(solution)/shard_map/far_dots_sum/ppermute | solution.py:302
  174.5 14.3 %collective-permute-start.4 = (f32[16,128]{1,0:T(8,128)S(1)}, f32[16,128]{1,0:T(8,128)S(1)}, u32[]{:S(2)}, u32[]{:S(2)}) collective-permute-start(f32[16,128]{1,0:T(8,128)S(1)} %add.9), channel_id=1, source_target_pairs={{0,64},{32,96},{64,0},{96,32},{128,192},{160,224},{192,128},{224,1... | collective-permute-start | bytes 24584 | tf_op jit(solution)/shard_map/far_dots_sum/ppermute | solution.py:302
  188.8 23.9 %collective-permute-start.5 = (f32[16,128]{1,0:T(8,128)S(1)}, f32[16,128]{1,0:T(8,128)S(1)}, u32[]{:S(2)}, u32[]{:S(2)}) collective-permute-start(f32[16,128]{1,0:T(8,128)S(1)} %add.10), channel_id=1, source_target_pairs={{0,128},{32,160},{64,192},{96,224},{128,0},{160,32},{192,64},{224,... | collective-permute-start | bytes 24584 | tf_op jit(solution)/shard_map/far_dots_sum/ppermute | solution.py:302

commit v2 on v1

--- a/solution.py
+++ b/solution.py
@@ -16,28 +16,49 @@
 FAR = 32
 FAR_Z = 8
 WIDTH = 8
+GAIN_AT = 16
 PIECE = 32
 LANES = 128
 VMEM_SPEC = pl.BlockSpec(memory_space=pltpu.VMEM)
 SMEM_SPEC = pl.BlockSpec(memory_space=pltpu.SMEM)
+PARAMS = pltpu.CompilerParams(vmem_limit_bytes=16 << 20)
 
 
 def factor(cross, own_sq):
     return 1.0 - cross / (2.0 * (jnp.maximum(own_sq, 0.0) + eps_merge))
 
 
-def grads_kernel(place, hidden, cot, gain, weight, p0, p1, p2, p3, gain_out, inv_wide, pieces):
+def grads_kernel(
+    place, hidden_hbm, cot_hbm, gain_hbm, weight_hbm, p0, p1, p2, p3, gain_out,
+    hidden, cot, gain, weight, inv_wide, pieces, gain_rows, sems,
+):
     tokens, width = hidden.shape
+    parts = 8
+    height = tokens // parts
+    copies = [
+        pltpu.make_async_copy(
+            hidden_hbm.at[pl.ds(part * height, height)],
+            hidden.at[pl.ds(part * height, height)],
+            sems.at[part],
+        )
+        for part in range(parts)
+    ]
+    for at, (there, here) in enumerate(((cot_hbm, cot), (gain_hbm, gain), (weight_hbm, weight))):
+        copies.append(pltpu.make_async_copy(there, here, sems.at[parts + at]))
+    for copy in copies:
+        copy.start()
     blocks = width // LANES
-    half = tokens // 2
-    for part in range(2):
-        rows = pl.ds(part * half, half)
-        total = jnp.zeros((half, LANES), f32)
+    for part in range(parts):
+        rows = pl.ds(part * height, height)
+        copies[part].wait()
+        totals = [jnp.zeros((height, LANES), f32) for _ in range(2)]
         for block in range(blocks):
             x = hidden[rows, pl.ds(block * LANES, LANES)].astype(f32)
-            total = total + x * x
-        mean = jnp.sum(total, axis=1, keepdims=True) * (1.0 / width)
-        inv_wide[rows, :] = jnp.broadcast_to(lax.rsqrt(mean + eps_norm), (half, LANES))
+            totals[block % 2] = totals[block % 2] + x * x
+        mean = jnp.sum(totals[0] + totals[1], axis=1, keepdims=True) * (1.0 / width)
+        inv_wide[rows, :] = jnp.broadcast_to(lax.rsqrt(mean + eps_norm), (height, LANES))
+    for copy in copies[parts:]:
+        copy.wait()
     step = 4 * LANES
     for chunk in range(width // step):
         inv = inv_wide[...]
@@ -65,28 +86,41 @@
             for near in range(NEAR):
                 at = sub * LANES + near * PIECE
                 pieces[near, pl.ds(block * PIECE, PIECE), :] = grad[at : at + PIECE]
-            row = jnp.sum(
+            gain_rows[pl.ds(block, 1), :] = jnp.sum(
                 back[:, sub * LANES : (sub + 1) * LANES] * normed[sub], axis=0, keepdims=True
             )
-            for other in range(WIDTH):
-                gain_out[other, pl.ds(block, 1), :] = row
     here = place[0]
     for apart, out in enumerate((p0, p1, p2, p3)):
         out[...] = pieces[here ^ apart]
+    lane = lax.broadcasted_iota(jnp.int32, (8, LANES), 1)
+    for near in range(NEAR):
+        total = jnp.zeros((8, LANES), f32)
+        for block in range(4):
+            part = jnp.where(lane // PIECE == near, gain_rows[pl.ds(8 * block, 8), :], 0.0)
+            turn = PIECE * (block - near) % LANES
+            total = total + (pltpu.roll(part, turn, 1) if turn else part)
+        for other in range(WIDTH):
+            gain_out[near * WIDTH + other] = total
 
 
 def local_grads(place, hidden, cot, gain, weight):
     piece = jax.ShapeDtypeStruct((FAR * PIECE, LANES), bf16)
     return pl.pallas_call(
         grads_kernel,
-        out_shape=[piece] * NEAR + [jax.ShapeDtypeStruct((WIDTH, FAR, LANES), f32)],
-        in_specs=[SMEM_SPEC] + [VMEM_SPEC] * 4,
+        out_shape=[piece] * NEAR + [jax.ShapeDtypeStruct((NEAR * WIDTH, 8, LANES), f32)],
+        in_specs=[SMEM_SPEC] + [pl.BlockSpec(memory_space=pltpu.HBM)] * 4,
         out_specs=[VMEM_SPEC] * (NEAR + 1),
         scratch_shapes=[
+            pltpu.VMEM(hidden.shape, bf16),
+            pltpu.VMEM(cot.shape, bf16),
+            pltpu.VMEM(gain.shape, f32),
+            pltpu.VMEM(weight.shape, bf16),
             pltpu.VMEM((hidden.shape[0], LANES), f32),
             pltpu.VMEM((NEAR, FAR * PIECE, LANES), bf16),
+            pltpu.VMEM((FAR, LANES), f32),
+            pltpu.SemaphoreType.DMA((11,)),
         ],
-        compiler_params=pltpu.CompilerParams(vmem_limit_bytes=32 << 20),
+        compiler_params=PARAMS,
         name="local_grads",
     )(place, hidden, cot, gain, weight)
 
@@ -95,7 +129,7 @@
     return jnp.sum(jnp.sum(x, axis=0, keepdims=True), axis=1, keepdims=True)
 
 
-def near_dots_kernel(place, p0, p1, p2, p3, out):
+def near_dots_kernel(place, gain_parts, p0, p1, p2, p3, out, gain_out):
     refs = (p0, p1, p2, p3)
     pairs = [(a, b) for a in range(NEAR) for b in range(a, NEAR)]
     rows = 64
@@ -117,17 +151,30 @@
         dot = all_sum(total)
         row = jnp.where(lane == ((NEAR * a + b) ^ (5 * here)), dot, row)
         row = jnp.where(lane == ((NEAR * b + a) ^ (5 * here)), dot, row)
+    gain = []
+    for near in range(NEAR):
+        total = gain_parts[near * WIDTH]
+        for other in range(1, WIDTH):
+            total = total + gain_parts[near * WIDTH + other]
+        gain.append(total.astype(bf16).astype(f32))
+        gain_out[pl.ds(8 * near, 8), :] = gain[near]
+    for a, b in pairs:
+        row = jnp.where(lane == GAIN_AT + NEAR * a + b, all_sum(gain[a] * gain[b]), row)
     out[...] = jnp.broadcast_to(row.reshape(1, 1, LANES), out.shape)
 
 
-def near_dots(place, pieces):
+def near_dots(place, gain_parts, pieces):
     return pl.pallas_call(
         near_dots_kernel,
-        out_shape=jax.ShapeDtypeStruct((NEAR * WIDTH, 1, LANES), f32),
-        in_specs=[SMEM_SPEC] + [VMEM_SPEC] * NEAR,
-        out_specs=VMEM_SPEC,
+        out_shape=[
+            jax.ShapeDtypeStruct((NEAR * WIDTH, 1, LANES), f32),
+            jax.ShapeDtypeStruct((NEAR * 8, LANES), f32),
+        ],
+        in_specs=[SMEM_SPEC] + [VMEM_SPEC] * (1 + NEAR),
+        out_specs=[VMEM_SPEC] * 2,
+        compiler_params=PARAMS,
         name="near_dots",
-    )(place, *pieces)
+    )(place, gain_parts, *pieces)
 
 
 def near_shares(dots):
@@ -151,15 +198,38 @@
     return (of_low * low[0], of_low * low[1], of_high * high[0], of_high * high[1])
 
 
+def packed(dots):
+    total = dots[0:8]
+    for block in range(1, 4):
+        total = total + pltpu.roll(dots[8 * block : 8 * block + 8], 32 * block, 1)
+    return total
+
+
+def unpacked(rows):
+    lane = lax.broadcasted_iota(jnp.int32, (8, LANES), 1)
+    blocks = []
+    for block in range(4):
+        moved = rows if block == 0 else pltpu.roll(rows, LANES - 32 * block, 1)
+        blocks.append(jnp.where(lane < FAR, moved, 0.0))
+    return jnp.concatenate(blocks, axis=0)
+
+
 def near_merge_kernel(place, dots, gains, p0, p1, p2, p3, out):
     here = place[0]
     row = jnp.sum(dots[...], axis=0)
     lane = lax.broadcasted_iota(jnp.int32, (1, LANES), 1)
-
-    def entry(a, b):
-        return jnp.sum(jnp.where(lane == NEAR * a + b, row, 0.0), axis=1, keepdims=True)
-
-    shares = near_shares([[entry(a, b) if a <= b else None for b in range(NEAR)] for a in range(NEAR)])
+    row = jnp.where(lane < GAIN_AT, row, row * (1.0 / WIDTH))
+
+    def shares_at(first):
+        def entry(a, b):
+            at = first + NEAR * a + b
+            return jnp.sum(jnp.where(lane == at, row, 0.0), axis=1, keepdims=True)
+
+        return near_shares(
+            [[entry(a, b) if a <= b else None for b in range(NEAR)] for a in range(NEAR)]
+        )
+
+    shares = shares_at(0)
     by_apart = []
     for apart in range(NEAR):
         share = shares[apart]
@@ -173,13 +243,11 @@
             total = total + share * ref[rows, :].astype(f32)
         out[far, pl.ds(0, PIECE), :] = total.astype(bf16)
 
-    gain = [gains[near] for near in range(NEAR)]
-    gain_shares = near_shares(
-        [[all_sum(gain[a] * gain[b]) if a <= b else None for b in range(NEAR)] for a in range(NEAR)]
-    )
-    merged = gain_shares[0] * gain[0]
+    gain_shares = shares_at(GAIN_AT)
+    merged = gain_shares[0] * gains[pl.ds(0, 8), :]
     for near in range(1, NEAR):
-        merged = merged + gain_shares[near] * gain[near]
+        merged = merged + gain_shares[near] * gains[pl.ds(8 * near, 8), :]
+    merged = unpacked(merged)
     for far in range(FAR):
         out[far, pl.ds(PIECE, 8), :] = jnp.broadcast_to(merged[far : far + 1], (8, LANES)).astype(bf16)
 
@@ -190,27 +258,12 @@
         out_shape=jax.ShapeDtypeStruct((FAR, PIECE + 8, LANES), bf16),
         in_specs=[SMEM_SPEC] + [VMEM_SPEC] * (2 + NEAR),
         out_specs=VMEM_SPEC,
+        compiler_params=PARAMS,
         name="near_merge",
     )(place, dots, gains, *pieces)
 
 
-def packed(dots):
-    total = dots[0:8]
-    for block in range(1, 4):
-        total = total + pltpu.roll(dots[8 * block : 8 * block + 8], 32 * block, 1)
-    return total
-
-
-def unpacked(rows):
-    lane = lax.broadcasted_iota(jnp.int32, (8, LANES), 1)
-    blocks = []
-    for block in range(4):
-        moved = rows if block == 0 else pltpu.roll(rows, LANES - 32 * block, 1)
-        blocks.append(jnp.where(lane < FAR, moved, 0.0))
-    return jnp.concatenate(blocks, axis=0)
-
-
-def far_dots_kernel(values, key_out, gain_out, by_row, wide):
+def far_dots_kernel(values, out, by_row, wide):
     for far in range(FAR):
         wide[pl.ds(far * (PIECE + 8), PIECE + 8), :] = values[far].astype(f32)
     columns = []
@@ -228,21 +281,21 @@
         )
 
     key_rows = packed(dots(jnp.concatenate(columns[:PIECE], axis=1)))
-    key_out[...] = jnp.broadcast_to(key_rows[None], key_out.shape)
-    gain_out[...] = packed(dots(columns[PIECE]))
+    gain_rows = packed(dots(columns[PIECE])) * (1.0 / WIDTH)
+    out[...] = jnp.broadcast_to(jnp.concatenate([key_rows, gain_rows], axis=0)[None], out.shape)
 
 
 def far_dots(values):
     return pl.pallas_call(
         far_dots_kernel,
         out_shape=[
-            jax.ShapeDtypeStruct((NEAR * WIDTH, 8, LANES), f32),
-            jax.ShapeDtypeStruct((8, LANES), f32),
+            jax.ShapeDtypeStruct((4 * WIDTH, 16, LANES), f32),
             jax.ShapeDtypeStruct(((PIECE + 1) * FAR, LANES), f32),
         ],
         in_specs=[VMEM_SPEC],
-        out_specs=[VMEM_SPEC] * 3,
+        out_specs=[VMEM_SPEC] * 2,
         scratch_shapes=[pltpu.VMEM((FAR * (PIECE + 8), LANES), f32)],
+        compiler_params=PARAMS,
         name="far_dots",
     )(values)
 
@@ -267,7 +320,7 @@
     return share
 
 
-def far_merge_kernel(place, dots, by_row, key_out, gain_out):
+def far_merge_kernel(dots, by_row, key_out, gain_out):
     key_share = far_shares(unpacked(dots[pl.ds(0, 8), :]))
     gain_share = far_shares(unpacked(dots[pl.ds(8, 8), :]))
     key_wide = jnp.broadcast_to(key_share, (FAR, LANES))
@@ -278,24 +331,21 @@
         )
     key_out[...] = jnp.concatenate(rows, axis=0).astype(bf16)
     gain = jnp.sum(gain_share * by_row[pl.ds(PIECE * FAR, FAR), :], axis=0, keepdims=True)
-    wide = jnp.broadcast_to(gain, (8, LANES))
-    moved = wide
-    for near in range(1, NEAR):
-        moved = jnp.where(place[0] == near, pltpu.roll(wide, LANES - PIECE * near, 1), moved)
-    gain_out[...] = moved[0:1].astype(bf16)
-
-
-def far_merge(place, dots, by_row):
+    gain_out[...] = gain[:, :PIECE].astype(bf16)
+
+
+def far_merge(dots, by_row):
     return pl.pallas_call(
         far_merge_kernel,
         out_shape=[
             jax.ShapeDtypeStruct((PIECE, LANES), bf16),
-            jax.ShapeDtypeStruct((1, LANES), bf16),
+            jax.ShapeDtypeStruct((1, PIECE), bf16),
         ],
-        in_specs=[SMEM_SPEC] + [VMEM_SPEC] * 2,
+        in_specs=[VMEM_SPEC] * 2,
         out_specs=[VMEM_SPEC] * 2,
+        compiler_params=PARAMS,
         name="far_merge",
-    )(place, dots, by_row)
+    )(dots, by_row)
 
 
 def paired(x, axis, apart):
@@ -313,25 +363,21 @@
     )
     with jax.named_scope("near_exchange"):
         arrived = {apart: paired(pieces[apart], "zl", apart) for apart in (2, 3, 1)}
-    with jax.named_scope("gain_sum"):
-        gain = jnp.sum(exchanged(gain_parts, ("x", "core")), axis=0)
-        gain = lax.reduce_precision(gain, 8, 7)
-        gains = exchanged(jnp.broadcast_to(gain[None], (NEAR, FAR, LANES)), "zl")
+    with jax.named_scope("gain_exchange"):
+        gain_parts = exchanged(gain_parts, ("zl", "x", "core"))
     pieces = [pieces[0]] + [arrived[apart] for apart in range(1, NEAR)]
+    dots, gains = near_dots(place, gain_parts, pieces)
     with jax.named_scope("near_dots_sum"):
-        dots = exchanged(near_dots(place, pieces), ("zl", "x", "core"))
+        dots = exchanged(dots, ("zl", "x", "core"))
     values = near_merge(place, dots, gains, pieces)
     with jax.named_scope("far_exchange"):
         values = exchanged(values, ("y", "zh"))
-    key_dots, gain_dots, by_row = far_dots(values)
+    dots, by_row = far_dots(values)
     with jax.named_scope("far_dots_sum"):
-        key_dots = jnp.sum(exchanged(key_dots, ("zl", "x", "core")), axis=0)
-        dots = jnp.concatenate([key_dots, gain_dots], axis=0)
-        dots = jnp.sum(exchanged(jnp.broadcast_to(dots[None], (4, 16, LANES)), "y"), axis=0)
-        for apart in (1, 2, 4):
-            dots = dots + paired(dots, "zh", apart)
-    merged_key, merged_gain = far_merge(place, dots, by_row)
-    return (merged_key, merged_gain[0, :PIECE])
+        dots = jnp.sum(exchanged(dots, ("y", "x", "core")), axis=0)
+        dots = lax.psum(lax.psum(dots, "zl"), "zh")
+    merged_key, merged_gain = far_merge(dots, by_row)
+    return (merged_key, merged_gain.reshape(PIECE))
 
 
 def solution(mesh):

time: 218 us -> 185 us (0.85)
  the two profiles are of different devices: /device:TPU:2 before, /device:TPU:32 now
where the time goes in v2:
time: 185 us
  blocking collectives  127 us (69%)
  starting transfers between devices  25.5 us (14%)
  waiting for transfers between devices  21 us (11%)
  Pallas kernels  6.46 us (3%)
  local copies, waits for them, and re-layouts  4.36 us (2%)
    all_to_all x3, blocking collectives, exchanged(): return lax.all_to_all(x, axes, 0, 0)  87.9 us
    psum x2, blocking collectives, body(): dots = lax.psum(lax.psum(dots, 'zl'), 'zh')  38.8 us
    ppermute x3, waiting for transfers between devices, paired(): lax.ppermute(x, axis, [(i, i ^ apart) for i in range(lax.axis_size(axis))])  21 us
    all_to_all x1, starting transfers between devices, exchanged(): return lax.all_to_all(x, axes, 0, 0)  16.3 us
    ppermute x3, starting transfers between devices, paired(): lax.ppermute(x, axis, [(i, i ^ apart) for i in range(lax.axis_size(axis))])  9.21 us
    unnamed x8, local copies, waits for them, and re-layouts  4.36 us
    pallas_call x1, Pallas kernels, local_grads(): pl.pallas_call(grads_kernel, out_shape=[piece] * NEAR + [jax.ShapeDtypeSt...  3.8 us
  transfers between devices with their start and end apart: 4, of which 3 were waited for; matrix products, arithmetic and copies ran while one was open for 0% of the time, Pallas kernels for 0%

profile of v2, /device:TPU:32, one launch (start us, length us, event | category | flops | bytes accessed | tf_op | source)
XLA Modules:
  0.0 184.8 jit_solution(16334198318510582667)
XLA Ops:
  0.6 0.0 copy-start
  0.6 1.6 copy-done
  2.2 0.0 copy-start.1
  2.2 1.2 copy-done.1
  3.5 0.0 copy-start.2
  3.5 0.8 copy-done.2
  4.3 0.0 copy-start.3
  4.3 0.7 copy-done.3
  5.0 3.8 %local_grads.1 = (bf16[1024,128]{1,0:T(8,128)(2,1)S(1)}, bf16[1024,128]{1,0:T(8,128)(2,1)S(1)}, bf16[1024,128]{1,0:T(8,128)(2,1)S(1)}, bf16[1024,128]{1,0:T(8,128)(2,1)S(1)}, f32[32,8,128]{2,1,0:T(8,128)}) custom-call(s32[1]{0:T(128)} %bitcast.place, bf16[256,4096]{1,0:T(8,128)(2,1)S(1)} %copy-done, bf16[256,128]{1,0:T(8,128)(2,1)S(1)} %copy-done.2, ...), custom_call_target="tpu_custom_call" | custom-call | tf_op jit(solution)/shard_map/local_grads/pallas_call | solution.py:108
  8.8 16.3 %all-to-all-start = ((f32[32,8,128]{2,1,0:T(8,128)}), f32[32,8,128]{2,1,0:T(8,128)S(1)}, u32[]{:S(2)}, u32[]{:S(2)}) async-start(f32[32,8,128]{2,1,0:T(8,128)} %get-tuple-element.13), calls=%async_computation | async-start | bytes 262144 | tf_op jit(solution)/shard_map/gain_exchange/all_to_all | solution.py:356
  25.1 2.2 %collective-permute-start = (bf16[1024,128]{1,0:T(8,128)(2,1)S(1)}, bf16[1024,128]{1,0:T(8,128)(2,1)S(1)}, u32[]{:S(2)}, u32[]{:S(2)}) collective-permute-start(bf16[1024,128]{1,0:T(8,128)(2,1)S(1)} %get-tuple-element.15), channel_id=1, source_target_pairs={{0,8},{8,0},{16,24},{24,16},{1,9},{9,1},{17,25},{25,17},{2,10},{10... | collective-permute-start | bytes 786440 | tf_op jit(solution)/shard_map/near_exchange/ppermute | solution.py:352
  27.4 4.6 %collective-permute-start.1 = (bf16[1024,128]{1,0:T(8,128)(2,1)S(1)}, bf16[1024,128]{1,0:T(8,128)(2,1)S(1)}, u32[]{:S(2)}, u32[]{:S(2)}) collective-permute-start(bf16[1024,128]{1,0:T(8,128)(2,1)S(1)} %get-tuple-element.16), channel_id=1, source_target_pairs={{0,16},{8,24},{16,0},{24,8},{1,17},{9,25},{17,1},{25,9},{2,18},{10... | collective-permute-start | bytes 786440 | tf_op jit(solution)/shard_map/near_exchange/ppermute | solution.py:352
  32.0 2.4 %collective-permute-start.2 = (bf16[1024,128]{1,0:T(8,128)(2,1)S(1)}, bf16[1024,128]{1,0:T(8,128)(2,1)S(1)}, u32[]{:S(2)}, u32[]{:S(2)}) collective-permute-start(bf16[1024,128]{1,0:T(8,128)(2,1)S(1)} %get-tuple-element.17), channel_id=1, source_target_pairs={{0,24},{8,16},{16,8},{24,0},{1,25},{9,17},{17,9},{25,1},{2,26},{10... | collective-permute-start | bytes 786440 | tf_op jit(solution)/shard_map/near_exchange/ppermute | solution.py:352
  34.4 3.5 %collective-permute-done.p1 = bf16[1024,128]{1,0:T(8,128)(2,1)S(1)} collective-permute-done((bf16[1024,128]{1,0:T(8,128)(2,1)S(1)}, bf16[1024,128]{1,0:T(8,128)(2,1)S(1)}, u32[]{:S(2)}, u32[]{:S(2)}) %collective-permute-start) | collective-permute-done | bytes 262176 | tf_op jit(solution)/shard_map/near_exchange/ppermute | solution.py:352
  37.8 12.0 %collective-permute-done.1.p2 = bf16[1024,128]{1,0:T(8,128)(2,1)S(1)} collective-permute-done((bf16[1024,128]{1,0:T(8,128)(2,1)S(1)}, bf16[1024,128]{1,0:T(8,128)(2,1)S(1)}, u32[]{:S(2)}, u32[]{:S(2)}) %collective-permute-start.1) | collective-permute-done | bytes 262176 | tf_op jit(solution)/shard_map/near_exchange/ppermute | solution.py:352
  49.9 5.5 %collective-permute-done.2.p3 = bf16[1024,128]{1,0:T(8,128)(2,1)S(1)} collective-permute-done((bf16[1024,128]{1,0:T(8,128)(2,1)S(1)}, bf16[1024,128]{1,0:T(8,128)(2,1)S(1)}, u32[]{:S(2)}, u32[]{:S(2)}) %collective-permute-start.2) | collective-permute-done | bytes 262176 | tf_op jit(solution)/shard_map/near_exchange/ppermute | solution.py:352
  55.4 0.0 all-to-all-done.gain_parts
  55.4 0.7 near_dots.1
  56.1 13.1 %all_to_all.20.dots = f32[32,1,128]{2,1,0:T(1,128)S(1)} all-to-all(f32[32,1,128]{2,1,0:T(1,128)S(1)} %get-tuple-element.18), channel_id=1, replica_groups=mesh['y'=4,'zh'=8,'zl'=4,'x'=4,'core'=2] {'zl','x','core'}, dimensions={0} | all-to-all | bytes 32768 | tf_op jit(solution)/shard_map/near_dots_sum/all_to_all | solution.py:356
  69.2 0.4 near_merge.1
  69.6 60.9 %all_to_all.21.values = bf16[32,40,128]{2,1,0:T(8,128)(2,1)S(1)} all-to-all(bf16[32,40,128]{2,1,0:T(8,128)(2,1)S(1)} %near_merge.1), channel_id=1, replica_groups=mesh['y'=4,'zh'=8,'zl'=4,'x'=4,'core'=2] {'y','zh'}, dimensions={0} | all-to-all | bytes 655360 | tf_op jit(solution)/shard_map/far_exchange/all_to_all | solution.py:356
  130.5 0.4 far_dots.1
  130.8 13.9 %all_to_all.22 = f32[32,16,128]{2,1,0:T(8,128)S(1)} all-to-all(f32[32,16,128]{2,1,0:T(8,128)S(1)} %get-tuple-element.20), channel_id=1, replica_groups=mesh['y'=4,'zh'=8,'zl'=4,'x'=4,'core'=2] {'y','x','core'}, dimensions={0} | all-to-all | bytes 524288 | tf_op jit(solution)/shard_map/far_dots_sum/all_to_all | solution.py:356
  144.8 14.4 %psum.14 = f32[16,128]{1,0:T(8,128)S(1)} all-reduce(f32[16,128]{1,0:T(8,128)S(1)} %reduce_sum.9), channel_id=1, replica_groups=mesh['y'=4,'zh'=8,'zl'=4,'x'=4,'core'=2] {'zl'}, use_global_device_ids=true, to_apply=%region_1.0 | all-reduce | flops 2048 | bytes 16384 | tf_op jit(solution)/shard_map/far_dots_sum/psum | solution.py:378
  159.1 24.4 %psum.15.dots = f32[16,128]{1,0:T(8,128)S(1)} all-reduce(f32[16,128]{1,0:T(8,128)S(1)} %psum.14), channel_id=1, replica_groups=mesh['y'=4,'zh'=8,'zl'=4,'x'=4,'core'=2] {'zh'}, use_global_device_ids=true, to_apply=%region_2.0 | all-reduce | flops 2048 | bytes 16384 | tf_op jit(solution)/shard_map/far_dots_sum/psum | solution.py:378
  183.6 1.3 far_merge.1
  (1 shorter events, 0.0 us)
Async XLA Ops:
  0.6 1.6 copy-start
  2.2 1.2 copy-start.1
  3.5 0.8 copy-start.2
  4.3 0.7 copy-start.3
  8.8 46.6 %all-to-all-start = ((f32[32,8,128]{2,1,0:T(8,128)}), f32[32,8,128]{2,1,0:T(8,128)S(1)}, u32[]{:S(2)}, u32[]{:S(2)}) async-start(f32[32,8,128]{2,1,0:T(8,128)} %get-tuple-element.13), calls=%async_computation | async-start | bytes 262144 | tf_op jit(solution)/shard_map/gain_exchange/all_to_all | solution.py:356
  25.1 12.7 %collective-permute-start = (bf16[1024,128]{1,0:T(8,128)(2,1)S(1)}, bf16[1024,128]{1,0:T(8,128)(2,1)S(1)}, u32[]{:S(2)}, u32[]{:S(2)}) collective-permute-start(bf16[1024,128]{1,0:T(8,128)(2,1)S(1)} %get-tuple-element.15), channel_id=1, source_target_pairs={{0,8},{8,0},{16,24},{24,16},{1,9},{9,1},{17,25},{25,17},{2,10},{10... | collective-permute-start | bytes 786440 | tf_op jit(solution)/shard_map/near_exchange/ppermute | solution.py:352
  27.4 22.5 %collective-permute-start.1 = (bf16[1024,128]{1,0:T(8,128)(2,1)S(1)}, bf16[1024,128]{1,0:T(8,128)(2,1)S(1)}, u32[]{:S(2)}, u32[]{:S(2)}) collective-permute-start(bf16[1024,128]{1,0:T(8,128)(2,1)S(1)} %get-tuple-element.16), channel_id=1, source_target_pairs={{0,16},{8,24},{16,0},{24,8},{1,17},{9,25},{17,1},{25,9},{2,18},{10... | collective-permute-start | bytes 786440 | tf_op jit(solution)/shard_map/near_exchange/ppermute | solution.py:352
  32.0 23.4 %collective-permute-start.2 = (bf16[1024,128]{1,0:T(8,128)(2,1)S(1)}, bf16[1024,128]{1,0:T(8,128)(2,1)S(1)}, u32[]{:S(2)}, u32[]{:S(2)}) collective-permute-start(bf16[1024,128]{1,0:T(8,128)(2,1)S(1)} %get-tuple-element.17), channel_id=1, source_target_pairs={{0,24},{8,16},{16,8},{24,0},{1,25},{9,17},{17,9},{25,1},{2,26},{10... | collective-permute-start | bytes 786440 | tf_op jit(solution)/shard_map/near_exchange/ppermute | solution.py:352

commit v3 on v2

--- a/solution.py
+++ b/solution.py
@@ -21,7 +21,12 @@
 LANES = 128
 VMEM_SPEC = pl.BlockSpec(memory_space=pltpu.VMEM)
 SMEM_SPEC = pl.BlockSpec(memory_space=pltpu.SMEM)
+HBM_SPEC = pl.BlockSpec(memory_space=pltpu.HBM)
 PARAMS = pltpu.CompilerParams(vmem_limit_bytes=16 << 20)
+
+
+def in_hbm(x):
+    return pltpu.with_memory_space_constraint(x, pltpu.HBM)
 
 
 def factor(cross, own_sq):
@@ -29,8 +34,7 @@
 
 
 def grads_kernel(
-    place, hidden_hbm, cot_hbm, gain_hbm, weight_hbm, p0, p1, p2, p3, gain_out,
-    hidden, cot, gain, weight, inv_wide, pieces, gain_rows, sems,
+    place, hidden_hbm, cot_hbm, gain_hbm, p0, p1, p2, p3, inv_wide, hidden, cot, gain, pieces, sems
 ):
     tokens, width = hidden.shape
     parts = 8
@@ -43,7 +47,7 @@
         )
         for part in range(parts)
     ]
-    for at, (there, here) in enumerate(((cot_hbm, cot), (gain_hbm, gain), (weight_hbm, weight))):
+    for at, (there, here) in enumerate(((cot_hbm, cot), (gain_hbm, gain))):
         copies.append(pltpu.make_async_copy(there, here, sems.at[parts + at]))
     for copy in copies:
         copy.start()
@@ -59,15 +63,11 @@
         inv_wide[rows, :] = jnp.broadcast_to(lax.rsqrt(mean + eps_norm), (height, LANES))
     for copy in copies[parts:]:
         copy.wait()
-    step = 4 * LANES
-    for chunk in range(width // step):
+    for chunk in range(blocks // 4):
         inv = inv_wide[...]
-        normed = []
         inputs = []
-        for sub in range(4):
-            block = 4 * chunk + sub
+        for block in range(4 * chunk, 4 * chunk + 4):
             x = hidden[:, pl.ds(block * LANES, LANES)].astype(f32) * inv
-            normed.append(x)
             inputs.append((x * gain[pl.ds(block, 1), :]).astype(bf16))
         grad = lax.dot_general(
             jnp.concatenate(inputs, axis=1),
@@ -75,61 +75,114 @@
             (((0,), (0,)), ((), ())),
             preferred_element_type=f32,
         ).astype(bf16)
+        for sub in range(4):
+            for near in range(NEAR):
+                at = sub * LANES + near * PIECE
+                pieces[near, pl.ds((4 * chunk + sub) * PIECE, PIECE), :] = grad[at : at + PIECE]
+    here = place[0]
+    for apart, out in enumerate((p0, p1, p2, p3)):
+        out[...] = pieces[here ^ apart]
+
+
+def local_grads(place, hidden, cot, gain):
+    piece = jax.ShapeDtypeStruct((FAR * PIECE, LANES), bf16)
+    return pl.pallas_call(
+        grads_kernel,
+        out_shape=[piece] * NEAR + [jax.ShapeDtypeStruct((hidden.shape[0], LANES), f32)],
+        in_specs=[SMEM_SPEC] + [HBM_SPEC] * 3,
+        out_specs=[VMEM_SPEC] * (NEAR + 1),
+        scratch_shapes=[
+            pltpu.VMEM(hidden.shape, bf16),
+            pltpu.VMEM(cot.shape, bf16),
+            pltpu.VMEM(gain.shape, f32),
+            pltpu.VMEM((NEAR, FAR * PIECE, LANES), bf16),
+            pltpu.SemaphoreType.DMA((10,)),
+        ],
+        compiler_params=PARAMS,
+        name="local_grads",
+    )(place, in_hbm(hidden), in_hbm(cot), in_hbm(gain))
+
+
+def gains_kernel(
+    hidden_hbm, cot_hbm, weight_hbm, inv_wide, p1, p1_out, out, hidden, cot, weight, rows, sems
+):
+    blocks = hidden.shape[1] // LANES
+    step = 4 * LANES
+    copies = [pltpu.make_async_copy(cot_hbm, cot, sems.at[0])]
+    for part in range(2):
+        half = pl.ds(part * (blocks // 2) * LANES, (blocks // 2) * LANES)
+        copies.append(
+            pltpu.make_async_copy(weight_hbm.at[half], weight.at[half], sems.at[1 + part])
+        )
+        copies.append(
+            pltpu.make_async_copy(
+                hidden_hbm.at[:, half], hidden.at[:, half], sems.at[3 + part]
+            )
+        )
+    for copy in copies:
+        copy.start()
+    p1_out[...] = p1[...]
+    for copy in copies[:3]:
+        copy.wait()
+    for chunk in range(blocks // 4):
+        if chunk == blocks // 8:
+            for copy in copies[3:]:
+                copy.wait()
         back = lax.dot_general(
             cot[...],
             weight[pl.ds(chunk * step, step), :],
             (((1,), (1,)), ((), ())),
             preferred_element_type=f32,
         )
+        inv = inv_wide[...]
         for sub in range(4):
             block = 4 * chunk + sub
-            for near in range(NEAR):
-                at = sub * LANES + near * PIECE
-                pieces[near, pl.ds(block * PIECE, PIECE), :] = grad[at : at + PIECE]
-            gain_rows[pl.ds(block, 1), :] = jnp.sum(
-                back[:, sub * LANES : (sub + 1) * LANES] * normed[sub], axis=0, keepdims=True
+            normed = hidden[:, pl.ds(block * LANES, LANES)].astype(f32) * inv
+            rows[pl.ds(block, 1), :] = jnp.sum(
+                back[:, sub * LANES : (sub + 1) * LANES] * normed, axis=0, keepdims=True
             )
-    here = place[0]
-    for apart, out in enumerate((p0, p1, p2, p3)):
-        out[...] = pieces[here ^ apart]
     lane = lax.broadcasted_iota(jnp.int32, (8, LANES), 1)
     for near in range(NEAR):
         total = jnp.zeros((8, LANES), f32)
         for block in range(4):
-            part = jnp.where(lane // PIECE == near, gain_rows[pl.ds(8 * block, 8), :], 0.0)
+            part = jnp.where(lane // PIECE == near, rows[pl.ds(8 * block, 8), :], 0.0)
             turn = PIECE * (block - near) % LANES
             total = total + (pltpu.roll(part, turn, 1) if turn else part)
         for other in range(WIDTH):
-            gain_out[near * WIDTH + other] = total
-
-
-def local_grads(place, hidden, cot, gain, weight):
-    piece = jax.ShapeDtypeStruct((FAR * PIECE, LANES), bf16)
-    return pl.pallas_call(
-        grads_kernel,
-        out_shape=[piece] * NEAR + [jax.ShapeDtypeStruct((NEAR * WIDTH, 8, LANES), f32)],
-        in_specs=[SMEM_SPEC] + [pl.BlockSpec(memory_space=pltpu.HBM)] * 4,
-        out_specs=[VMEM_SPEC] * (NEAR + 1),
+            out[near * WIDTH + other] = total
+
+
+def local_gains(hidden, cot, weight, inv_wide, p1):
+    return pl.pallas_call(
+        gains_kernel,
+        out_shape=[
+            jax.ShapeDtypeStruct(p1.shape, bf16),
+            jax.ShapeDtypeStruct((NEAR * WIDTH, 8, LANES), f32),
+        ],
+        in_specs=[HBM_SPEC] * 3 + [VMEM_SPEC] * 2,
+        out_specs=[VMEM_SPEC] * 2,
         scratch_shapes=[
             pltpu.VMEM(hidden.shape, bf16),
             pltpu.VMEM(cot.shape, bf16),
-            pltpu.VMEM(gain.shape, f32),
             pltpu.VMEM(weight.shape, bf16),
-            pltpu.VMEM((hidden.shape[0], LANES), f32),
-            pltpu.VMEM((NEAR, FAR * PIECE, LANES), bf16),
             pltpu.VMEM((FAR, LANES), f32),
-            pltpu.SemaphoreType.DMA((11,)),
-        ],
-        compiler_params=PARAMS,
-        name="local_grads",
-    )(place, hidden, cot, gain, weight)
+            pltpu.SemaphoreType.DMA((5,)),
+        ],
+        compiler_params=PARAMS,
+        cost_estimate=pl.CostEstimate(
+            flops=2 * hidden.shape[0] * weight.size,
+            bytes_accessed=2 * (hidden.size + weight.size),
+            transcendentals=0,
+        ),
+        name="local_gains",
+    )(in_hbm(hidden), in_hbm(cot), in_hbm(weight), inv_wide, p1)
 
 
 def all_sum(x):
     return jnp.sum(jnp.sum(x, axis=0, keepdims=True), axis=1, keepdims=True)
 
 
-def near_dots_kernel(place, gain_parts, p0, p1, p2, p3, out, gain_out):
+def near_dots_kernel(place, p3, p2, p1, p0, gain_parts, out, gain_out):
     refs = (p0, p1, p2, p3)
     pairs = [(a, b) for a in range(NEAR) for b in range(a, NEAR)]
     rows = 64
@@ -174,7 +227,7 @@
         out_specs=[VMEM_SPEC] * 2,
         compiler_params=PARAMS,
         name="near_dots",
-    )(place, gain_parts, *pieces)
+    )(place, *pieces[::-1], gain_parts)
 
 
 def near_shares(dots):
@@ -198,6 +251,10 @@
     return (of_low * low[0], of_low * low[1], of_high * high[0], of_high * high[1])
 
 
+def sent_at(far):
+    return far % FAR_Z * (FAR // FAR_Z) + far // FAR_Z
+
+
 def packed(dots):
     total = dots[0:8]
     for block in range(1, 4):
@@ -214,7 +271,7 @@
     return jnp.concatenate(blocks, axis=0)
 
 
-def near_merge_kernel(place, dots, gains, p0, p1, p2, p3, out):
+def near_merge_kernel(place, p3, p2, p1, p0, dots, gains, out):
     here = place[0]
     row = jnp.sum(dots[...], axis=0)
     lane = lax.broadcasted_iota(jnp.int32, (1, LANES), 1)
@@ -241,7 +298,7 @@
         total = by_apart[0] * p0[rows, :].astype(f32)
         for share, ref in zip(by_apart[1:], (p1, p2, p3)):
             total = total + share * ref[rows, :].astype(f32)
-        out[far, pl.ds(0, PIECE), :] = total.astype(bf16)
+        out[sent_at(far), pl.ds(0, PIECE), :] = total.astype(bf16)
 
     gain_shares = shares_at(GAIN_AT)
     merged = gain_shares[0] * gains[pl.ds(0, 8), :]
@@ -249,7 +306,7 @@
         merged = merged + gain_shares[near] * gains[pl.ds(8 * near, 8), :]
     merged = unpacked(merged)
     for far in range(FAR):
-        out[far, pl.ds(PIECE, 8), :] = jnp.broadcast_to(merged[far : far + 1], (8, LANES)).astype(bf16)
+        out[sent_at(far), pl.ds(PIECE, 8), :] = jnp.broadcast_to(merged[far : far + 1], (8, LANES)).astype(bf16)
 
 
 def near_merge(place, dots, gains, pieces):
@@ -260,12 +317,12 @@
         out_specs=VMEM_SPEC,
         compiler_params=PARAMS,
         name="near_merge",
-    )(place, dots, gains, *pieces)
+    )(place, *pieces[::-1], dots, gains)
 
 
 def far_dots_kernel(values, out, by_row, wide):
     for far in range(FAR):
-        wide[pl.ds(far * (PIECE + 8), PIECE + 8), :] = values[far].astype(f32)
+        wide[pl.ds(far * (PIECE + 8), PIECE + 8), :] = values[sent_at(far)].astype(f32)
     columns = []
     for row in range(PIECE + 1):
         block = wide[pl.ds(row, FAR, stride=PIECE + 8), :]
@@ -358,11 +415,15 @@
 
 def body(hidden_states, key_cotangent, norm_gain, key_weight):
     place = lax.axis_index("zl").astype(jnp.int32).reshape(1)
-    *pieces, gain_parts = local_grads(
-        place, hidden_states, key_cotangent, norm_gain.reshape(FAR, LANES), key_weight
+    *pieces, inv_wide = local_grads(
+        place, hidden_states, key_cotangent, norm_gain.reshape(FAR, LANES)
     )
     with jax.named_scope("near_exchange"):
-        arrived = {apart: paired(pieces[apart], "zl", apart) for apart in (2, 3, 1)}
+        arrived = {apart: paired(pieces[apart], "zl", apart) for apart in (3, 2)}
+        piece, gain_parts = local_gains(
+            hidden_states, key_cotangent, key_weight, inv_wide, pieces[1]
+        )
+        arrived[1] = paired(piece, "zl", 1)
     with jax.named_scope("gain_exchange"):
         gain_parts = exchanged(gain_parts, ("zl", "x", "core"))
     pieces = [pieces[0]] + [arrived[apart] for apart in range(1, NEAR)]
@@ -371,7 +432,7 @@
         dots = exchanged(dots, ("zl", "x", "core"))
     values = near_merge(place, dots, gains, pieces)
     with jax.named_scope("far_exchange"):
-        values = exchanged(values, ("y", "zh"))
+        values = exchanged(values, ("zh", "y"))
     dots, by_row = far_dots(values)
     with jax.named_scope("far_dots_sum"):
         dots = jnp.sum(exchanged(dots, ("y", "x", "core")), axis=0)

time: 185 us -> 181 us (0.978)
  waiting for transfers between devices: 21 us -> 16.5 us
  local copies, waits for them, and re-layouts: 4.36 us -> 0 us
  Pallas kernels: 6.46 us -> 8.79 us
    all_to_all x3, blocking collectives: 87.9 us -> 96.6 us  [exchanged(): return lax.all_to_all(x, axes, 0, 0)]
    psum x2, blocking collectives: 38.8 us -> 31.7 us  [body(): dots = lax.psum(lax.psum(dots, 'zl'), 'zh')]
    ppermute x3, waiting for transfers between devices: 21 us -> 16.5 us  [paired(): lax.ppermute(x, axis, [(i, i ^ apart) for i in range(lax.axis_size(axis))])]
    unnamed x8 -> x0, local copies, waits for them, and re-layouts: 4.36 us -> none
    pallas_call x0 -> x1, Pallas kernels: none -> 3.1 us  [local_gains(): pl.pallas_call(gains_kernel, out_shape=[jax.ShapeDtypeStruct(p1.shape, bf...]
  transfers between devices with their start and end apart: 4 -> 4, of which waited for: 3 -> 2; matrix products, arithmetic and copies ran while one was open for 0% -> 0% of each run, Pallas kernels for 0% -> 0%
where the time goes in v3:
time: 181 us; the launch traced here: 180 us
  blocking collectives  128 us (71%)
  starting transfers between devices  26 us (14%)
  waiting for transfers between devices  16.5 us (9%)
  Pallas kernels  8.79 us (5%)
    all_to_all x3, blocking collectives, exchanged(): return lax.all_to_all(x, axes, 0, 0)  96.6 us
    psum x2, blocking collectives, body(): dots = lax.psum(lax.psum(dots, 'zl'), 'zh')  31.7 us
    ppermute x3, waiting for transfers between devices, paired(): lax.ppermute(x, axis, [(i, i ^ apart) for i in range(lax.axis_size(axis))])  16.5 us
    all_to_all x1, starting transfers between devices, exchanged(): return lax.all_to_all(x, axes, 0, 0)  16.3 us
    ppermute x3, starting transfers between devices, paired(): lax.ppermute(x, axis, [(i, i ^ apart) for i in range(lax.axis_size(axis))])  9.67 us
  transfers between devices with their start and end apart: 4, of which 2 were waited for; matrix products, arithmetic and copies ran while one was open for 0% of the time, Pallas kernels for 0%

profile of v3, /device:TPU:32, one launch (start us, length us, event | category | flops | bytes accessed | tf_op | source)
XLA Modules:
  0.0 180.2 jit_solution(17899531028693143730)
XLA Ops:
  0.6 3.0 %local_grads.1 = (bf16[1024,128]{1,0:T(8,128)(2,1)S(1)}, bf16[1024,128]{1,0:T(8,128)(2,1)S(1)}, bf16[1024,128]{1,0:T(8,128)(2,1)S(1)}, bf16[1024,128]{1,0:T(8,128)(2,1)S(1)}, f32[256,128]{1,0:T(8,128)S(1)}) custom-call(s32[1]{0:T(128)} %bitcast.place, bf16[256,4096]{1,0:T(8,128)(2,1)} %hidden_hbm.3, bf16[256,128]{1,0:T(8,128)(2,1)} %cot_hbm.3, f32[32,128]{1,0:T(8,128)} %bitcast.3), custom_call_target="tpu_custom_call" | custom-call | tf_op jit(solution)/shard_map/local_grads/pallas_call | solution.py:89
  3.7 3.1 %local_gains.1 = (bf16[1024,128]{1,0:T(8,128)(2,1)S(1)}, f32[32,8,128]{2,1,0:T(8,128)}) custom-call(bf16[256,4096]{1,0:T(8,128)(2,1)} %hidden_hbm.3, bf16[256,128]{1,0:T(8,128)(2,1)} %cot_hbm.3, bf16[4096,128]{1,0:T(8,128)(2,1)} %weight_hbm.1, f32[256,128]{1,0:T(8,128)S(1)} %get-tuple-element.17.inv_wide, bf16[1024,128]{1,0:T(8,128)(2,1)S(1)} %get-tuple-element.18.p1), custom_call_target="tpu_custom_call" | custom-call | flops 268435456 | bytes 3145728 | tf_op jit(solution)/shard_map/near_exchange/local_gains/pallas_call | solution.py:156
  6.8 16.3 %all-to-all-start = ((f32[32,8,128]{2,1,0:T(8,128)}), f32[32,8,128]{2,1,0:T(8,128)S(1)}, u32[]{:S(2)}, u32[]{:S(2)}) async-start(f32[32,8,128]{2,1,0:T(8,128)} %get-tuple-element.21), calls=%async_computation | async-start | bytes 262144 | tf_op jit(solution)/shard_map/gain_exchange/all_to_all | solution.py:413
  23.1 3.4 %collective-permute-start = (bf16[1024,128]{1,0:T(8,128)(2,1)S(1)}, bf16[1024,128]{1,0:T(8,128)(2,1)S(1)}, u32[]{:S(2)}, u32[]{:S(2)}) collective-permute-start(bf16[1024,128]{1,0:T(8,128)(2,1)S(1)} %get-tuple-element.15), channel_id=1, source_target_pairs={{0,24},{8,16},{16,8},{24,0},{1,25},{9,17},{17,9},{25,1},{2,26},{10... | collective-permute-start | bytes 786440 | tf_op jit(solution)/shard_map/near_exchange/ppermute | solution.py:409
  26.5 3.1 %collective-permute-start.1 = (bf16[1024,128]{1,0:T(8,128)(2,1)S(1)}, bf16[1024,128]{1,0:T(8,128)(2,1)S(1)}, u32[]{:S(2)}, u32[]{:S(2)}) collective-permute-start(bf16[1024,128]{1,0:T(8,128)(2,1)S(1)} %get-tuple-element.16), channel_id=1, source_target_pairs={{0,16},{8,24},{16,0},{24,8},{1,17},{9,25},{17,1},{25,9},{2,18},{10... | collective-permute-start | bytes 786440 | tf_op jit(solution)/shard_map/near_exchange/ppermute | solution.py:409
  29.6 3.2 %collective-permute-start.2 = (bf16[1024,128]{1,0:T(8,128)(2,1)S(1)}, bf16[1024,128]{1,0:T(8,128)(2,1)S(1)}, u32[]{:S(2)}, u32[]{:S(2)}) collective-permute-start(bf16[1024,128]{1,0:T(8,128)(2,1)S(1)} %get-tuple-element.19), channel_id=1, source_target_pairs={{0,8},{8,0},{16,24},{24,16},{1,9},{9,1},{17,25},{25,17},{2,10},{10... | collective-permute-start | bytes 786440 | tf_op jit(solution)/shard_map/near_exchange/ppermute | solution.py:409
  32.8 12.8 %collective-permute-done.p3 = bf16[1024,128]{1,0:T(8,128)(2,1)S(1)} collective-permute-done((bf16[1024,128]{1,0:T(8,128)(2,1)S(1)}, bf16[1024,128]{1,0:T(8,128)(2,1)S(1)}, u32[]{:S(2)}, u32[]{:S(2)}) %collective-permute-start) | collective-permute-done | bytes 262176 | tf_op jit(solution)/shard_map/near_exchange/ppermute | solution.py:409
  45.6 3.7 %collective-permute-done.1.p2 = bf16[1024,128]{1,0:T(8,128)(2,1)S(1)} collective-permute-done((bf16[1024,128]{1,0:T(8,128)(2,1)S(1)}, bf16[1024,128]{1,0:T(8,128)(2,1)S(1)}, u32[]{:S(2)}, u32[]{:S(2)}) %collective-permute-start.1) | collective-permute-done | bytes 262176 | tf_op jit(solution)/shard_map/near_exchange/ppermute | solution.py:409
  49.3 0.0 collective-permute-done.2.p1
  49.3 0.0 all-to-all-done.gain_parts
  49.3 0.7 near_dots.1
  49.9 15.0 %all_to_all.20.dots = f32[32,1,128]{2,1,0:T(1,128)S(1)} all-to-all(f32[32,1,128]{2,1,0:T(1,128)S(1)} %get-tuple-element.22), channel_id=1, replica_groups=mesh['y'=4,'zh'=8,'zl'=4,'x'=4,'core'=2] {'zl','x','core'}, dimensions={0} | all-to-all | bytes 32768 | tf_op jit(solution)/shard_map/near_dots_sum/all_to_all | solution.py:413
  64.9 0.4 near_merge.1
  65.3 66.8 %all_to_all.21.values = bf16[32,40,128]{2,1,0:T(8,128)(2,1)S(1)} all-to-all(bf16[32,40,128]{2,1,0:T(8,128)(2,1)S(1)} %near_merge.1), channel_id=1, replica_groups=mesh['y'=4,'zh'=8,'zl'=4,'x'=4,'core'=2] {'zh','y'}, dimensions={0} | all-to-all | bytes 655360 | tf_op jit(solution)/shard_map/far_exchange/all_to_all | solution.py:413
  132.2 0.4 far_dots.1
  132.5 14.7 %all_to_all.22 = f32[32,16,128]{2,1,0:T(8,128)S(1)} all-to-all(f32[32,16,128]{2,1,0:T(8,128)S(1)} %get-tuple-element.24), channel_id=1, replica_groups=mesh['y'=4,'zh'=8,'zl'=4,'x'=4,'core'=2] {'y','x','core'}, dimensions={0} | all-to-all | bytes 524288 | tf_op jit(solution)/shard_map/far_dots_sum/all_to_all | solution.py:413
  147.3 8.6 %psum.14 = f32[16,128]{1,0:T(8,128)S(1)} all-reduce(f32[16,128]{1,0:T(8,128)S(1)} %reduce_sum.9), channel_id=1, replica_groups=mesh['y'=4,'zh'=8,'zl'=4,'x'=4,'core'=2] {'zl'}, use_global_device_ids=true, to_apply=%region_1.0 | all-reduce | flops 2048 | bytes 16384 | tf_op jit(solution)/shard_map/far_dots_sum/psum | solution.py:439
  155.9 23.0 %psum.15.dots = f32[16,128]{1,0:T(8,128)S(1)} all-reduce(f32[16,128]{1,0:T(8,128)S(1)} %psum.14), channel_id=1, replica_groups=mesh['y'=4,'zh'=8,'zl'=4,'x'=4,'core'=2] {'zh'}, use_global_device_ids=true, to_apply=%region_2.0 | all-reduce | flops 2048 | bytes 16384 | tf_op jit(solution)/shard_map/far_dots_sum/psum | solution.py:439
  178.9 1.3 far_merge.1
  (1 shorter events, 0.0 us)
Async XLA Ops:
  6.8 42.5 %all-to-all-start = ((f32[32,8,128]{2,1,0:T(8,128)}), f32[32,8,128]{2,1,0:T(8,128)S(1)}, u32[]{:S(2)}, u32[]{:S(2)}) async-start(f32[32,8,128]{2,1,0:T(8,128)} %get-tuple-element.21), calls=%async_computation | async-start | bytes 262144 | tf_op jit(solution)/shard_map/gain_exchange/all_to_all | solution.py:413
  23.1 22.5 %collective-permute-start = (bf16[1024,128]{1,0:T(8,128)(2,1)S(1)}, bf16[1024,128]{1,0:T(8,128)(2,1)S(1)}, u32[]{:S(2)}, u32[]{:S(2)}) collective-permute-start(bf16[1024,128]{1,0:T(8,128)(2,1)S(1)} %get-tuple-element.15), channel_id=1, source_target_pairs={{0,24},{8,16},{16,8},{24,0},{1,25},{9,17},{17,9},{25,1},{2,26},{10... | collective-permute-start | bytes 786440 | tf_op jit(solution)/shard_map/near_exchange/ppermute | solution.py:409
  26.5 22.7 %collective-permute-start.1 = (bf16[1024,128]{1,0:T(8,128)(2,1)S(1)}, bf16[1024,128]{1,0:T(8,128)(2,1)S(1)}, u32[]{:S(2)}, u32[]{:S(2)}) collective-permute-start(bf16[1024,128]{1,0:T(8,128)(2,1)S(1)} %get-tuple-element.16), channel_id=1, source_target_pairs={{0,16},{8,24},{16,0},{24,8},{1,17},{9,25},{17,1},{25,9},{2,18},{10... | collective-permute-start | bytes 786440 | tf_op jit(solution)/shard_map/near_exchange/ppermute | solution.py:409
  29.6 19.7 %collective-permute-start.2 = (bf16[1024,128]{1,0:T(8,128)(2,1)S(1)}, bf16[1024,128]{1,0:T(8,128)(2,1)S(1)}, u32[]{:S(2)}, u32[]{:S(2)}) collective-permute-start(bf16[1024,128]{1,0:T(8,128)(2,1)S(1)} %get-tuple-element.19), channel_id=1, source_target_pairs={{0,8},{8,0},{16,24},{24,16},{1,9},{9,1},{17,25},{25,17},{2,10},{10... | collective-permute-start | bytes 786440 | tf_op jit(solution)/shard_map/near_exchange/ppermute | solution.py:409

commit v4 on v3

--- a/solution.py
+++ b/solution.py
@@ -16,7 +16,7 @@
 FAR = 32
 FAR_Z = 8
 WIDTH = 8
-GAIN_AT = 16
+NEAR_PAIRS = [(a, b) for a in range(NEAR) for b in range(a, NEAR)]
 PIECE = 32
 LANES = 128
 VMEM_SPEC = pl.BlockSpec(memory_space=pltpu.VMEM)
@@ -104,7 +104,7 @@
 
 
 def gains_kernel(
-    hidden_hbm, cot_hbm, weight_hbm, inv_wide, p1, p1_out, out, hidden, cot, weight, rows, sems
+    hidden_hbm, cot_hbm, weight_hbm, inv_wide, rows, hidden, cot, weight, sems
 ):
     blocks = hidden.shape[1] // LANES
     step = 4 * LANES
@@ -121,7 +121,6 @@
         )
     for copy in copies:
         copy.start()
-    p1_out[...] = p1[...]
     for copy in copies[:3]:
         copy.wait()
     for chunk in range(blocks // 4):
@@ -141,31 +140,18 @@
             rows[pl.ds(block, 1), :] = jnp.sum(
                 back[:, sub * LANES : (sub + 1) * LANES] * normed, axis=0, keepdims=True
             )
-    lane = lax.broadcasted_iota(jnp.int32, (8, LANES), 1)
-    for near in range(NEAR):
-        total = jnp.zeros((8, LANES), f32)
-        for block in range(4):
-            part = jnp.where(lane // PIECE == near, rows[pl.ds(8 * block, 8), :], 0.0)
-            turn = PIECE * (block - near) % LANES
-            total = total + (pltpu.roll(part, turn, 1) if turn else part)
-        for other in range(WIDTH):
-            out[near * WIDTH + other] = total
-
-
-def local_gains(hidden, cot, weight, inv_wide, p1):
+
+
+def local_gains(hidden, cot, weight, inv_wide):
     return pl.pallas_call(
         gains_kernel,
-        out_shape=[
-            jax.ShapeDtypeStruct(p1.shape, bf16),
-            jax.ShapeDtypeStruct((NEAR * WIDTH, 8, LANES), f32),
-        ],
-        in_specs=[HBM_SPEC] * 3 + [VMEM_SPEC] * 2,
-        out_specs=[VMEM_SPEC] * 2,
+        out_shape=jax.ShapeDtypeStruct((FAR, LANES), f32),
+        in_specs=[HBM_SPEC] * 3 + [VMEM_SPEC],
+        out_specs=VMEM_SPEC,
         scratch_shapes=[
             pltpu.VMEM(hidden.shape, bf16),
             pltpu.VMEM(cot.shape, bf16),
             pltpu.VMEM(weight.shape, bf16),
-            pltpu.VMEM((FAR, LANES), f32),
             pltpu.SemaphoreType.DMA((5,)),
         ],
         compiler_params=PARAMS,
@@ -175,16 +161,16 @@
             transcendentals=0,
         ),
         name="local_gains",
-    )(in_hbm(hidden), in_hbm(cot), in_hbm(weight), inv_wide, p1)
+    )(in_hbm(hidden), in_hbm(cot), in_hbm(weight), inv_wide)
 
 
 def all_sum(x):
     return jnp.sum(jnp.sum(x, axis=0, keepdims=True), axis=1, keepdims=True)
 
 
-def near_dots_kernel(place, p3, p2, p1, p0, gain_parts, out, gain_out):
+def near_dots_kernel(place, p3, p2, p1, p0, gains, out, gain_out):
     refs = (p0, p1, p2, p3)
-    pairs = [(a, b) for a in range(NEAR) for b in range(a, NEAR)]
+    pairs = NEAR_PAIRS
     rows = 64
 
     def add(step, totals):
@@ -204,30 +190,32 @@
         dot = all_sum(total)
         row = jnp.where(lane == ((NEAR * a + b) ^ (5 * here)), dot, row)
         row = jnp.where(lane == ((NEAR * b + a) ^ (5 * here)), dot, row)
-    gain = []
-    for near in range(NEAR):
-        total = gain_parts[near * WIDTH]
-        for other in range(1, WIDTH):
-            total = total + gain_parts[near * WIDTH + other]
-        gain.append(total.astype(bf16).astype(f32))
-        gain_out[pl.ds(8 * near, 8), :] = gain[near]
-    for a, b in pairs:
-        row = jnp.where(lane == GAIN_AT + NEAR * a + b, all_sum(gain[a] * gain[b]), row)
     out[...] = jnp.broadcast_to(row.reshape(1, 1, LANES), out.shape)
-
-
-def near_dots(place, gain_parts, pieces):
+    gain = [gains[near] for near in range(NEAR)]
+    gain_shares = near_shares(
+        [[all_sum(gain[a] * gain[b]) if a <= b else None for b in range(NEAR)] for a in range(NEAR)]
+    )
+    merged = gain_shares[0] * gain[0]
+    for near in range(1, NEAR):
+        merged = merged + gain_shares[near] * gain[near]
+    gain_out[...] = merged
+
+
+def near_dots(place, pieces, gains):
     return pl.pallas_call(
         near_dots_kernel,
         out_shape=[
             jax.ShapeDtypeStruct((NEAR * WIDTH, 1, LANES), f32),
-            jax.ShapeDtypeStruct((NEAR * 8, LANES), f32),
+            jax.ShapeDtypeStruct((FAR, LANES), f32),
         ],
-        in_specs=[SMEM_SPEC] + [VMEM_SPEC] * (1 + NEAR),
+        in_specs=[SMEM_SPEC] + [VMEM_SPEC] * (NEAR + 1),
         out_specs=[VMEM_SPEC] * 2,
         compiler_params=PARAMS,
+        cost_estimate=pl.CostEstimate(
+            flops=20 * pieces[0].size, bytes_accessed=8 * pieces[0].size, transcendentals=0
+        ),
         name="near_dots",
-    )(place, *pieces[::-1], gain_parts)
+    )(place, *pieces[::-1], gains)
 
 
 def near_shares(dots):
@@ -275,18 +263,11 @@
     here = place[0]
     row = jnp.sum(dots[...], axis=0)
     lane = lax.broadcasted_iota(jnp.int32, (1, LANES), 1)
-    row = jnp.where(lane < GAIN_AT, row, row * (1.0 / WIDTH))
-
-    def shares_at(first):
-        def entry(a, b):
-            at = first + NEAR * a + b
-            return jnp.sum(jnp.where(lane == at, row, 0.0), axis=1, keepdims=True)
-
-        return near_shares(
-            [[entry(a, b) if a <= b else None for b in range(NEAR)] for a in range(NEAR)]
-        )
-
-    shares = shares_at(0)
+
+    def entry(a, b):
+        return jnp.sum(jnp.where(lane == NEAR * a + b, row, 0.0), axis=1, keepdims=True)
+
+    shares = near_shares([[entry(a, b) if a <= b else None for b in range(NEAR)] for a in range(NEAR)])
     by_apart = []
     for apart in range(NEAR):
         share = shares[apart]
@@ -300,11 +281,7 @@
             total = total + share * ref[rows, :].astype(f32)
         out[sent_at(far), pl.ds(0, PIECE), :] = total.astype(bf16)
 
-    gain_shares = shares_at(GAIN_AT)
-    merged = gain_shares[0] * gains[pl.ds(0, 8), :]
-    for near in range(1, NEAR):
-        merged = merged + gain_shares[near] * gains[pl.ds(8 * near, 8), :]
-    merged = unpacked(merged)
+    merged = gains[...]
     for far in range(FAR):
         out[sent_at(far), pl.ds(PIECE, 8), :] = jnp.broadcast_to(merged[far : far + 1], (8, LANES)).astype(bf16)
 
@@ -338,7 +315,7 @@
         )
 
     key_rows = packed(dots(jnp.concatenate(columns[:PIECE], axis=1)))
-    gain_rows = packed(dots(columns[PIECE])) * (1.0 / WIDTH)
+    gain_rows = packed(dots(columns[PIECE])) * (1.0 / (NEAR * WIDTH))
     out[...] = jnp.broadcast_to(jnp.concatenate([key_rows, gain_rows], axis=0)[None], out.shape)
 
 
@@ -377,7 +354,7 @@
     return share
 
 
-def far_merge_kernel(dots, by_row, key_out, gain_out):
+def far_merge_kernel(place, dots, by_row, key_out, gain_out):
     key_share = far_shares(unpacked(dots[pl.ds(0, 8), :]))
     gain_share = far_shares(unpacked(dots[pl.ds(8, 8), :]))
     key_wide = jnp.broadcast_to(key_share, (FAR, LANES))
@@ -388,21 +365,25 @@
         )
     key_out[...] = jnp.concatenate(rows, axis=0).astype(bf16)
     gain = jnp.sum(gain_share * by_row[pl.ds(PIECE * FAR, FAR), :], axis=0, keepdims=True)
-    gain_out[...] = gain[:, :PIECE].astype(bf16)
-
-
-def far_merge(dots, by_row):
+    wide = jnp.broadcast_to(gain, (8, LANES))
+    moved = wide
+    for near in range(1, NEAR):
+        moved = jnp.where(place[0] == near, pltpu.roll(wide, LANES - PIECE * near, 1), moved)
+    gain_out[...] = moved[0:1, :PIECE].astype(bf16)
+
+
+def far_merge(place, dots, by_row):
     return pl.pallas_call(
         far_merge_kernel,
         out_shape=[
             jax.ShapeDtypeStruct((PIECE, LANES), bf16),
             jax.ShapeDtypeStruct((1, PIECE), bf16),
         ],
-        in_specs=[VMEM_SPEC] * 2,
+        in_specs=[SMEM_SPEC] + [VMEM_SPEC] * 2,
         out_specs=[VMEM_SPEC] * 2,
         compiler_params=PARAMS,
         name="far_merge",
-    )(dots, by_row)
+    )(place, dots, by_row)
 
 
 def paired(x, axis, apart):
@@ -419,25 +400,23 @@
         place, hidden_states, key_cotangent, norm_gain.reshape(FAR, LANES)
     )
     with jax.named_scope("near_exchange"):
-        arrived = {apart: paired(pieces[apart], "zl", apart) for apart in (3, 2)}
-        piece, gain_parts = local_gains(
-            hidden_states, key_cotangent, key_weight, inv_wide, pieces[1]
-        )
-        arrived[1] = paired(piece, "zl", 1)
-    with jax.named_scope("gain_exchange"):
-        gain_parts = exchanged(gain_parts, ("zl", "x", "core"))
+        arrived = {apart: paired(pieces[apart], "zl", apart) for apart in (3, 2, 1)}
+    with jax.named_scope("gain_sum"):
+        gain = local_gains(hidden_states, key_cotangent, key_weight, inv_wide)
+        gain = jnp.sum(lax.all_gather(gain, ("x", "core")), axis=0)
+        gains = lax.all_gather(lax.reduce_precision(gain, 8, 7), "zl")
     pieces = [pieces[0]] + [arrived[apart] for apart in range(1, NEAR)]
-    dots, gains = near_dots(place, gain_parts, pieces)
+    dots, gain = near_dots(place, pieces, gains)
     with jax.named_scope("near_dots_sum"):
         dots = exchanged(dots, ("zl", "x", "core"))
-    values = near_merge(place, dots, gains, pieces)
+    values = near_merge(place, dots, gain, pieces)
     with jax.named_scope("far_exchange"):
         values = exchanged(values, ("zh", "y"))
     dots, by_row = far_dots(values)
     with jax.named_scope("far_dots_sum"):
         dots = jnp.sum(exchanged(dots, ("y", "x", "core")), axis=0)
         dots = lax.psum(lax.psum(dots, "zl"), "zh")
-    merged_key, merged_gain = far_merge(dots, by_row)
+    merged_key, merged_gain = far_merge(place, dots, by_row)
     return (merged_key, merged_gain.reshape(PIECE))
 
 

time: 181 us -> 181 us (level)
  blocking collectives: 128 us -> 151 us
  waiting for transfers between devices: 16.5 us -> 0.01 us
  starting transfers between devices: 26 us -> 20.9 us
    all_gather x0 -> x2, blocking collectives: none -> 24.1 us  [the longest x1 12.8 us: body(): gain = jnp.sum(lax.all_gather(gain, ('x', 'core')), axis=0)]
    ppermute x3, waiting for transfers between devices: 16.5 us -> 0.01 us  [paired(): lax.ppermute(x, axis, [(i, i ^ apart) for i in range(lax.axis_size(axis))])]
    all_to_all x1 -> x0, starting transfers between devices: 16.3 us -> none  [exchanged(): return lax.all_to_all(x, axes, 0, 0)]
    ppermute x3, starting transfers between devices: 9.67 us -> 20.9 us  [paired(): lax.ppermute(x, axis, [(i, i ^ apart) for i in range(lax.axis_size(axis))])]
  transfers between devices with their start and end apart: 4 -> 3, of which waited for: 2 -> 0; matrix products, arithmetic and copies ran while one was open for 0% -> 0% of each run, Pallas kernels for 0% -> 1%
where the time goes in v4:
time: 181 us
  blocking collectives  151 us (83%)
  starting transfers between devices  20.9 us (12%)
  Pallas kernels  8.08 us (4%)
    all_to_all x3, blocking collectives, exchanged(): return lax.all_to_all(x, axes, 0, 0)  95 us
    psum x2, blocking collectives, body(): dots = lax.psum(lax.psum(dots, 'zl'), 'zh')  31.7 us
    ppermute x3, starting transfers between devices, paired(): lax.ppermute(x, axis, [(i, i ^ apart) for i in range(lax.axis_size(axis))])  20.9 us
    all_gather x1, blocking collectives, body(): gain = jnp.sum(lax.all_gather(gain, ('x', 'core')), axis=0)  12.8 us
    all_gather x1, blocking collectives, body(): gains = lax.all_gather(lax.reduce_precision(gain, 8, 7), 'zl')  11.4 us
  transfers between devices with their start and end apart: 3, of which 0 were waited for; matrix products, arithmetic and copies ran while one was open for 0% of the time, Pallas kernels for 1%

profile of v4, /device:TPU:32, one launch (start us, length us, event | category | flops | bytes accessed | tf_op | source)
XLA Modules:
  0.0 180.5 jit_solution(13226111844176407858)
XLA Ops:
  0.6 3.0 %local_grads.1 = (bf16[1024,128]{1,0:T(8,128)(2,1)S(1)}, bf16[1024,128]{1,0:T(8,128)(2,1)S(1)}, bf16[1024,128]{1,0:T(8,128)(2,1)S(1)}, bf16[1024,128]{1,0:T(8,128)(2,1)S(1)}, f32[256,128]{1,0:T(8,128)S(1)}) custom-call(s32[1]{0:T(128)} %bitcast.place, bf16[256,4096]{1,0:T(8,128)(2,1)} %hidden_hbm.3, bf16[256,128]{1,0:T(8,128)(2,1)} %cot_hbm.3, f32[32,128]{1,0:T(8,128)} %bitcast.7), custom_call_target="tpu_custom_call" | custom-call | tf_op jit(solution)/shard_map/local_grads/pallas_call | solution.py:89
  3.7 3.8 %collective-permute-start = (bf16[1024,128]{1,0:T(8,128)(2,1)S(1)}, bf16[1024,128]{1,0:T(8,128)(2,1)S(1)}, u32[]{:S(2)}, u32[]{:S(2)}) collective-permute-start(bf16[1024,128]{1,0:T(8,128)(2,1)S(1)} %get-tuple-element.13), channel_id=1, source_target_pairs={{0,24},{8,16},{16,8},{24,0},{1,25},{9,17},{17,9},{25,1},{2,26},{10... | collective-permute-start | bytes 786440 | tf_op jit(solution)/shard_map/near_exchange/ppermute | solution.py:390
  7.5 15.1 %collective-permute-start.1 = (bf16[1024,128]{1,0:T(8,128)(2,1)S(1)}, bf16[1024,128]{1,0:T(8,128)(2,1)S(1)}, u32[]{:S(2)}, u32[]{:S(2)}) collective-permute-start(bf16[1024,128]{1,0:T(8,128)(2,1)S(1)} %get-tuple-element.14), channel_id=1, source_target_pairs={{0,16},{8,24},{16,0},{24,8},{1,17},{9,25},{17,1},{25,9},{2,18},{10... | collective-permute-start | bytes 786440 | tf_op jit(solution)/shard_map/near_exchange/ppermute | solution.py:390
  22.6 1.9 %collective-permute-start.2 = (bf16[1024,128]{1,0:T(8,128)(2,1)S(1)}, bf16[1024,128]{1,0:T(8,128)(2,1)S(1)}, u32[]{:S(2)}, u32[]{:S(2)}) collective-permute-start(bf16[1024,128]{1,0:T(8,128)(2,1)S(1)} %get-tuple-element.15), channel_id=1, source_target_pairs={{0,8},{8,0},{16,24},{24,16},{1,9},{9,1},{17,25},{25,17},{2,10},{10... | collective-permute-start | bytes 786440 | tf_op jit(solution)/shard_map/near_exchange/ppermute | solution.py:390
  24.6 2.4 %local_gains.1 = f32[32,128]{1,0:T(8,128)S(1)} custom-call(bf16[256,4096]{1,0:T(8,128)(2,1)} %hidden_hbm.3, bf16[256,128]{1,0:T(8,128)(2,1)} %cot_hbm.3, bf16[4096,128]{1,0:T(8,128)(2,1)} %weight_hbm.1, f32[256,128]{1,0:T(8,128)S(1)} %get-tuple-element.17.inv_wide), custom_call_target="tpu_custom_call" | custom-call | flops 268435456 | bytes 3145728 | tf_op jit(solution)/shard_map/gain_sum/local_gains/pallas_call | solution.py:146
  27.0 12.8 %all-gather = f32[256,128]{1,0:T(8,128)S(1)} all-gather(f32[32,128]{1,0:T(8,128)S(1)} %local_gains.1), channel_id=2, replica_groups=mesh['y'=4,'zh'=8,'zl'=4,'x'=4,'core'=2] {'x','core'}, dimensions={0}, use_global_device_ids=true | all-gather | bytes 147456 | tf_op jit(solution)/shard_map/gain_sum/all_gather | solution.py:406
  39.7 11.4 %all-gather.1 = f32[128,128]{1,0:T(8,128)S(1)} all-gather(f32[32,128]{1,0:T(8,128)S(1)} %reduce_precision.13), channel_id=3, replica_groups=mesh['y'=4,'zh'=8,'zl'=4,'x'=4,'core'=2] {'zl'}, dimensions={0}, use_global_device_ids=true | all-gather | bytes 81920 | tf_op jit(solution)/shard_map/gain_sum/all_gather | solution.py:407
  51.1 0.0 collective-permute-done.p3
  51.1 0.0 collective-permute-done.1.p2
  51.1 0.0 collective-permute-done.2.p1
  51.2 0.7 near_dots.1
  51.8 13.0 %all_to_all.15.dots = f32[32,1,128]{2,1,0:T(1,128)S(1)} all-to-all(f32[32,1,128]{2,1,0:T(1,128)S(1)} %get-tuple-element.18), channel_id=1, replica_groups=mesh['y'=4,'zh'=8,'zl'=4,'x'=4,'core'=2] {'zl','x','core'}, dimensions={0} | all-to-all | bytes 32768 | tf_op jit(solution)/shard_map/near_dots_sum/all_to_all | solution.py:394
  64.8 0.3 near_merge.1
  65.2 67.3 %all_to_all.16.values = bf16[32,40,128]{2,1,0:T(8,128)(2,1)S(1)} all-to-all(bf16[32,40,128]{2,1,0:T(8,128)(2,1)S(1)} %near_merge.1), channel_id=1, replica_groups=mesh['y'=4,'zh'=8,'zl'=4,'x'=4,'core'=2] {'zh','y'}, dimensions={0} | all-to-all | bytes 655360 | tf_op jit(solution)/shard_map/far_exchange/all_to_all | solution.py:394
  132.4 0.4 far_dots.1
  132.8 14.7 %all_to_all.17 = f32[32,16,128]{2,1,0:T(8,128)S(1)} all-to-all(f32[32,16,128]{2,1,0:T(8,128)S(1)} %get-tuple-element.20), channel_id=1, replica_groups=mesh['y'=4,'zh'=8,'zl'=4,'x'=4,'core'=2] {'y','x','core'}, dimensions={0} | all-to-all | bytes 524288 | tf_op jit(solution)/shard_map/far_dots_sum/all_to_all | solution.py:394
  147.5 8.6 %psum.14 = f32[16,128]{1,0:T(8,128)S(1)} all-reduce(f32[16,128]{1,0:T(8,128)S(1)} %reduce_sum.19), channel_id=1, replica_groups=mesh['y'=4,'zh'=8,'zl'=4,'x'=4,'core'=2] {'zl'}, use_global_device_ids=true, to_apply=%region_2.0 | all-reduce | flops 2048 | bytes 16384 | tf_op jit(solution)/shard_map/far_dots_sum/psum | solution.py:418
  156.2 23.0 %psum.15.dots = f32[16,128]{1,0:T(8,128)S(1)} all-reduce(f32[16,128]{1,0:T(8,128)S(1)} %psum.14), channel_id=1, replica_groups=mesh['y'=4,'zh'=8,'zl'=4,'x'=4,'core'=2] {'zh'}, use_global_device_ids=true, to_apply=%region_3.0 | all-reduce | flops 2048 | bytes 16384 | tf_op jit(solution)/shard_map/far_dots_sum/psum | solution.py:418
  179.2 1.3 far_merge.1
  (3 shorter events, 0.1 us)
Async XLA Ops:
  3.7 47.5 %collective-permute-start = (bf16[1024,128]{1,0:T(8,128)(2,1)S(1)}, bf16[1024,128]{1,0:T(8,128)(2,1)S(1)}, u32[]{:S(2)}, u32[]{:S(2)}) collective-permute-start(bf16[1024,128]{1,0:T(8,128)(2,1)S(1)} %get-tuple-element.13), channel_id=1, source_target_pairs={{0,24},{8,16},{16,8},{24,0},{1,25},{9,17},{17,9},{25,1},{2,26},{10... | collective-permute-start | bytes 786440 | tf_op jit(solution)/shard_map/near_exchange/ppermute | solution.py:390
  7.5 43.6 %collective-permute-start.1 = (bf16[1024,128]{1,0:T(8,128)(2,1)S(1)}, bf16[1024,128]{1,0:T(8,128)(2,1)S(1)}, u32[]{:S(2)}, u32[]{:S(2)}) collective-permute-start(bf16[1024,128]{1,0:T(8,128)(2,1)S(1)} %get-tuple-element.14), channel_id=1, source_target_pairs={{0,16},{8,24},{16,0},{24,8},{1,17},{9,25},{17,1},{25,9},{2,18},{10... | collective-permute-start | bytes 786440 | tf_op jit(solution)/shard_map/near_exchange/ppermute | solution.py:390
  22.6 28.5 %collective-permute-start.2 = (bf16[1024,128]{1,0:T(8,128)(2,1)S(1)}, bf16[1024,128]{1,0:T(8,128)(2,1)S(1)}, u32[]{:S(2)}, u32[]{:S(2)}) collective-permute-start(bf16[1024,128]{1,0:T(8,128)(2,1)S(1)} %get-tuple-element.15), channel_id=1, source_target_pairs={{0,8},{8,0},{16,24},{24,16},{1,9},{9,1},{17,25},{25,17},{2,10},{10... | collective-permute-start | bytes 786440 | tf_op jit(solution)/shard_map/near_exchange/ppermute | solution.py:390

commit v5 on v4

--- a/solution.py
+++ b/solution.py
@@ -168,7 +168,7 @@
     return jnp.sum(jnp.sum(x, axis=0, keepdims=True), axis=1, keepdims=True)
 
 
-def near_dots_kernel(place, p3, p2, p1, p0, gains, out, gain_out):
+def near_dots_kernel(place, p3, p2, p1, p0, gain_parts, out, gain_out):
     refs = (p0, p1, p2, p3)
     pairs = NEAR_PAIRS
     rows = 64
@@ -191,22 +191,18 @@
         row = jnp.where(lane == ((NEAR * a + b) ^ (5 * here)), dot, row)
         row = jnp.where(lane == ((NEAR * b + a) ^ (5 * here)), dot, row)
     out[...] = jnp.broadcast_to(row.reshape(1, 1, LANES), out.shape)
-    gain = [gains[near] for near in range(NEAR)]
-    gain_shares = near_shares(
-        [[all_sum(gain[a] * gain[b]) if a <= b else None for b in range(NEAR)] for a in range(NEAR)]
-    )
-    merged = gain_shares[0] * gain[0]
-    for near in range(1, NEAR):
-        merged = merged + gain_shares[near] * gain[near]
-    gain_out[...] = merged
-
-
-def near_dots(place, pieces, gains):
+    total = gain_parts[0]
+    for part in range(1, WIDTH):
+        total = total + gain_parts[part]
+    gain_out[...] = total.astype(bf16)
+
+
+def near_dots(place, pieces, gain_parts):
     return pl.pallas_call(
         near_dots_kernel,
         out_shape=[
             jax.ShapeDtypeStruct((NEAR * WIDTH, 1, LANES), f32),
-            jax.ShapeDtypeStruct((FAR, LANES), f32),
+            jax.ShapeDtypeStruct((FAR, LANES), bf16),
         ],
         in_specs=[SMEM_SPEC] + [VMEM_SPEC] * (NEAR + 1),
         out_specs=[VMEM_SPEC] * 2,
@@ -215,7 +211,7 @@
             flops=20 * pieces[0].size, bytes_accessed=8 * pieces[0].size, transcendentals=0
         ),
         name="near_dots",
-    )(place, *pieces[::-1], gains)
+    )(place, *pieces[::-1], gain_parts)
 
 
 def near_shares(dots):
@@ -236,7 +232,19 @@
     )
     of_low = factor(cross, low_sq)
     of_high = factor(cross, high_sq)
-    return (of_low * low[0], of_low * low[1], of_high * high[0], of_high * high[1])
+    square = (
+        of_low * of_low * low_sq + 2.0 * (of_low * of_high * cross) + of_high * of_high * high_sq
+    )
+    return (of_low * low[0], of_low * low[1], of_high * high[0], of_high * high[1]), square
+
+
+def bf16_parts(x):
+    parts = []
+    for _ in range(3):
+        part = x.astype(bf16).astype(f32)
+        parts.append(part)
+        x = x - part
+    return parts
 
 
 def sent_at(far):
@@ -267,7 +275,7 @@
     def entry(a, b):
         return jnp.sum(jnp.where(lane == NEAR * a + b, row, 0.0), axis=1, keepdims=True)
 
-    shares = near_shares([[entry(a, b) if a <= b else None for b in range(NEAR)] for a in range(NEAR)])
+    shares, square = near_shares([[entry(a, b) if a <= b else None for b in range(NEAR)] for a in range(NEAR)])
     by_apart = []
     for apart in range(NEAR):
         share = shares[apart]
@@ -281,9 +289,20 @@
             total = total + share * ref[rows, :].astype(f32)
         out[sent_at(far), pl.ds(0, PIECE), :] = total.astype(bf16)
 
-    merged = gains[...]
+    gain = [gains[near].astype(f32) for near in range(NEAR)]
+    gain_shares, gain_square = near_shares(
+        [[all_sum(gain[a] * gain[b]) if a <= b else None for b in range(NEAR)] for a in range(NEAR)]
+    )
+    merged = gain_shares[0] * gain[0]
+    for near in range(1, NEAR):
+        merged = merged + gain_shares[near] * gain[near]
+    squares = jnp.zeros((1, LANES), f32)
+    for at, part in enumerate(bf16_parts(square) + bf16_parts(gain_square)):
+        squares = jnp.where(lane == at, part, squares)
+    which = lax.broadcasted_iota(jnp.int32, (8, LANES), 0)
     for far in range(FAR):
-        out[sent_at(far), pl.ds(PIECE, 8), :] = jnp.broadcast_to(merged[far : far + 1], (8, LANES)).astype(bf16)
+        last = jnp.where(which == 0, merged[far : far + 1], jnp.where(which == 1, squares, 0.0))
+        out[sent_at(far), pl.ds(PIECE, 8), :] = last.astype(bf16)
 
 
 def near_merge(place, dots, gains, pieces):
@@ -301,7 +320,7 @@
     for far in range(FAR):
         wide[pl.ds(far * (PIECE + 8), PIECE + 8), :] = values[sent_at(far)].astype(f32)
     columns = []
-    for row in range(PIECE + 1):
+    for row in range(PIECE + 2):
         block = wide[pl.ds(row, FAR, stride=PIECE + 8), :]
         by_row[pl.ds(row * FAR, FAR), :] = block
         columns.append(block.astype(bf16))
@@ -314,17 +333,20 @@
             matrix, padded, (((1,), (1,)), ((), ())), preferred_element_type=f32
         )
 
-    key_rows = packed(dots(jnp.concatenate(columns[:PIECE], axis=1)))
-    gain_rows = packed(dots(columns[PIECE])) * (1.0 / (NEAR * WIDTH))
-    out[...] = jnp.broadcast_to(jnp.concatenate([key_rows, gain_rows], axis=0)[None], out.shape)
+    key_dots = dots(jnp.concatenate(columns[:PIECE], axis=1))
+    gain_dots = dots(columns[PIECE]) * (1.0 / (NEAR * WIDTH))
+    row = lax.broadcasted_iota(jnp.int32, key_dots.shape, 0)
+    lane = lax.broadcasted_iota(jnp.int32, key_dots.shape, 1)
+    both = jnp.where(row < lane, key_dots, jnp.where(row > lane, gain_dots, 0.0))
+    out[...] = jnp.broadcast_to(packed(both)[None], out.shape)
 
 
 def far_dots(values):
     return pl.pallas_call(
         far_dots_kernel,
         out_shape=[
-            jax.ShapeDtypeStruct((4 * WIDTH, 16, LANES), f32),
-            jax.ShapeDtypeStruct(((PIECE + 1) * FAR, LANES), f32),
+            jax.ShapeDtypeStruct((4 * WIDTH, 8, LANES), f32),
+            jax.ShapeDtypeStruct(((PIECE + 2) * FAR, LANES), f32),
         ],
         in_specs=[VMEM_SPEC],
         out_specs=[VMEM_SPEC] * 2,
@@ -334,35 +356,43 @@
     )(values)
 
 
-def far_shares(dots):
-    shape = dots.shape
-    row = lax.broadcasted_iota(jnp.int32, shape, 0)
-    lane = lax.broadcasted_iota(jnp.int32, shape, 1)
-    share = jnp.ones((shape[0], 1), f32)
+def far_shares(dots, squares):
+    row = lax.broadcasted_iota(jnp.int32, dots.shape, 0)
+    lane = lax.broadcasted_iota(jnp.int32, dots.shape, 1)
+    share = jnp.ones((dots.shape[0], 1), f32)
+    square_row = jnp.sum(jnp.where(row == lane, squares, 0.0), axis=0, keepdims=True)
     for level in range(5):
         same = (row >> level) == (lane >> level)
-        across = ((row >> level) ^ 1) == (lane >> level)
+        pair = (row >> (level + 1)) == (lane >> (level + 1))
         own_part = jnp.sum(jnp.where(same, dots, 0.0), axis=0, keepdims=True)
-        cross_part = jnp.sum(jnp.where(across, dots, 0.0), axis=0, keepdims=True)
+        cross_part = jnp.sum(jnp.where(same, 0.0, jnp.where(pair, dots, 0.0)), axis=0, keepdims=True)
+        own_part = 2.0 * own_part + square_row
         own_sq = jnp.sum(jnp.where(same, own_part, 0.0), axis=1, keepdims=True)
-        cross = jnp.sum(jnp.where(same, cross_part, 0.0), axis=1, keepdims=True)
+        cross = jnp.sum(jnp.where(pair, cross_part, 0.0), axis=1, keepdims=True)
         scale = factor(cross, own_sq)
         share = share * scale
         if level < 4:
             scale_row = jnp.sum(jnp.where(row == lane, scale, 0.0), axis=0, keepdims=True)
             dots = dots * scale * scale_row
+            square_row = square_row * scale_row * scale_row
     return share
 
 
 def far_merge_kernel(place, dots, by_row, key_out, gain_out):
-    key_share = far_shares(unpacked(dots[pl.ds(0, 8), :]))
-    gain_share = far_shares(unpacked(dots[pl.ds(8, 8), :]))
+    dots = unpacked(dots[...])
+    row = lax.broadcasted_iota(jnp.int32, dots.shape, 0)
+    lane = lax.broadcasted_iota(jnp.int32, dots.shape, 1)
+    squares = by_row[pl.ds((PIECE + 1) * FAR, FAR), :]
+    key_square = jnp.sum(jnp.where(lane < 3, squares, 0.0), axis=1, keepdims=True)
+    gain_square = jnp.sum(
+        jnp.where(lane < 3, 0.0, jnp.where(lane < 6, squares, 0.0)), axis=1, keepdims=True
+    )
+    key_share = far_shares(jnp.where(row < lane, dots, 0.0), key_square)
+    gain_share = far_shares(jnp.where(row > lane, dots, 0.0), gain_square)
     key_wide = jnp.broadcast_to(key_share, (FAR, LANES))
     rows = []
-    for row in range(PIECE):
-        rows.append(
-            jnp.sum(key_wide * by_row[pl.ds(row * FAR, FAR), :], axis=0, keepdims=True)
-        )
+    for at in range(PIECE):
+        rows.append(jnp.sum(key_wide * by_row[pl.ds(at * FAR, FAR), :], axis=0, keepdims=True))
     key_out[...] = jnp.concatenate(rows, axis=0).astype(bf16)
     gain = jnp.sum(gain_share * by_row[pl.ds(PIECE * FAR, FAR), :], axis=0, keepdims=True)
     wide = jnp.broadcast_to(gain, (8, LANES))
@@ -401,15 +431,16 @@
     )
     with jax.named_scope("near_exchange"):
         arrived = {apart: paired(pieces[apart], "zl", apart) for apart in (3, 2, 1)}
-    with jax.named_scope("gain_sum"):
+    with jax.named_scope("gain_parts"):
         gain = local_gains(hidden_states, key_cotangent, key_weight, inv_wide)
-        gain = jnp.sum(lax.all_gather(gain, ("x", "core")), axis=0)
-        gains = lax.all_gather(lax.reduce_precision(gain, 8, 7), "zl")
+        gain_parts = lax.all_gather(gain, ("x", "core"))
     pieces = [pieces[0]] + [arrived[apart] for apart in range(1, NEAR)]
-    dots, gain = near_dots(place, pieces, gains)
+    dots, gain = near_dots(place, pieces, gain_parts)
     with jax.named_scope("near_dots_sum"):
         dots = exchanged(dots, ("zl", "x", "core"))
-    values = near_merge(place, dots, gain, pieces)
+    with jax.named_scope("near_gains"):
+        gains = lax.all_gather(gain, "zl")
+    values = near_merge(place, dots, gains, pieces)
     with jax.named_scope("far_exchange"):
         values = exchanged(values, ("zh", "y"))
     dots, by_row = far_dots(values)

time: 181 us -> 174 us (0.961)
  the two profiles are of different devices: /device:TPU:32 before, /device:TPU:2 now
where the time goes in v5:
time: 174 us
  blocking collectives  147 us (84%)
  starting transfers between devices  17.5 us (10%)
  Pallas kernels  8.72 us (5%)
    all_to_all x2, blocking collectives, exchanged(): return lax.all_to_all(x, axes, 0, 0)  78.8 us
    psum x2, blocking collectives, body(): dots = lax.psum(lax.psum(dots, 'zl'), 'zh')  32.9 us
    all_gather x1, blocking collectives, body(): gain_parts = lax.all_gather(gain, ('x', 'core'))  21.9 us
    all_gather x1, blocking collectives, body(): gains = lax.all_gather(gain, 'zl')  13.2 us
    ppermute x3, starting transfers between devices, paired(): lax.ppermute(x, axis, [(i, i ^ apart) for i in range(lax.axis_size(axis))])  10.9 us
    all_to_all x1, starting transfers between devices, exchanged(): return lax.all_to_all(x, axes, 0, 0)  6.6 us
  transfers between devices with their start and end apart: 4, of which 0 were waited for; matrix products, arithmetic and copies ran while one was open for 0% of the time, Pallas kernels for 1%

profile of v5, /device:TPU:2, one launch (start us, length us, event | category | flops | bytes accessed | tf_op | source)
XLA Modules:
  0.0 173.9 jit_solution(14915707026019399923)
XLA Ops:
  0.6 3.0 %local_grads.1 = (bf16[1024,128]{1,0:T(8,128)(2,1)S(1)}, bf16[1024,128]{1,0:T(8,128)(2,1)S(1)}, bf16[1024,128]{1,0:T(8,128)(2,1)S(1)}, bf16[1024,128]{1,0:T(8,128)(2,1)S(1)}, f32[256,128]{1,0:T(8,128)S(1)}) custom-call(s32[1]{0:T(128)} %bitcast.place, bf16[256,4096]{1,0:T(8,128)(2,1)} %hidden_hbm.3, bf16[256,128]{1,0:T(8,128)(2,1)} %cot_hbm.3, f32[32,128]{1,0:T(8,128)} %bitcast.7), custom_call_target="tpu_custom_call" | custom-call | tf_op jit(solution)/shard_map/local_grads/pallas_call | solution.py:89
  3.7 6.5 %collective-permute-start = (bf16[1024,128]{1,0:T(8,128)(2,1)S(1)}, bf16[1024,128]{1,0:T(8,128)(2,1)S(1)}, u32[]{:S(2)}, u32[]{:S(2)}) collective-permute-start(bf16[1024,128]{1,0:T(8,128)(2,1)S(1)} %get-tuple-element.13), channel_id=1, source_target_pairs={{0,24},{8,16},{16,8},{24,0},{1,25},{9,17},{17,9},{25,1},{2,26},{10... | collective-permute-start | bytes 786440 | tf_op jit(solution)/shard_map/near_exchange/ppermute | solution.py:420
  10.2 1.9 %collective-permute-start.1 = (bf16[1024,128]{1,0:T(8,128)(2,1)S(1)}, bf16[1024,128]{1,0:T(8,128)(2,1)S(1)}, u32[]{:S(2)}, u32[]{:S(2)}) collective-permute-start(bf16[1024,128]{1,0:T(8,128)(2,1)S(1)} %get-tuple-element.14), channel_id=1, source_target_pairs={{0,16},{8,24},{16,0},{24,8},{1,17},{9,25},{17,1},{25,9},{2,18},{10... | collective-permute-start | bytes 786440 | tf_op jit(solution)/shard_map/near_exchange/ppermute | solution.py:420
  12.2 2.5 %collective-permute-start.2 = (bf16[1024,128]{1,0:T(8,128)(2,1)S(1)}, bf16[1024,128]{1,0:T(8,128)(2,1)S(1)}, u32[]{:S(2)}, u32[]{:S(2)}) collective-permute-start(bf16[1024,128]{1,0:T(8,128)(2,1)S(1)} %get-tuple-element.15), channel_id=1, source_target_pairs={{0,8},{8,0},{16,24},{24,16},{1,9},{9,1},{17,25},{25,17},{2,10},{10... | collective-permute-start | bytes 786440 | tf_op jit(solution)/shard_map/near_exchange/ppermute | solution.py:420
  14.6 2.4 %local_gains.1 = f32[32,128]{1,0:T(8,128)S(1)} custom-call(bf16[256,4096]{1,0:T(8,128)(2,1)} %hidden_hbm.3, bf16[256,128]{1,0:T(8,128)(2,1)} %cot_hbm.3, bf16[4096,128]{1,0:T(8,128)(2,1)} %weight_hbm.1, f32[256,128]{1,0:T(8,128)S(1)} %get-tuple-element.17.inv_wide), custom_call_target="tpu_custom_call" | custom-call | flops 268435456 | bytes 3145728 | tf_op jit(solution)/shard_map/gain_parts/local_gains/pallas_call | solution.py:146
  17.0 21.9 %all-gather = f32[256,128]{1,0:T(8,128)S(1)} all-gather(f32[32,128]{1,0:T(8,128)S(1)} %local_gains.1), channel_id=2, replica_groups=mesh['y'=4,'zh'=8,'zl'=4,'x'=4,'core'=2] {'x','core'}, dimensions={0}, use_global_device_ids=true | all-gather | bytes 147456 | tf_op jit(solution)/shard_map/gain_parts/all_gather | solution.py:436
  39.0 0.0 collective-permute-done.p3
  39.0 0.0 collective-permute-done.1.p2
  39.0 0.0 collective-permute-done.2.p1
  39.0 1.2 near_dots.1
  40.2 6.6 %all-to-all-start = ((f32[32,1,128]{2,1,0:T(1,128)}), f32[32,1,128]{2,1,0:T(1,128)S(1)}, u32[]{:S(2)}, u32[]{:S(2)}) async-start(f32[32,1,128]{2,1,0:T(1,128)} %get-tuple-element.18), calls=%async_computation | async-start | bytes 32768 | tf_op jit(solution)/shard_map/near_dots_sum/all_to_all | solution.py:424
  46.9 13.2 %all-gather.1 = bf16[128,128]{1,0:T(8,128)(2,1)S(1)} all-gather(bf16[32,128]{1,0:T(8,128)(2,1)S(1)} %get-tuple-element.19), channel_id=3, replica_groups=mesh['y'=4,'zh'=8,'zl'=4,'x'=4,'core'=2] {'zl'}, dimensions={0}, use_global_device_ids=true | all-gather | bytes 40960 | tf_op jit(solution)/shard_map/near_gains/all_gather | solution.py:442
  60.1 0.0 all-to-all-done.dots
  60.1 0.4 near_merge.1
  60.5 66.3 %all_to_all.15.values = bf16[32,40,128]{2,1,0:T(8,128)(2,1)S(1)} all-to-all(bf16[32,40,128]{2,1,0:T(8,128)(2,1)S(1)} %near_merge.1), channel_id=1, replica_groups=mesh['y'=4,'zh'=8,'zl'=4,'x'=4,'core'=2] {'zh','y'}, dimensions={0} | all-to-all | bytes 655360 | tf_op jit(solution)/shard_map/far_exchange/all_to_all | solution.py:424
  126.8 0.3 far_dots.1
  127.1 12.5 %all_to_all.16 = f32[32,8,128]{2,1,0:T(8,128)S(1)} all-to-all(f32[32,8,128]{2,1,0:T(8,128)S(1)} %get-tuple-element.20), channel_id=1, replica_groups=mesh['y'=4,'zh'=8,'zl'=4,'x'=4,'core'=2] {'y','x','core'}, dimensions={0} | all-to-all | bytes 262144 | tf_op jit(solution)/shard_map/far_dots_sum/all_to_all | solution.py:424
  139.7 11.8 %psum.14 = f32[8,128]{1,0:T(8,128)S(1)} all-reduce(f32[8,128]{1,0:T(8,128)S(1)} %reduce_sum.9), channel_id=1, replica_groups=mesh['y'=4,'zh'=8,'zl'=4,'x'=4,'core'=2] {'zl'}, use_global_device_ids=true, to_apply=%region_1.0 | all-reduce | flops 1024 | bytes 8192 | tf_op jit(solution)/shard_map/far_dots_sum/psum | solution.py:449
  151.5 21.1 %psum.15.dots = f32[8,128]{1,0:T(8,128)S(1)} all-reduce(f32[8,128]{1,0:T(8,128)S(1)} %psum.14), channel_id=1, replica_groups=mesh['y'=4,'zh'=8,'zl'=4,'x'=4,'core'=2] {'zh'}, use_global_device_ids=true, to_apply=%region_2.0 | all-reduce | flops 1024 | bytes 8192 | tf_op jit(solution)/shard_map/far_dots_sum/psum | solution.py:449
  172.6 1.3 far_merge.1
  (1 shorter events, 0.0 us)
Async XLA Ops:
  3.7 35.3 %collective-permute-start = (bf16[1024,128]{1,0:T(8,128)(2,1)S(1)}, bf16[1024,128]{1,0:T(8,128)(2,1)S(1)}, u32[]{:S(2)}, u32[]{:S(2)}) collective-permute-start(bf16[1024,128]{1,0:T(8,128)(2,1)S(1)} %get-tuple-element.13), channel_id=1, source_target_pairs={{0,24},{8,16},{16,8},{24,0},{1,25},{9,17},{17,9},{25,1},{2,26},{10... | collective-permute-start | bytes 786440 | tf_op jit(solution)/shard_map/near_exchange/ppermute | solution.py:420
  10.2 28.8 %collective-permute-start.1 = (bf16[1024,128]{1,0:T(8,128)(2,1)S(1)}, bf16[1024,128]{1,0:T(8,128)(2,1)S(1)}, u32[]{:S(2)}, u32[]{:S(2)}) collective-permute-start(bf16[1024,128]{1,0:T(8,128)(2,1)S(1)} %get-tuple-element.14), channel_id=1, source_target_pairs={{0,16},{8,24},{16,0},{24,8},{1,17},{9,25},{17,1},{25,9},{2,18},{10... | collective-permute-start | bytes 786440 | tf_op jit(solution)/shard_map/near_exchange/ppermute | solution.py:420
  12.2 26.8 %collective-permute-start.2 = (bf16[1024,128]{1,0:T(8,128)(2,1)S(1)}, bf16[1024,128]{1,0:T(8,128)(2,1)S(1)}, u32[]{:S(2)}, u32[]{:S(2)}) collective-permute-start(bf16[1024,128]{1,0:T(8,128)(2,1)S(1)} %get-tuple-element.15), channel_id=1, source_target_pairs={{0,8},{8,0},{16,24},{24,16},{1,9},{9,1},{17,25},{25,17},{2,10},{10... | collective-permute-start | bytes 786440 | tf_op jit(solution)/shard_map/near_exchange/ppermute | solution.py:420
  40.2 19.9 %all-to-all-start = ((f32[32,1,128]{2,1,0:T(1,128)}), f32[32,1,128]{2,1,0:T(1,128)S(1)}, u32[]{:S(2)}, u32[]{:S(2)}) async-start(f32[32,1,128]{2,1,0:T(1,128)} %get-tuple-element.18), calls=%async_computation | async-start | bytes 32768 | tf_op jit(solution)/shard_map/near_dots_sum/all_to_all | solution.py:424

commit v6 on v5

--- a/solution.py
+++ b/solution.py
@@ -16,6 +16,7 @@
 FAR = 32
 FAR_Z = 8
 WIDTH = 8
+GAIN_ROWS = FAR // WIDTH
 NEAR_PAIRS = [(a, b) for a in range(NEAR) for b in range(a, NEAR)]
 PIECE = 32
 LANES = 128
@@ -79,7 +80,7 @@
             for near in range(NEAR):
                 at = sub * LANES + near * PIECE
                 pieces[near, pl.ds((4 * chunk + sub) * PIECE, PIECE), :] = grad[at : at + PIECE]
-    here = place[0]
+    here = place[0] // WIDTH
     for apart, out in enumerate((p0, p1, p2, p3)):
         out[...] = pieces[here ^ apart]
 
@@ -168,7 +169,7 @@
     return jnp.sum(jnp.sum(x, axis=0, keepdims=True), axis=1, keepdims=True)
 
 
-def near_dots_kernel(place, p3, p2, p1, p0, gain_parts, out, gain_out):
+def near_dots_kernel(place, p3, p2, p1, p0, gain_parts, out, shares_of):
     refs = (p0, p1, p2, p3)
     pairs = NEAR_PAIRS
     rows = 64
@@ -183,29 +184,32 @@
     totals = lax.fori_loop(
         0, p0.shape[0] // rows, add, tuple(jnp.zeros((8, LANES), f32) for _ in pairs)
     )
-    here = place[0]
+    here = place[0] // WIDTH
     lane = lax.broadcasted_iota(jnp.int32, (1, LANES), 1)
     row = jnp.zeros((1, LANES), f32)
     for total, (a, b) in zip(totals, pairs):
         dot = all_sum(total)
         row = jnp.where(lane == ((NEAR * a + b) ^ (5 * here)), dot, row)
         row = jnp.where(lane == ((NEAR * b + a) ^ (5 * here)), dot, row)
-    out[...] = jnp.broadcast_to(row.reshape(1, 1, LANES), out.shape)
     total = gain_parts[0]
     for part in range(1, WIDTH):
         total = total + gain_parts[part]
-    gain_out[...] = total.astype(bf16)
+    total = total.astype(bf16).astype(f32)
+    for part in range(WIDTH):
+        shares_of[part] = total[part * GAIN_ROWS : (part + 1) * GAIN_ROWS]
+    message = jnp.concatenate(
+        [row, shares_of[place[0] % WIDTH], jnp.zeros((7 - GAIN_ROWS, LANES), f32)], axis=0
+    )
+    out[...] = jnp.broadcast_to(message[None], out.shape)
 
 
 def near_dots(place, pieces, gain_parts):
     return pl.pallas_call(
         near_dots_kernel,
-        out_shape=[
-            jax.ShapeDtypeStruct((NEAR * WIDTH, 1, LANES), f32),
-            jax.ShapeDtypeStruct((FAR, LANES), bf16),
-        ],
+        out_shape=jax.ShapeDtypeStruct((NEAR * WIDTH, 8, LANES), f32),
         in_specs=[SMEM_SPEC] + [VMEM_SPEC] * (NEAR + 1),
-        out_specs=[VMEM_SPEC] * 2,
+        out_specs=VMEM_SPEC,
+        scratch_shapes=[pltpu.VMEM((WIDTH, GAIN_ROWS, LANES), f32)],
         compiler_params=PARAMS,
         cost_estimate=pl.CostEstimate(
             flops=20 * pieces[0].size, bytes_accessed=8 * pieces[0].size, transcendentals=0
@@ -267,9 +271,9 @@
     return jnp.concatenate(blocks, axis=0)
 
 
-def near_merge_kernel(place, p3, p2, p1, p0, dots, gains, out):
-    here = place[0]
-    row = jnp.sum(dots[...], axis=0)
+def near_merge_kernel(place, p3, p2, p1, p0, messages, out, gains):
+    here = place[0] // WIDTH
+    row = jnp.sum(messages[:, pl.ds(0, 1), :], axis=0)
     lane = lax.broadcasted_iota(jnp.int32, (1, LANES), 1)
 
     def entry(a, b):
@@ -289,7 +293,12 @@
             total = total + share * ref[rows, :].astype(f32)
         out[sent_at(far), pl.ds(0, PIECE), :] = total.astype(bf16)
 
-    gain = [gains[near].astype(f32) for near in range(NEAR)]
+    for near in range(NEAR):
+        for part in range(WIDTH):
+            gains[near, pl.ds(part * GAIN_ROWS, GAIN_ROWS), :] = messages[
+                near * WIDTH + part, pl.ds(1, GAIN_ROWS), :
+            ]
+    gain = [gains[near] for near in range(NEAR)]
     gain_shares, gain_square = near_shares(
         [[all_sum(gain[a] * gain[b]) if a <= b else None for b in range(NEAR)] for a in range(NEAR)]
     )
@@ -305,15 +314,16 @@
         out[sent_at(far), pl.ds(PIECE, 8), :] = last.astype(bf16)
 
 
-def near_merge(place, dots, gains, pieces):
+def near_merge(place, messages, pieces):
     return pl.pallas_call(
         near_merge_kernel,
         out_shape=jax.ShapeDtypeStruct((FAR, PIECE + 8, LANES), bf16),
-        in_specs=[SMEM_SPEC] + [VMEM_SPEC] * (2 + NEAR),
+        in_specs=[SMEM_SPEC] + [VMEM_SPEC] * (1 + NEAR),
         out_specs=VMEM_SPEC,
+        scratch_shapes=[pltpu.VMEM((NEAR, FAR, LANES), f32)],
         compiler_params=PARAMS,
         name="near_merge",
-    )(place, *pieces[::-1], dots, gains)
+    )(place, *pieces[::-1], messages)
 
 
 def far_dots_kernel(values, out, by_row, wide):
@@ -398,7 +408,7 @@
     wide = jnp.broadcast_to(gain, (8, LANES))
     moved = wide
     for near in range(1, NEAR):
-        moved = jnp.where(place[0] == near, pltpu.roll(wide, LANES - PIECE * near, 1), moved)
+        moved = jnp.where(place[0] // WIDTH == near, pltpu.roll(wide, LANES - PIECE * near, 1), moved)
     gain_out[...] = moved[0:1, :PIECE].astype(bf16)
 
 
@@ -425,7 +435,7 @@
 
 
 def body(hidden_states, key_cotangent, norm_gain, key_weight):
-    place = lax.axis_index("zl").astype(jnp.int32).reshape(1)
+    place = lax.axis_index(("zl", "x", "core")).astype(jnp.int32).reshape(1)
     *pieces, inv_wide = local_grads(
         place, hidden_states, key_cotangent, norm_gain.reshape(FAR, LANES)
     )
@@ -435,12 +445,10 @@
         gain = local_gains(hidden_states, key_cotangent, key_weight, inv_wide)
         gain_parts = lax.all_gather(gain, ("x", "core"))
     pieces = [pieces[0]] + [arrived[apart] for apart in range(1, NEAR)]
-    dots, gain = near_dots(place, pieces, gain_parts)
+    messages = near_dots(place, pieces, gain_parts)
     with jax.named_scope("near_dots_sum"):
-        dots = exchanged(dots, ("zl", "x", "core"))
-    with jax.named_scope("near_gains"):
-        gains = lax.all_gather(gain, "zl")
-    values = near_merge(place, dots, gains, pieces)
+        messages = exchanged(messages, ("zl", "x", "core"))
+    values = near_merge(place, messages, pieces)
     with jax.named_scope("far_exchange"):
         values = exchanged(values, ("zh", "y"))
     dots, by_row = far_dots(values)

time: 174 us -> 170 us (0.977)
  starting transfers between devices: 17.5 us -> 10.9 us
  blocking collectives: 147 us -> 150 us
    all_gather x1 -> x0, blocking collectives: 13.2 us -> none  [body(): gains = lax.all_gather(gain, 'zl')]
    all_to_all x2 -> x3, blocking collectives: 78.8 us -> 87.9 us  [exchanged(): return lax.all_to_all(x, axes, 0, 0)]
    psum x2, blocking collectives: 32.9 us -> 39.7 us  [body(): dots = lax.psum(lax.psum(dots, 'zl'), 'zh')]
    all_to_all x1 -> x0, starting transfers between devices: 6.6 us -> none  [exchanged(): return lax.all_to_all(x, axes, 0, 0)]
  transfers between devices with their start and end apart: 4 -> 3, of which waited for: 0 -> 0; matrix products, arithmetic and copies ran while one was open for 0% -> 0% of each run, Pallas kernels for 1% -> 1%
where the time goes in v6:
time: 170 us; the launch traced here: 169 us
  blocking collectives  150 us (88%)
  starting transfers between devices  10.9 us (6%)
  Pallas kernels  8.17 us (5%)
    all_to_all x3, blocking collectives, exchanged(): return lax.all_to_all(x, axes, 0, 0)  87.9 us
    psum x2, blocking collectives, body(): dots = lax.psum(lax.psum(dots, 'zl'), 'zh')  39.7 us
    all_gather x1, blocking collectives, body(): gain_parts = lax.all_gather(gain, ('x', 'core'))  21.9 us
    ppermute x3, starting transfers between devices, paired(): lax.ppermute(x, axis, [(i, i ^ apart) for i in range(lax.axis_size(axis))])  10.9 us
  transfers between devices with their start and end apart: 3, of which 0 were waited for; matrix products, arithmetic and copies ran while one was open for 0% of the time, Pallas kernels for 1%

profile of v6, /device:TPU:2, one launch (start us, length us, event | category | flops | bytes accessed | tf_op | source)
XLA Modules:
  0.0 169.5 jit_solution(1486953622400015798)
XLA Ops:
  0.6 3.0 %local_grads.1 = (bf16[1024,128]{1,0:T(8,128)(2,1)S(1)}, bf16[1024,128]{1,0:T(8,128)(2,1)S(1)}, bf16[1024,128]{1,0:T(8,128)(2,1)S(1)}, bf16[1024,128]{1,0:T(8,128)(2,1)S(1)}, f32[256,128]{1,0:T(8,128)S(1)}) custom-call(s32[1]{0:T(128)} %bitcast.place, bf16[256,4096]{1,0:T(8,128)(2,1)} %hidden_hbm.3, bf16[256,128]{1,0:T(8,128)(2,1)} %cot_hbm.3, f32[32,128]{1,0:T(8,128)} %bitcast.5), custom_call_target="tpu_custom_call" | custom-call | tf_op jit(solution)/shard_map/local_grads/pallas_call | solution.py:90
  3.7 6.5 %collective-permute-start = (bf16[1024,128]{1,0:T(8,128)(2,1)S(1)}, bf16[1024,128]{1,0:T(8,128)(2,1)S(1)}, u32[]{:S(2)}, u32[]{:S(2)}) collective-permute-start(bf16[1024,128]{1,0:T(8,128)(2,1)S(1)} %get-tuple-element.11), channel_id=1, source_target_pairs={{0,24},{8,16},{16,8},{24,0},{1,25},{9,17},{17,9},{25,1},{2,26},{10... | collective-permute-start | bytes 786440 | tf_op jit(solution)/shard_map/near_exchange/ppermute | solution.py:430
  10.2 1.9 %collective-permute-start.1 = (bf16[1024,128]{1,0:T(8,128)(2,1)S(1)}, bf16[1024,128]{1,0:T(8,128)(2,1)S(1)}, u32[]{:S(2)}, u32[]{:S(2)}) collective-permute-start(bf16[1024,128]{1,0:T(8,128)(2,1)S(1)} %get-tuple-element.12), channel_id=1, source_target_pairs={{0,16},{8,24},{16,0},{24,8},{1,17},{9,25},{17,1},{25,9},{2,18},{10... | collective-permute-start | bytes 786440 | tf_op jit(solution)/shard_map/near_exchange/ppermute | solution.py:430
  12.2 2.5 %collective-permute-start.2 = (bf16[1024,128]{1,0:T(8,128)(2,1)S(1)}, bf16[1024,128]{1,0:T(8,128)(2,1)S(1)}, u32[]{:S(2)}, u32[]{:S(2)}) collective-permute-start(bf16[1024,128]{1,0:T(8,128)(2,1)S(1)} %get-tuple-element.13), channel_id=1, source_target_pairs={{0,8},{8,0},{16,24},{24,16},{1,9},{9,1},{17,25},{25,17},{2,10},{10... | collective-permute-start | bytes 786440 | tf_op jit(solution)/shard_map/near_exchange/ppermute | solution.py:430
  14.6 2.4 %local_gains.1 = f32[32,128]{1,0:T(8,128)S(1)} custom-call(bf16[256,4096]{1,0:T(8,128)(2,1)} %hidden_hbm.3, bf16[256,128]{1,0:T(8,128)(2,1)} %cot_hbm.3, bf16[4096,128]{1,0:T(8,128)(2,1)} %weight_hbm.1, f32[256,128]{1,0:T(8,128)S(1)} %get-tuple-element.15.inv_wide), custom_call_target="tpu_custom_call" | custom-call | flops 268435456 | bytes 3145728 | tf_op jit(solution)/shard_map/gain_parts/local_gains/pallas_call | solution.py:147
  17.0 21.9 %all-gather = f32[256,128]{1,0:T(8,128)S(1)} all-gather(f32[32,128]{1,0:T(8,128)S(1)} %local_gains.1), channel_id=2, replica_groups=mesh['y'=4,'zh'=8,'zl'=4,'x'=4,'core'=2] {'x','core'}, dimensions={0}, use_global_device_ids=true | all-gather | bytes 147456 | tf_op jit(solution)/shard_map/gain_parts/all_gather | solution.py:446
  39.0 0.0 collective-permute-done.p3
  39.0 0.0 collective-permute-done.1.p2
  39.0 0.0 collective-permute-done.2.p1
  39.0 0.7 near_dots.1
  39.7 13.4 %all_to_all.15.messages = f32[32,8,128]{2,1,0:T(8,128)S(1)} all-to-all(f32[32,8,128]{2,1,0:T(8,128)S(1)} %near_dots.1), channel_id=1, replica_groups=mesh['y'=4,'zh'=8,'zl'=4,'x'=4,'core'=2] {'zl','x','core'}, dimensions={0} | all-to-all | bytes 262144 | tf_op jit(solution)/shard_map/near_dots_sum/all_to_all | solution.py:434
  53.1 0.4 near_merge.1
  53.5 63.2 %all_to_all.16.values = bf16[32,40,128]{2,1,0:T(8,128)(2,1)S(1)} all-to-all(bf16[32,40,128]{2,1,0:T(8,128)(2,1)S(1)} %near_merge.1), channel_id=1, replica_groups=mesh['y'=4,'zh'=8,'zl'=4,'x'=4,'core'=2] {'zh','y'}, dimensions={0} | all-to-all | bytes 655360 | tf_op jit(solution)/shard_map/far_exchange/all_to_all | solution.py:434
  116.6 0.3 far_dots.1
  117.0 11.4 %all_to_all.17 = f32[32,8,128]{2,1,0:T(8,128)S(1)} all-to-all(f32[32,8,128]{2,1,0:T(8,128)S(1)} %get-tuple-element.16), channel_id=1, replica_groups=mesh['y'=4,'zh'=8,'zl'=4,'x'=4,'core'=2] {'y','x','core'}, dimensions={0} | all-to-all | bytes 262144 | tf_op jit(solution)/shard_map/far_dots_sum/all_to_all | solution.py:434
  128.4 18.8 %psum.14 = f32[8,128]{1,0:T(8,128)S(1)} all-reduce(f32[8,128]{1,0:T(8,128)S(1)} %reduce_sum.9), channel_id=1, replica_groups=mesh['y'=4,'zh'=8,'zl'=4,'x'=4,'core'=2] {'zl'}, use_global_device_ids=true, to_apply=%region_1.0 | all-reduce | flops 1024 | bytes 8192 | tf_op jit(solution)/shard_map/far_dots_sum/psum | solution.py:457
  147.2 21.0 %psum.15.dots = f32[8,128]{1,0:T(8,128)S(1)} all-reduce(f32[8,128]{1,0:T(8,128)S(1)} %psum.14), channel_id=1, replica_groups=mesh['y'=4,'zh'=8,'zl'=4,'x'=4,'core'=2] {'zh'}, use_global_device_ids=true, to_apply=%region_2.0 | all-reduce | flops 1024 | bytes 8192 | tf_op jit(solution)/shard_map/far_dots_sum/psum | solution.py:457
  168.1 1.3 far_merge.1
  (1 shorter events, 0.0 us)
Async XLA Ops:
  3.7 35.3 %collective-permute-start = (bf16[1024,128]{1,0:T(8,128)(2,1)S(1)}, bf16[1024,128]{1,0:T(8,128)(2,1)S(1)}, u32[]{:S(2)}, u32[]{:S(2)}) collective-permute-start(bf16[1024,128]{1,0:T(8,128)(2,1)S(1)} %get-tuple-element.11), channel_id=1, source_target_pairs={{0,24},{8,16},{16,8},{24,0},{1,25},{9,17},{17,9},{25,1},{2,26},{10... | collective-permute-start | bytes 786440 | tf_op jit(solution)/shard_map/near_exchange/ppermute | solution.py:430
  10.2 28.8 %collective-permute-start.1 = (bf16[1024,128]{1,0:T(8,128)(2,1)S(1)}, bf16[1024,128]{1,0:T(8,128)(2,1)S(1)}, u32[]{:S(2)}, u32[]{:S(2)}) collective-permute-start(bf16[1024,128]{1,0:T(8,128)(2,1)S(1)} %get-tuple-element.12), channel_id=1, source_target_pairs={{0,16},{8,24},{16,0},{24,8},{1,17},{9,25},{17,1},{25,9},{2,18},{10... | collective-permute-start | bytes 786440 | tf_op jit(solution)/shard_map/near_exchange/ppermute | solution.py:430
  12.2 26.8 %collective-permute-start.2 = (bf16[1024,128]{1,0:T(8,128)(2,1)S(1)}, bf16[1024,128]{1,0:T(8,128)(2,1)S(1)}, u32[]{:S(2)}, u32[]{:S(2)}) collective-permute-start(bf16[1024,128]{1,0:T(8,128)(2,1)S(1)} %get-tuple-element.13), channel_id=1, source_target_pairs={{0,8},{8,0},{16,24},{24,16},{1,9},{9,1},{17,25},{25,17},{2,10},{10... | collective-permute-start | bytes 786440 | tf_op jit(solution)/shard_map/near_exchange/ppermute | solution.py:430

commit v7 on v6

--- a/solution.py
+++ b/solution.py
@@ -291,7 +291,7 @@
         total = by_apart[0] * p0[rows, :].astype(f32)
         for share, ref in zip(by_apart[1:], (p1, p2, p3)):
             total = total + share * ref[rows, :].astype(f32)
-        out[sent_at(far), pl.ds(0, PIECE), :] = total.astype(bf16)
+        out[sent_at(far), pl.ds(0, PIECE // 2)] = total.astype(bf16).reshape(PIECE // 2, 2, LANES)
 
     for near in range(NEAR):
         for part in range(WIDTH):
@@ -308,16 +308,16 @@
     squares = jnp.zeros((1, LANES), f32)
     for at, part in enumerate(bf16_parts(square) + bf16_parts(gain_square)):
         squares = jnp.where(lane == at, part, squares)
-    which = lax.broadcasted_iota(jnp.int32, (8, LANES), 0)
+    which = lax.broadcasted_iota(jnp.int32, (2, LANES), 0)
     for far in range(FAR):
-        last = jnp.where(which == 0, merged[far : far + 1], jnp.where(which == 1, squares, 0.0))
-        out[sent_at(far), pl.ds(PIECE, 8), :] = last.astype(bf16)
+        last = jnp.where(which == 0, merged[far : far + 1], squares)
+        out[sent_at(far), PIECE // 2] = last.astype(bf16)
 
 
 def near_merge(place, messages, pieces):
     return pl.pallas_call(
         near_merge_kernel,
-        out_shape=jax.ShapeDtypeStruct((FAR, PIECE + 8, LANES), bf16),
+        out_shape=jax.ShapeDtypeStruct((FAR, PIECE // 2 + 1, 2, LANES), bf16),
         in_specs=[SMEM_SPEC] + [VMEM_SPEC] * (1 + NEAR),
         out_specs=VMEM_SPEC,
         scratch_shapes=[pltpu.VMEM((NEAR, FAR, LANES), f32)],
@@ -326,14 +326,17 @@
     )(place, *pieces[::-1], messages)
 
 
-def far_dots_kernel(values, out, by_row, wide):
+def far_dots_kernel(values, out, last, wide):
+    height = PIECE + 8
     for far in range(FAR):
-        wide[pl.ds(far * (PIECE + 8), PIECE + 8), :] = values[sent_at(far)].astype(f32)
-    columns = []
-    for row in range(PIECE + 2):
-        block = wide[pl.ds(row, FAR, stride=PIECE + 8), :]
-        by_row[pl.ds(row * FAR, FAR), :] = block
-        columns.append(block.astype(bf16))
+        at = far * height
+        wide[pl.ds(at, PIECE), :] = piece_of(values, far)
+        wide[pl.ds(at + PIECE, 2), :] = values[sent_at(far), PIECE // 2].astype(f32)
+    columns = [
+        wide[pl.ds(row, FAR, stride=height), :].astype(bf16) for row in range(PIECE + 1)
+    ]
+    for row in range(2):
+        last[pl.ds(row * FAR, FAR), :] = wide[pl.ds(PIECE + row, FAR, stride=height), :]
 
     def dots(matrix):
         padded = jnp.concatenate(
@@ -351,12 +354,16 @@
     out[...] = jnp.broadcast_to(packed(both)[None], out.shape)
 
 
+def piece_of(values, far):
+    return values[sent_at(far), pl.ds(0, PIECE // 2)].reshape(PIECE, LANES).astype(f32)
+
+
 def far_dots(values):
     return pl.pallas_call(
         far_dots_kernel,
         out_shape=[
-            jax.ShapeDtypeStruct((4 * WIDTH, 8, LANES), f32),
-            jax.ShapeDtypeStruct(((PIECE + 2) * FAR, LANES), f32),
+            jax.ShapeDtypeStruct((WIDTH, 8, LANES), f32),
+            jax.ShapeDtypeStruct((2 * FAR, LANES), f32),
         ],
         in_specs=[VMEM_SPEC],
         out_specs=[VMEM_SPEC] * 2,
@@ -364,6 +371,24 @@
         compiler_params=PARAMS,
         name="far_dots",
     )(values)
+
+
+def total_kernel(parts, out):
+    total = parts[0]
+    for part in range(1, parts.shape[0]):
+        total = total + parts[part]
+    out[...] = jnp.broadcast_to(total[None], out.shape)
+
+
+def total_of(parts, copies):
+    return pl.pallas_call(
+        total_kernel,
+        out_shape=jax.ShapeDtypeStruct((copies,) + parts.shape[1:], f32),
+        in_specs=[VMEM_SPEC],
+        out_specs=VMEM_SPEC,
+        compiler_params=PARAMS,
+        name="total_of",
+    )(parts)
 
 
 def far_shares(dots, squares):
@@ -388,11 +413,11 @@
     return share
 
 
-def far_merge_kernel(place, dots, by_row, key_out, gain_out):
+def far_merge_kernel(place, dots, values, last, key_out, gain_out):
     dots = unpacked(dots[...])
     row = lax.broadcasted_iota(jnp.int32, dots.shape, 0)
     lane = lax.broadcasted_iota(jnp.int32, dots.shape, 1)
-    squares = by_row[pl.ds((PIECE + 1) * FAR, FAR), :]
+    squares = last[pl.ds(FAR, FAR), :]
     key_square = jnp.sum(jnp.where(lane < 3, squares, 0.0), axis=1, keepdims=True)
     gain_square = jnp.sum(
         jnp.where(lane < 3, 0.0, jnp.where(lane < 6, squares, 0.0)), axis=1, keepdims=True
@@ -400,11 +425,11 @@
     key_share = far_shares(jnp.where(row < lane, dots, 0.0), key_square)
     gain_share = far_shares(jnp.where(row > lane, dots, 0.0), gain_square)
     key_wide = jnp.broadcast_to(key_share, (FAR, LANES))
-    rows = []
-    for at in range(PIECE):
-        rows.append(jnp.sum(key_wide * by_row[pl.ds(at * FAR, FAR), :], axis=0, keepdims=True))
-    key_out[...] = jnp.concatenate(rows, axis=0).astype(bf16)
-    gain = jnp.sum(gain_share * by_row[pl.ds(PIECE * FAR, FAR), :], axis=0, keepdims=True)
+    totals = [jnp.zeros((PIECE, LANES), f32) for _ in range(2)]
+    for far in range(FAR):
+        totals[far % 2] = totals[far % 2] + key_wide[far : far + 1] * piece_of(values, far)
+    key_out[...] = (totals[0] + totals[1]).astype(bf16)
+    gain = jnp.sum(gain_share * last[pl.ds(0, FAR), :], axis=0, keepdims=True)
     wide = jnp.broadcast_to(gain, (8, LANES))
     moved = wide
     for near in range(1, NEAR):
@@ -412,18 +437,18 @@
     gain_out[...] = moved[0:1, :PIECE].astype(bf16)
 
 
-def far_merge(place, dots, by_row):
+def far_merge(place, dots, values, last):
     return pl.pallas_call(
         far_merge_kernel,
         out_shape=[
             jax.ShapeDtypeStruct((PIECE, LANES), bf16),
             jax.ShapeDtypeStruct((1, PIECE), bf16),
         ],
-        in_specs=[SMEM_SPEC] + [VMEM_SPEC] * 2,
+        in_specs=[SMEM_SPEC] + [VMEM_SPEC] * 3,
         out_specs=[VMEM_SPEC] * 2,
         compiler_params=PARAMS,
         name="far_merge",
-    )(place, dots, by_row)
+    )(place, dots, values, last)
 
 
 def paired(x, axis, apart):
@@ -451,11 +476,12 @@
     values = near_merge(place, messages, pieces)
     with jax.named_scope("far_exchange"):
         values = exchanged(values, ("zh", "y"))
-    dots, by_row = far_dots(values)
+    dots, last = far_dots(values)
     with jax.named_scope("far_dots_sum"):
-        dots = jnp.sum(exchanged(dots, ("y", "x", "core")), axis=0)
-        dots = lax.psum(lax.psum(dots, "zl"), "zh")
-    merged_key, merged_gain = far_merge(place, dots, by_row)
+        dots = total_of(exchanged(dots, ("x", "core")), 4 * NEAR)
+        dots = total_of(exchanged(dots, ("y", "zl")), 1)
+        dots = lax.psum(dots[0], "zh")
+    merged_key, merged_gain = far_merge(place, dots, values, last)
     return (merged_key, merged_gain.reshape(PIECE))
 
 

time: 170 us -> 164 us (0.965)
  blocking collectives: 150 us -> 144 us
    psum x2 -> x1, blocking collectives: 39.7 us -> 21 us  [body(): dots = lax.psum(dots[0], 'zh')]
    all_to_all x3 -> x4, blocking collectives: 87.9 us -> 101 us  [exchanged(): return lax.all_to_all(x, axes, 0, 0)]
where the time goes in v7:
time: 164 us
  blocking collectives  144 us (88%)
  starting transfers between devices  10.9 us (7%)
  Pallas kernels  8.58 us (5%)
    all_to_all x4, blocking collectives, exchanged(): return lax.all_to_all(x, axes, 0, 0)  101 us
    all_gather x1, blocking collectives, body(): gain_parts = lax.all_gather(gain, ('x', 'core'))  21.9 us
    psum x1, blocking collectives, body(): dots = lax.psum(dots[0], 'zh')  21 us
    ppermute x3, starting transfers between devices, paired(): lax.ppermute(x, axis, [(i, i ^ apart) for i in range(lax.axis_size(axis))])  10.9 us
  transfers between devices with their start and end apart: 3, of which 0 were waited for; matrix products, arithmetic and copies ran while one was open for 0% of the time, Pallas kernels for 1%

profile of v7, /device:TPU:2, one launch (start us, length us, event | category | flops | bytes accessed | tf_op | source)
XLA Modules:
  0.0 164.0 jit_solution(2541542107705569121)
XLA Ops:
  0.6 3.0 %local_grads.1 = (bf16[1024,128]{1,0:T(8,128)(2,1)S(1)}, bf16[1024,128]{1,0:T(8,128)(2,1)S(1)}, bf16[1024,128]{1,0:T(8,128)(2,1)S(1)}, bf16[1024,128]{1,0:T(8,128)(2,1)S(1)}, f32[256,128]{1,0:T(8,128)S(1)}) custom-call(s32[1]{0:T(128)} %bitcast.place, bf16[256,4096]{1,0:T(8,128)(2,1)} %hidden_hbm.3, bf16[256,128]{1,0:T(8,128)(2,1)} %cot_hbm.3, f32[32,128]{1,0:T(8,128)} %bitcast.7), custom_call_target="tpu_custom_call" | custom-call | tf_op jit(solution)/shard_map/local_grads/pallas_call | solution.py:90
  3.7 6.5 %collective-permute-start = (bf16[1024,128]{1,0:T(8,128)(2,1)S(1)}, bf16[1024,128]{1,0:T(8,128)(2,1)S(1)}, u32[]{:S(2)}, u32[]{:S(2)}) collective-permute-start(bf16[1024,128]{1,0:T(8,128)(2,1)S(1)} %get-tuple-element.11), channel_id=1, source_target_pairs={{0,24},{8,16},{16,8},{24,0},{1,25},{9,17},{17,9},{25,1},{2,26},{10... | collective-permute-start | bytes 786440 | tf_op jit(solution)/shard_map/near_exchange/ppermute | solution.py:455
  10.2 1.9 %collective-permute-start.1 = (bf16[1024,128]{1,0:T(8,128)(2,1)S(1)}, bf16[1024,128]{1,0:T(8,128)(2,1)S(1)}, u32[]{:S(2)}, u32[]{:S(2)}) collective-permute-start(bf16[1024,128]{1,0:T(8,128)(2,1)S(1)} %get-tuple-element.12), channel_id=1, source_target_pairs={{0,16},{8,24},{16,0},{24,8},{1,17},{9,25},{17,1},{25,9},{2,18},{10... | collective-permute-start | bytes 786440 | tf_op jit(solution)/shard_map/near_exchange/ppermute | solution.py:455
  12.2 2.5 %collective-permute-start.2 = (bf16[1024,128]{1,0:T(8,128)(2,1)S(1)}, bf16[1024,128]{1,0:T(8,128)(2,1)S(1)}, u32[]{:S(2)}, u32[]{:S(2)}) collective-permute-start(bf16[1024,128]{1,0:T(8,128)(2,1)S(1)} %get-tuple-element.13), channel_id=1, source_target_pairs={{0,8},{8,0},{16,24},{24,16},{1,9},{9,1},{17,25},{25,17},{2,10},{10... | collective-permute-start | bytes 786440 | tf_op jit(solution)/shard_map/near_exchange/ppermute | solution.py:455
  14.6 2.4 %local_gains.1 = f32[32,128]{1,0:T(8,128)S(1)} custom-call(bf16[256,4096]{1,0:T(8,128)(2,1)} %hidden_hbm.3, bf16[256,128]{1,0:T(8,128)(2,1)} %cot_hbm.3, bf16[4096,128]{1,0:T(8,128)(2,1)} %weight_hbm.1, f32[256,128]{1,0:T(8,128)S(1)} %get-tuple-element.15.inv_wide), custom_call_target="tpu_custom_call" | custom-call | flops 268435456 | bytes 3145728 | tf_op jit(solution)/shard_map/gain_parts/local_gains/pallas_call | solution.py:147
  17.0 21.9 %all-gather = f32[256,128]{1,0:T(8,128)S(1)} all-gather(f32[32,128]{1,0:T(8,128)S(1)} %local_gains.1), channel_id=2, replica_groups=mesh['y'=4,'zh'=8,'zl'=4,'x'=4,'core'=2] {'x','core'}, dimensions={0}, use_global_device_ids=true | all-gather | bytes 147456 | tf_op jit(solution)/shard_map/gain_parts/all_gather | solution.py:471
  39.0 0.0 collective-permute-done.p3
  39.0 0.0 collective-permute-done.1.p2
  39.0 0.0 collective-permute-done.2.p1
  39.0 0.7 near_dots.1
  39.7 13.4 %all_to_all.20.messages = f32[32,8,128]{2,1,0:T(8,128)S(1)} all-to-all(f32[32,8,128]{2,1,0:T(8,128)S(1)} %near_dots.1), channel_id=1, replica_groups=mesh['y'=4,'zh'=8,'zl'=4,'x'=4,'core'=2] {'zl','x','core'}, dimensions={0} | all-to-all | bytes 262144 | tf_op jit(solution)/shard_map/near_dots_sum/all_to_all | solution.py:459
  53.1 0.5 near_merge.1
  53.6 60.9 %all_to_all.21.values = bf16[32,17,2,128]{3,2,1,0:T(2,128)(2,1)S(1)} all-to-all(bf16[32,17,2,128]{3,2,1,0:T(2,128)(2,1)S(1)} %near_merge.1), channel_id=1, replica_groups=mesh['y'=4,'zh'=8,'zl'=4,'x'=4,'core'=2] {'zh','y'}, dimensions={0} | all-to-all | bytes 557056 | tf_op jit(solution)/shard_map/far_exchange/all_to_all | solution.py:459
  114.5 0.5 far_dots.1
  115.0 7.8 %all_to_all.22.parts = f32[8,8,128]{2,1,0:T(8,128)S(1)} all-to-all(f32[8,8,128]{2,1,0:T(8,128)S(1)} %get-tuple-element.16), channel_id=1, replica_groups=mesh['y'=4,'zh'=8,'zl'=4,'x'=4,'core'=2] {'x','core'}, dimensions={0} | all-to-all | bytes 65536 | tf_op jit(solution)/shard_map/far_dots_sum/all_to_all | solution.py:459
  122.8 18.7 %all_to_all.23.parts = f32[16,8,128]{2,1,0:T(8,128)S(1)} all-to-all(f32[16,8,128]{2,1,0:T(8,128)S(1)} %total_of.2), channel_id=1, replica_groups=mesh['y'=4,'zh'=8,'zl'=4,'x'=4,'core'=2] {'y','zl'}, dimensions={0} | all-to-all | bytes 131072 | tf_op jit(solution)/shard_map/far_dots_sum/all_to_all | solution.py:459
  141.5 21.0 %psum.7.dots = f32[8,128]{1,0:T(8,128)S(1)} all-reduce(f32[8,128]{1,0:T(8,128)S(1)} %bitcast.6), channel_id=1, replica_groups=mesh['y'=4,'zh'=8,'zl'=4,'x'=4,'core'=2] {'zh'}, use_global_device_ids=true, to_apply=%region_0.0 | all-reduce | flops 1024 | bytes 8192 | tf_op jit(solution)/shard_map/far_dots_sum/psum | solution.py:483
  162.5 1.5 far_merge.1
  (2 shorter events, 0.0 us)
Async XLA Ops:
  3.7 35.3 %collective-permute-start = (bf16[1024,128]{1,0:T(8,128)(2,1)S(1)}, bf16[1024,128]{1,0:T(8,128)(2,1)S(1)}, u32[]{:S(2)}, u32[]{:S(2)}) collective-permute-start(bf16[1024,128]{1,0:T(8,128)(2,1)S(1)} %get-tuple-element.11), channel_id=1, source_target_pairs={{0,24},{8,16},{16,8},{24,0},{1,25},{9,17},{17,9},{25,1},{2,26},{10... | collective-permute-start | bytes 786440 | tf_op jit(solution)/shard_map/near_exchange/ppermute | solution.py:455
  10.2 28.8 %collective-permute-start.1 = (bf16[1024,128]{1,0:T(8,128)(2,1)S(1)}, bf16[1024,128]{1,0:T(8,128)(2,1)S(1)}, u32[]{:S(2)}, u32[]{:S(2)}) collective-permute-start(bf16[1024,128]{1,0:T(8,128)(2,1)S(1)} %get-tuple-element.12), channel_id=1, source_target_pairs={{0,16},{8,24},{16,0},{24,8},{1,17},{9,25},{17,1},{25,9},{2,18},{10... | collective-permute-start | bytes 786440 | tf_op jit(solution)/shard_map/near_exchange/ppermute | solution.py:455
  12.2 26.8 %collective-permute-start.2 = (bf16[1024,128]{1,0:T(8,128)(2,1)S(1)}, bf16[1024,128]{1,0:T(8,128)(2,1)S(1)}, u32[]{:S(2)}, u32[]{:S(2)}) collective-permute-start(bf16[1024,128]{1,0:T(8,128)(2,1)S(1)} %get-tuple-element.13), channel_id=1, source_target_pairs={{0,8},{8,0},{16,24},{24,16},{1,9},{9,1},{17,25},{25,17},{2,10},{10... | collective-permute-start | bytes 786440 | tf_op jit(solution)/shard_map/near_exchange/ppermute | solution.py:455

commit v8 on v7

--- a/solution.py
+++ b/solution.py
@@ -60,8 +60,9 @@
         for block in range(blocks):
             x = hidden[rows, pl.ds(block * LANES, LANES)].astype(f32)
             totals[block % 2] = totals[block % 2] + x * x
-        mean = jnp.sum(totals[0] + totals[1], axis=1, keepdims=True) * (1.0 / width)
-        inv_wide[rows, :] = jnp.broadcast_to(lax.rsqrt(mean + eps_norm), (height, LANES))
+        inv_wide[rows, :] = totals[0] + totals[1]
+    mean = jnp.sum(inv_wide[...], axis=1, keepdims=True) * (1.0 / width)
+    inv_wide[...] = jnp.broadcast_to(lax.rsqrt(mean + eps_norm), inv_wide.shape)
     for copy in copies[parts:]:
         copy.wait()
     for chunk in range(blocks // 4):
@@ -192,7 +193,7 @@
         row = jnp.where(lane == ((NEAR * a + b) ^ (5 * here)), dot, row)
         row = jnp.where(lane == ((NEAR * b + a) ^ (5 * here)), dot, row)
     total = gain_parts[0]
-    for part in range(1, WIDTH):
+    for part in range(1, gain_parts.shape[0]):
         total = total + gain_parts[part]
     total = total.astype(bf16).astype(f32)
     for part in range(WIDTH):
@@ -468,7 +469,8 @@
         arrived = {apart: paired(pieces[apart], "zl", apart) for apart in (3, 2, 1)}
     with jax.named_scope("gain_parts"):
         gain = local_gains(hidden_states, key_cotangent, key_weight, inv_wide)
-        gain_parts = lax.all_gather(gain, ("x", "core"))
+        gain_parts = lax.all_gather(lax.all_gather(gain, "core"), "x")
+        gain_parts = gain_parts.reshape(WIDTH, FAR, LANES)
     pieces = [pieces[0]] + [arrived[apart] for apart in range(1, NEAR)]
     messages = near_dots(place, pieces, gain_parts)
     with jax.named_scope("near_dots_sum"):

time: 164 us -> 164 us (level)
    all_gather x1 -> x2, blocking collectives: 21.9 us -> 23 us  [body(): gain_parts = lax.all_gather(lax.all_gather(gain, 'core'), 'x')]
where the time goes in v8:
time: 164 us
  blocking collectives  144 us (88%)
  starting transfers between devices  10.9 us (7%)
  Pallas kernels  8.15 us (5%)
    all_to_all x4, blocking collectives, exchanged(): return lax.all_to_all(x, axes, 0, 0)  99.8 us
    all_gather x2, blocking collectives, body(): gain_parts = lax.all_gather(lax.all_gather(gain, 'core'), 'x')  23 us
    psum x1, blocking collectives, body(): dots = lax.psum(dots[0], 'zh')  21 us
    ppermute x3, starting transfers between devices, paired(): lax.ppermute(x, axis, [(i, i ^ apart) for i in range(lax.axis_size(axis))])  10.9 us
  transfers between devices with their start and end apart: 3, of which 0 were waited for; matrix products, arithmetic and copies ran while one was open for 0% of the time, Pallas kernels for 1%

profile of v8, /device:TPU:2, one launch (start us, length us, event | category | flops | bytes accessed | tf_op | source)
XLA Modules:
  0.0 163.6 jit_solution(14098165955374777165)
XLA Ops:
  0.6 2.6 %local_grads.1 = (bf16[1024,128]{1,0:T(8,128)(2,1)S(1)}, bf16[1024,128]{1,0:T(8,128)(2,1)S(1)}, bf16[1024,128]{1,0:T(8,128)(2,1)S(1)}, bf16[1024,128]{1,0:T(8,128)(2,1)S(1)}, f32[256,128]{1,0:T(8,128)S(1)}) custom-call(s32[1]{0:T(128)} %bitcast.place, bf16[256,4096]{1,0:T(8,128)(2,1)} %hidden_hbm.3, bf16[256,128]{1,0:T(8,128)(2,1)} %cot_hbm.3, f32[32,128]{1,0:T(8,128)} %bitcast.7), custom_call_target="tpu_custom_call" | custom-call | tf_op jit(solution)/shard_map/local_grads/pallas_call | solution.py:91
  3.3 6.5 %collective-permute-start = (bf16[1024,128]{1,0:T(8,128)(2,1)S(1)}, bf16[1024,128]{1,0:T(8,128)(2,1)S(1)}, u32[]{:S(2)}, u32[]{:S(2)}) collective-permute-start(bf16[1024,128]{1,0:T(8,128)(2,1)S(1)} %get-tuple-element.11), channel_id=1, source_target_pairs={{0,24},{8,16},{16,8},{24,0},{1,25},{9,17},{17,9},{25,1},{2,26},{10... | collective-permute-start | bytes 786440 | tf_op jit(solution)/shard_map/near_exchange/ppermute | solution.py:456
  9.8 1.9 %collective-permute-start.1 = (bf16[1024,128]{1,0:T(8,128)(2,1)S(1)}, bf16[1024,128]{1,0:T(8,128)(2,1)S(1)}, u32[]{:S(2)}, u32[]{:S(2)}) collective-permute-start(bf16[1024,128]{1,0:T(8,128)(2,1)S(1)} %get-tuple-element.12), channel_id=1, source_target_pairs={{0,16},{8,24},{16,0},{24,8},{1,17},{9,25},{17,1},{25,9},{2,18},{10... | collective-permute-start | bytes 786440 | tf_op jit(solution)/shard_map/near_exchange/ppermute | solution.py:456
  11.7 2.5 %collective-permute-start.2 = (bf16[1024,128]{1,0:T(8,128)(2,1)S(1)}, bf16[1024,128]{1,0:T(8,128)(2,1)S(1)}, u32[]{:S(2)}, u32[]{:S(2)}) collective-permute-start(bf16[1024,128]{1,0:T(8,128)(2,1)S(1)} %get-tuple-element.13), channel_id=1, source_target_pairs={{0,8},{8,0},{16,24},{24,16},{1,9},{9,1},{17,25},{25,17},{2,10},{10... | collective-permute-start | bytes 786440 | tf_op jit(solution)/shard_map/near_exchange/ppermute | solution.py:456
  14.2 2.4 %local_gains.1 = f32[32,128]{1,0:T(8,128)S(1)} custom-call(bf16[256,4096]{1,0:T(8,128)(2,1)} %hidden_hbm.3, bf16[256,128]{1,0:T(8,128)(2,1)} %cot_hbm.3, bf16[4096,128]{1,0:T(8,128)(2,1)} %weight_hbm.1, f32[256,128]{1,0:T(8,128)S(1)} %get-tuple-element.15.inv_wide), custom_call_target="tpu_custom_call" | custom-call | flops 268435456 | bytes 3145728 | tf_op jit(solution)/shard_map/gain_parts/local_gains/pallas_call | solution.py:148
  16.6 1.8 %all-gather = f32[64,128]{1,0:T(8,128)S(1)} all-gather(f32[32,128]{1,0:T(8,128)S(1)} %local_gains.1), channel_id=2, replica_groups=mesh['y'=4,'zh'=8,'zl'=4,'x'=4,'core'=2] {'core'}, dimensions={0}, use_global_device_ids=true | all-gather | bytes 49152 | tf_op jit(solution)/shard_map/gain_parts/all_gather | solution.py:472
  18.4 21.1 %all-gather.1.gain_parts = f32[8,32,128]{2,1,0:T(8,128)S(1)} all-gather(f32[2,32,128]{2,1,0:T(8,128)S(1)} %bitcast.6), channel_id=3, replica_groups=mesh['y'=4,'zh'=8,'zl'=4,'x'=4,'core'=2] {'x'}, dimensions={0}, use_global_device_ids=true | all-gather | bytes 163840 | tf_op jit(solution)/shard_map/gain_parts/all_gather | solution.py:472
  39.6 0.0 collective-permute-done.p3
  39.6 0.0 collective-permute-done.1.p2
  39.6 0.0 collective-permute-done.2.p1
  39.6 0.7 near_dots.1
  40.2 13.4 %all_to_all.20.messages = f32[32,8,128]{2,1,0:T(8,128)S(1)} all-to-all(f32[32,8,128]{2,1,0:T(8,128)S(1)} %near_dots.1), channel_id=1, replica_groups=mesh['y'=4,'zh'=8,'zl'=4,'x'=4,'core'=2] {'zl','x','core'}, dimensions={0} | all-to-all | bytes 262144 | tf_op jit(solution)/shard_map/near_dots_sum/all_to_all | solution.py:460
  53.7 0.5 near_merge.1
  54.2 59.9 %all_to_all.21.values = bf16[32,17,2,128]{3,2,1,0:T(2,128)(2,1)S(1)} all-to-all(bf16[32,17,2,128]{3,2,1,0:T(2,128)(2,1)S(1)} %near_merge.1), channel_id=1, replica_groups=mesh['y'=4,'zh'=8,'zl'=4,'x'=4,'core'=2] {'zh','y'}, dimensions={0} | all-to-all | bytes 557056 | tf_op jit(solution)/shard_map/far_exchange/all_to_all | solution.py:460
  114.1 0.5 far_dots.1
  114.6 7.8 %all_to_all.22.parts = f32[8,8,128]{2,1,0:T(8,128)S(1)} all-to-all(f32[8,8,128]{2,1,0:T(8,128)S(1)} %get-tuple-element.16), channel_id=1, replica_groups=mesh['y'=4,'zh'=8,'zl'=4,'x'=4,'core'=2] {'x','core'}, dimensions={0} | all-to-all | bytes 65536 | tf_op jit(solution)/shard_map/far_dots_sum/all_to_all | solution.py:460
  122.4 18.7 %all_to_all.23.parts = f32[16,8,128]{2,1,0:T(8,128)S(1)} all-to-all(f32[16,8,128]{2,1,0:T(8,128)S(1)} %total_of.2), channel_id=1, replica_groups=mesh['y'=4,'zh'=8,'zl'=4,'x'=4,'core'=2] {'y','zl'}, dimensions={0} | all-to-all | bytes 131072 | tf_op jit(solution)/shard_map/far_dots_sum/all_to_all | solution.py:460
  141.1 21.0 %psum.7.dots = f32[8,128]{1,0:T(8,128)S(1)} all-reduce(f32[8,128]{1,0:T(8,128)S(1)} %bitcast.5), channel_id=1, replica_groups=mesh['y'=4,'zh'=8,'zl'=4,'x'=4,'core'=2] {'zh'}, use_global_device_ids=true, to_apply=%region_0.0 | all-reduce | flops 1024 | bytes 8192 | tf_op jit(solution)/shard_map/far_dots_sum/psum | solution.py:485
  162.1 1.5 far_merge.1
  (2 shorter events, 0.0 us)
Async XLA Ops:
  3.3 36.3 %collective-permute-start = (bf16[1024,128]{1,0:T(8,128)(2,1)S(1)}, bf16[1024,128]{1,0:T(8,128)(2,1)S(1)}, u32[]{:S(2)}, u32[]{:S(2)}) collective-permute-start(bf16[1024,128]{1,0:T(8,128)(2,1)S(1)} %get-tuple-element.11), channel_id=1, source_target_pairs={{0,24},{8,16},{16,8},{24,0},{1,25},{9,17},{17,9},{25,1},{2,26},{10... | collective-permute-start | bytes 786440 | tf_op jit(solution)/shard_map/near_exchange/ppermute | solution.py:456
  9.8 29.8 %collective-permute-start.1 = (bf16[1024,128]{1,0:T(8,128)(2,1)S(1)}, bf16[1024,128]{1,0:T(8,128)(2,1)S(1)}, u32[]{:S(2)}, u32[]{:S(2)}) collective-permute-start(bf16[1024,128]{1,0:T(8,128)(2,1)S(1)} %get-tuple-element.12), channel_id=1, source_target_pairs={{0,16},{8,24},{16,0},{24,8},{1,17},{9,25},{17,1},{25,9},{2,18},{10... | collective-permute-start | bytes 786440 | tf_op jit(solution)/shard_map/near_exchange/ppermute | solution.py:456
  11.7 27.9 %collective-permute-start.2 = (bf16[1024,128]{1,0:T(8,128)(2,1)S(1)}, bf16[1024,128]{1,0:T(8,128)(2,1)S(1)}, u32[]{:S(2)}, u32[]{:S(2)}) collective-permute-start(bf16[1024,128]{1,0:T(8,128)(2,1)S(1)} %get-tuple-element.13), channel_id=1, source_target_pairs={{0,8},{8,0},{16,24},{24,16},{1,9},{9,1},{17,25},{25,17},{2,10},{10... | collective-permute-start | bytes 786440 | tf_op jit(solution)/shard_map/near_exchange/ppermute | solution.py:456

commit v9 on v8

--- a/solution.py
+++ b/solution.py
@@ -32,6 +32,11 @@
 
 def factor(cross, own_sq):
     return 1.0 - cross / (2.0 * (jnp.maximum(own_sq, 0.0) + eps_merge))
+
+
+def within(cross, low_sq, high_sq):
+    most = jnp.sqrt(jnp.maximum(low_sq, 0.0)) * jnp.sqrt(jnp.maximum(high_sq, 0.0))
+    return jnp.clip(cross, -most, most)
 
 
 def grads_kernel(
@@ -235,6 +240,7 @@
     cross = low[0] * (high[0] * dots[0][2] + high[1] * dots[0][3]) + low[1] * (
         high[0] * dots[1][2] + high[1] * dots[1][3]
     )
+    cross = within(cross, low_sq, high_sq)
     of_low = factor(cross, low_sq)
     of_high = factor(cross, high_sq)
     square = (
@@ -405,7 +411,10 @@
         own_part = 2.0 * own_part + square_row
         own_sq = jnp.sum(jnp.where(same, own_part, 0.0), axis=1, keepdims=True)
         cross = jnp.sum(jnp.where(pair, cross_part, 0.0), axis=1, keepdims=True)
-        scale = factor(cross, own_sq)
+        other_sq = jnp.sum(
+            jnp.where(same, 0.0, jnp.where(pair, own_part, 0.0)), axis=1, keepdims=True
+        )
+        scale = factor(within(cross, own_sq, other_sq), own_sq)
         share = share * scale
         if level < 4:
             scale_row = jnp.sum(jnp.where(row == lane, scale, 0.0), axis=0, keepdims=True)

time: 164 us -> 164 us (level)
  no operation moved by 1% of the time
where the time goes in v9:
time: 164 us
  blocking collectives  144 us (88%)
  starting transfers between devices  10.9 us (7%)
  Pallas kernels  8.2 us (5%)
    all_to_all x4, blocking collectives, exchanged(): return lax.all_to_all(x, axes, 0, 0)  99.8 us
    all_gather x2, blocking collectives, body(): gain_parts = lax.all_gather(lax.all_gather(gain, 'core'), 'x')  23 us
    psum x1, blocking collectives, body(): dots = lax.psum(dots[0], 'zh')  21 us
    ppermute x3, starting transfers between devices, paired(): lax.ppermute(x, axis, [(i, i ^ apart) for i in range(lax.axis_size(axis))])  10.9 us
  transfers between devices with their start and end apart: 3, of which 0 were waited for; matrix products, arithmetic and copies ran while one was open for 0% of the time, Pallas kernels for 1%

profile of v9, /device:TPU:2, one launch (start us, length us, event | category | flops | bytes accessed | tf_op | source)
XLA Modules:
  0.0 163.6 jit_solution(11703343881513059639)
XLA Ops:
  0.6 2.6 %local_grads.1 = (bf16[1024,128]{1,0:T(8,128)(2,1)S(1)}, bf16[1024,128]{1,0:T(8,128)(2,1)S(1)}, bf16[1024,128]{1,0:T(8,128)(2,1)S(1)}, bf16[1024,128]{1,0:T(8,128)(2,1)S(1)}, f32[256,128]{1,0:T(8,128)S(1)}) custom-call(s32[1]{0:T(128)} %bitcast.place, bf16[256,4096]{1,0:T(8,128)(2,1)} %hidden_hbm.3, bf16[256,128]{1,0:T(8,128)(2,1)} %cot_hbm.3, f32[32,128]{1,0:T(8,128)} %bitcast.7), custom_call_target="tpu_custom_call" | custom-call | tf_op jit(solution)/shard_map/local_grads/pallas_call | solution.py:96
  3.3 6.5 %collective-permute-start = (bf16[1024,128]{1,0:T(8,128)(2,1)S(1)}, bf16[1024,128]{1,0:T(8,128)(2,1)S(1)}, u32[]{:S(2)}, u32[]{:S(2)}) collective-permute-start(bf16[1024,128]{1,0:T(8,128)(2,1)S(1)} %get-tuple-element.11), channel_id=1, source_target_pairs={{0,24},{8,16},{16,8},{24,0},{1,25},{9,17},{17,9},{25,1},{2,26},{10... | collective-permute-start | bytes 786440 | tf_op jit(solution)/shard_map/near_exchange/ppermute | solution.py:465
  9.8 1.9 %collective-permute-start.1 = (bf16[1024,128]{1,0:T(8,128)(2,1)S(1)}, bf16[1024,128]{1,0:T(8,128)(2,1)S(1)}, u32[]{:S(2)}, u32[]{:S(2)}) collective-permute-start(bf16[1024,128]{1,0:T(8,128)(2,1)S(1)} %get-tuple-element.12), channel_id=1, source_target_pairs={{0,16},{8,24},{16,0},{24,8},{1,17},{9,25},{17,1},{25,9},{2,18},{10... | collective-permute-start | bytes 786440 | tf_op jit(solution)/shard_map/near_exchange/ppermute | solution.py:465
  11.7 2.5 %collective-permute-start.2 = (bf16[1024,128]{1,0:T(8,128)(2,1)S(1)}, bf16[1024,128]{1,0:T(8,128)(2,1)S(1)}, u32[]{:S(2)}, u32[]{:S(2)}) collective-permute-start(bf16[1024,128]{1,0:T(8,128)(2,1)S(1)} %get-tuple-element.13), channel_id=1, source_target_pairs={{0,8},{8,0},{16,24},{24,16},{1,9},{9,1},{17,25},{25,17},{2,10},{10... | collective-permute-start | bytes 786440 | tf_op jit(solution)/shard_map/near_exchange/ppermute | solution.py:465
  14.2 2.4 %local_gains.1 = f32[32,128]{1,0:T(8,128)S(1)} custom-call(bf16[256,4096]{1,0:T(8,128)(2,1)} %hidden_hbm.3, bf16[256,128]{1,0:T(8,128)(2,1)} %cot_hbm.3, bf16[4096,128]{1,0:T(8,128)(2,1)} %weight_hbm.1, f32[256,128]{1,0:T(8,128)S(1)} %get-tuple-element.15.inv_wide), custom_call_target="tpu_custom_call" | custom-call | flops 268435456 | bytes 3145728 | tf_op jit(solution)/shard_map/gain_parts/local_gains/pallas_call | solution.py:153
  16.6 1.8 %all-gather = f32[64,128]{1,0:T(8,128)S(1)} all-gather(f32[32,128]{1,0:T(8,128)S(1)} %local_gains.1), channel_id=2, replica_groups=mesh['y'=4,'zh'=8,'zl'=4,'x'=4,'core'=2] {'core'}, dimensions={0}, use_global_device_ids=true | all-gather | bytes 49152 | tf_op jit(solution)/shard_map/gain_parts/all_gather | solution.py:481
  18.4 21.1 %all-gather.1.gain_parts = f32[8,32,128]{2,1,0:T(8,128)S(1)} all-gather(f32[2,32,128]{2,1,0:T(8,128)S(1)} %bitcast.6), channel_id=3, replica_groups=mesh['y'=4,'zh'=8,'zl'=4,'x'=4,'core'=2] {'x'}, dimensions={0}, use_global_device_ids=true | all-gather | bytes 163840 | tf_op jit(solution)/shard_map/gain_parts/all_gather | solution.py:481
  39.6 0.0 collective-permute-done.p3
  39.6 0.0 collective-permute-done.1.p2
  39.6 0.0 collective-permute-done.2.p1
  39.6 0.7 near_dots.1
  40.2 13.4 %all_to_all.20.messages = f32[32,8,128]{2,1,0:T(8,128)S(1)} all-to-all(f32[32,8,128]{2,1,0:T(8,128)S(1)} %near_dots.1), channel_id=1, replica_groups=mesh['y'=4,'zh'=8,'zl'=4,'x'=4,'core'=2] {'zl','x','core'}, dimensions={0} | all-to-all | bytes 262144 | tf_op jit(solution)/shard_map/near_dots_sum/all_to_all | solution.py:469
  53.7 0.5 near_merge.1
  54.2 59.9 %all_to_all.21.values = bf16[32,17,2,128]{3,2,1,0:T(2,128)(2,1)S(1)} all-to-all(bf16[32,17,2,128]{3,2,1,0:T(2,128)(2,1)S(1)} %near_merge.1), channel_id=1, replica_groups=mesh['y'=4,'zh'=8,'zl'=4,'x'=4,'core'=2] {'zh','y'}, dimensions={0} | all-to-all | bytes 557056 | tf_op jit(solution)/shard_map/far_exchange/all_to_all | solution.py:469
  114.1 0.5 far_dots.1
  114.6 7.8 %all_to_all.22.parts = f32[8,8,128]{2,1,0:T(8,128)S(1)} all-to-all(f32[8,8,128]{2,1,0:T(8,128)S(1)} %get-tuple-element.16), channel_id=1, replica_groups=mesh['y'=4,'zh'=8,'zl'=4,'x'=4,'core'=2] {'x','core'}, dimensions={0} | all-to-all | bytes 65536 | tf_op jit(solution)/shard_map/far_dots_sum/all_to_all | solution.py:469
  122.4 18.7 %all_to_all.23.parts = f32[16,8,128]{2,1,0:T(8,128)S(1)} all-to-all(f32[16,8,128]{2,1,0:T(8,128)S(1)} %total_of.2), channel_id=1, replica_groups=mesh['y'=4,'zh'=8,'zl'=4,'x'=4,'core'=2] {'y','zl'}, dimensions={0} | all-to-all | bytes 131072 | tf_op jit(solution)/shard_map/far_dots_sum/all_to_all | solution.py:469
  141.1 21.0 %psum.7.dots = f32[8,128]{1,0:T(8,128)S(1)} all-reduce(f32[8,128]{1,0:T(8,128)S(1)} %bitcast.5), channel_id=1, replica_groups=mesh['y'=4,'zh'=8,'zl'=4,'x'=4,'core'=2] {'zh'}, use_global_device_ids=true, to_apply=%region_0.0 | all-reduce | flops 1024 | bytes 8192 | tf_op jit(solution)/shard_map/far_dots_sum/psum | solution.py:494
  162.1 1.5 far_merge.1
  (2 shorter events, 0.0 us)
Async XLA Ops:
  3.3 36.3 %collective-permute-start = (bf16[1024,128]{1,0:T(8,128)(2,1)S(1)}, bf16[1024,128]{1,0:T(8,128)(2,1)S(1)}, u32[]{:S(2)}, u32[]{:S(2)}) collective-permute-start(bf16[1024,128]{1,0:T(8,128)(2,1)S(1)} %get-tuple-element.11), channel_id=1, source_target_pairs={{0,24},{8,16},{16,8},{24,0},{1,25},{9,17},{17,9},{25,1},{2,26},{10... | collective-permute-start | bytes 786440 | tf_op jit(solution)/shard_map/near_exchange/ppermute | solution.py:465
  9.8 29.8 %collective-permute-start.1 = (bf16[1024,128]{1,0:T(8,128)(2,1)S(1)}, bf16[1024,128]{1,0:T(8,128)(2,1)S(1)}, u32[]{:S(2)}, u32[]{:S(2)}) collective-permute-start(bf16[1024,128]{1,0:T(8,128)(2,1)S(1)} %get-tuple-element.12), channel_id=1, source_target_pairs={{0,16},{8,24},{16,0},{24,8},{1,17},{9,25},{17,1},{25,9},{2,18},{10... | collective-permute-start | bytes 786440 | tf_op jit(solution)/shard_map/near_exchange/ppermute | solution.py:465
  11.7 27.9 %collective-permute-start.2 = (bf16[1024,128]{1,0:T(8,128)(2,1)S(1)}, bf16[1024,128]{1,0:T(8,128)(2,1)S(1)}, u32[]{:S(2)}, u32[]{:S(2)}) collective-permute-start(bf16[1024,128]{1,0:T(8,128)(2,1)S(1)} %get-tuple-element.13), channel_id=1, source_target_pairs={{0,8},{8,0},{16,24},{24,16},{1,9},{9,1},{17,25},{25,17},{2,10},{10... | collective-permute-start | bytes 786440 | tf_op jit(solution)/shard_map/near_exchange/ppermute | solution.py:465

commit v10 on v9

--- a/solution.py
+++ b/solution.py
@@ -374,7 +374,7 @@
         ],
         in_specs=[VMEM_SPEC],
         out_specs=[VMEM_SPEC] * 2,
-        scratch_shapes=[pltpu.VMEM((FAR * (PIECE + 8), LANES), f32)],
+        scratch_shapes=[pltpu.VMEM(((FAR + 1) * (PIECE + 8), LANES), f32)],
         compiler_params=PARAMS,
         name="far_dots",
     )(values)

time: 164 us -> 164 us (level)
  no operation moved by 1% of the time
where the time goes in v10:
time: 164 us
  blocking collectives  144 us (88%)
  starting transfers between devices  10.9 us (7%)
  Pallas kernels  8.2 us (5%)
    all_to_all x4, blocking collectives, exchanged(): return lax.all_to_all(x, axes, 0, 0)  99.8 us
    all_gather x2, blocking collectives, body(): gain_parts = lax.all_gather(lax.all_gather(gain, 'core'), 'x')  23 us
    psum x1, blocking collectives, body(): dots = lax.psum(dots[0], 'zh')  21 us
    ppermute x3, starting transfers between devices, paired(): lax.ppermute(x, axis, [(i, i ^ apart) for i in range(lax.axis_size(axis))])  10.9 us
  transfers between devices with their start and end apart: 3, of which 0 were waited for; matrix products, arithmetic and copies ran while one was open for 0% of the time, Pallas kernels for 1%

profile of v10, /device:TPU:2, one launch (start us, length us, event | category | flops | bytes accessed | tf_op | source)
XLA Modules:
  0.0 163.6 jit_solution(5198067251724255679)
XLA Ops:
  0.6 2.6 %local_grads.1 = (bf16[1024,128]{1,0:T(8,128)(2,1)S(1)}, bf16[1024,128]{1,0:T(8,128)(2,1)S(1)}, bf16[1024,128]{1,0:T(8,128)(2,1)S(1)}, bf16[1024,128]{1,0:T(8,128)(2,1)S(1)}, f32[256,128]{1,0:T(8,128)S(1)}) custom-call(s32[1]{0:T(128)} %bitcast.place, bf16[256,4096]{1,0:T(8,128)(2,1)} %hidden_hbm.3, bf16[256,128]{1,0:T(8,128)(2,1)} %cot_hbm.3, f32[32,128]{1,0:T(8,128)} %bitcast.7), custom_call_target="tpu_custom_call" | custom-call | tf_op jit(solution)/shard_map/local_grads/pallas_call | solution.py:96
  3.3 6.5 %collective-permute-start = (bf16[1024,128]{1,0:T(8,128)(2,1)S(1)}, bf16[1024,128]{1,0:T(8,128)(2,1)S(1)}, u32[]{:S(2)}, u32[]{:S(2)}) collective-permute-start(bf16[1024,128]{1,0:T(8,128)(2,1)S(1)} %get-tuple-element.11), channel_id=1, source_target_pairs={{0,24},{8,16},{16,8},{24,0},{1,25},{9,17},{17,9},{25,1},{2,26},{10... | collective-permute-start | bytes 786440 | tf_op jit(solution)/shard_map/near_exchange/ppermute | solution.py:465
  9.8 1.9 %collective-permute-start.1 = (bf16[1024,128]{1,0:T(8,128)(2,1)S(1)}, bf16[1024,128]{1,0:T(8,128)(2,1)S(1)}, u32[]{:S(2)}, u32[]{:S(2)}) collective-permute-start(bf16[1024,128]{1,0:T(8,128)(2,1)S(1)} %get-tuple-element.12), channel_id=1, source_target_pairs={{0,16},{8,24},{16,0},{24,8},{1,17},{9,25},{17,1},{25,9},{2,18},{10... | collective-permute-start | bytes 786440 | tf_op jit(solution)/shard_map/near_exchange/ppermute | solution.py:465
  11.7 2.5 %collective-permute-start.2 = (bf16[1024,128]{1,0:T(8,128)(2,1)S(1)}, bf16[1024,128]{1,0:T(8,128)(2,1)S(1)}, u32[]{:S(2)}, u32[]{:S(2)}) collective-permute-start(bf16[1024,128]{1,0:T(8,128)(2,1)S(1)} %get-tuple-element.13), channel_id=1, source_target_pairs={{0,8},{8,0},{16,24},{24,16},{1,9},{9,1},{17,25},{25,17},{2,10},{10... | collective-permute-start | bytes 786440 | tf_op jit(solution)/shard_map/near_exchange/ppermute | solution.py:465
  14.2 2.4 %local_gains.1 = f32[32,128]{1,0:T(8,128)S(1)} custom-call(bf16[256,4096]{1,0:T(8,128)(2,1)} %hidden_hbm.3, bf16[256,128]{1,0:T(8,128)(2,1)} %cot_hbm.3, bf16[4096,128]{1,0:T(8,128)(2,1)} %weight_hbm.1, f32[256,128]{1,0:T(8,128)S(1)} %get-tuple-element.15.inv_wide), custom_call_target="tpu_custom_call" | custom-call | flops 268435456 | bytes 3145728 | tf_op jit(solution)/shard_map/gain_parts/local_gains/pallas_call | solution.py:153
  16.6 1.8 %all-gather = f32[64,128]{1,0:T(8,128)S(1)} all-gather(f32[32,128]{1,0:T(8,128)S(1)} %local_gains.1), channel_id=2, replica_groups=mesh['y'=4,'zh'=8,'zl'=4,'x'=4,'core'=2] {'core'}, dimensions={0}, use_global_device_ids=true | all-gather | bytes 49152 | tf_op jit(solution)/shard_map/gain_parts/all_gather | solution.py:481
  18.4 21.1 %all-gather.1.gain_parts = f32[8,32,128]{2,1,0:T(8,128)S(1)} all-gather(f32[2,32,128]{2,1,0:T(8,128)S(1)} %bitcast.6), channel_id=3, replica_groups=mesh['y'=4,'zh'=8,'zl'=4,'x'=4,'core'=2] {'x'}, dimensions={0}, use_global_device_ids=true | all-gather | bytes 163840 | tf_op jit(solution)/shard_map/gain_parts/all_gather | solution.py:481
  39.6 0.0 collective-permute-done.p3
  39.6 0.0 collective-permute-done.1.p2
  39.6 0.0 collective-permute-done.2.p1
  39.6 0.7 near_dots.1
  40.2 13.4 %all_to_all.20.messages = f32[32,8,128]{2,1,0:T(8,128)S(1)} all-to-all(f32[32,8,128]{2,1,0:T(8,128)S(1)} %near_dots.1), channel_id=1, replica_groups=mesh['y'=4,'zh'=8,'zl'=4,'x'=4,'core'=2] {'zl','x','core'}, dimensions={0} | all-to-all | bytes 262144 | tf_op jit(solution)/shard_map/near_dots_sum/all_to_all | solution.py:469
  53.7 0.5 near_merge.1
  54.2 59.9 %all_to_all.21.values = bf16[32,17,2,128]{3,2,1,0:T(2,128)(2,1)S(1)} all-to-all(bf16[32,17,2,128]{3,2,1,0:T(2,128)(2,1)S(1)} %near_merge.1), channel_id=1, replica_groups=mesh['y'=4,'zh'=8,'zl'=4,'x'=4,'core'=2] {'zh','y'}, dimensions={0} | all-to-all | bytes 557056 | tf_op jit(solution)/shard_map/far_exchange/all_to_all | solution.py:469
  114.1 0.5 far_dots.1
  114.6 7.8 %all_to_all.22.parts = f32[8,8,128]{2,1,0:T(8,128)S(1)} all-to-all(f32[8,8,128]{2,1,0:T(8,128)S(1)} %get-tuple-element.16), channel_id=1, replica_groups=mesh['y'=4,'zh'=8,'zl'=4,'x'=4,'core'=2] {'x','core'}, dimensions={0} | all-to-all | bytes 65536 | tf_op jit(solution)/shard_map/far_dots_sum/all_to_all | solution.py:469
  122.4 18.7 %all_to_all.23.parts = f32[16,8,128]{2,1,0:T(8,128)S(1)} all-to-all(f32[16,8,128]{2,1,0:T(8,128)S(1)} %total_of.2), channel_id=1, replica_groups=mesh['y'=4,'zh'=8,'zl'=4,'x'=4,'core'=2] {'y','zl'}, dimensions={0} | all-to-all | bytes 131072 | tf_op jit(solution)/shard_map/far_dots_sum/all_to_all | solution.py:469
  141.1 21.0 %psum.7.dots = f32[8,128]{1,0:T(8,128)S(1)} all-reduce(f32[8,128]{1,0:T(8,128)S(1)} %bitcast.5), channel_id=1, replica_groups=mesh['y'=4,'zh'=8,'zl'=4,'x'=4,'core'=2] {'zh'}, use_global_device_ids=true, to_apply=%region_0.0 | all-reduce | flops 1024 | bytes 8192 | tf_op jit(solution)/shard_map/far_dots_sum/psum | solution.py:494
  162.1 1.5 far_merge.1
  (2 shorter events, 0.0 us)
Async XLA Ops:
  3.3 36.3 %collective-permute-start = (bf16[1024,128]{1,0:T(8,128)(2,1)S(1)}, bf16[1024,128]{1,0:T(8,128)(2,1)S(1)}, u32[]{:S(2)}, u32[]{:S(2)}) collective-permute-start(bf16[1024,128]{1,0:T(8,128)(2,1)S(1)} %get-tuple-element.11), channel_id=1, source_target_pairs={{0,24},{8,16},{16,8},{24,0},{1,25},{9,17},{17,9},{25,1},{2,26},{10... | collective-permute-start | bytes 786440 | tf_op jit(solution)/shard_map/near_exchange/ppermute | solution.py:465
  9.8 29.8 %collective-permute-start.1 = (bf16[1024,128]{1,0:T(8,128)(2,1)S(1)}, bf16[1024,128]{1,0:T(8,128)(2,1)S(1)}, u32[]{:S(2)}, u32[]{:S(2)}) collective-permute-start(bf16[1024,128]{1,0:T(8,128)(2,1)S(1)} %get-tuple-element.12), channel_id=1, source_target_pairs={{0,16},{8,24},{16,0},{24,8},{1,17},{9,25},{17,1},{25,9},{2,18},{10... | collective-permute-start | bytes 786440 | tf_op jit(solution)/shard_map/near_exchange/ppermute | solution.py:465
  11.7 27.9 %collective-permute-start.2 = (bf16[1024,128]{1,0:T(8,128)(2,1)S(1)}, bf16[1024,128]{1,0:T(8,128)(2,1)S(1)}, u32[]{:S(2)}, u32[]{:S(2)}) collective-permute-start(bf16[1024,128]{1,0:T(8,128)(2,1)S(1)} %get-tuple-element.13), channel_id=1, source_target_pairs={{0,8},{8,0},{16,24},{24,16},{1,9},{9,1},{17,25},{25,17},{2,10},{10... | collective-permute-start | bytes 786440 | tf_op jit(solution)/shard_map/near_exchange/ppermute | solution.py:465

commit v11 on v10

--- a/solution.py
+++ b/solution.py
@@ -489,8 +489,8 @@
         values = exchanged(values, ("zh", "y"))
     dots, last = far_dots(values)
     with jax.named_scope("far_dots_sum"):
-        dots = total_of(exchanged(dots, ("x", "core")), 4 * NEAR)
-        dots = total_of(exchanged(dots, ("y", "zl")), 1)
+        dots = total_of(exchanged(dots, ("y", "core")), 4 * NEAR)
+        dots = total_of(exchanged(dots, ("zl", "x")), 1)
         dots = lax.psum(dots[0], "zh")
     merged_key, merged_gain = far_merge(place, dots, values, last)
     return (merged_key, merged_gain.reshape(PIECE))

time: 164 us -> 164 us (level)
  no operation moved by 1% of the time
where the time goes in v11:
time: 164 us
  blocking collectives  144 us (88%)
  starting transfers between devices  10.9 us (7%)
  Pallas kernels  8.2 us (5%)
    all_to_all x4, blocking collectives, exchanged(): return lax.all_to_all(x, axes, 0, 0)  100 us
    all_gather x2, blocking collectives, body(): gain_parts = lax.all_gather(lax.all_gather(gain, 'core'), 'x')  23 us
    psum x1, blocking collectives, body(): dots = lax.psum(dots[0], 'zh')  20.8 us
    ppermute x3, starting transfers between devices, paired(): lax.ppermute(x, axis, [(i, i ^ apart) for i in range(lax.axis_size(axis))])  10.9 us
  transfers between devices with their start and end apart: 3, of which 0 were waited for; matrix products, arithmetic and copies ran while one was open for 0% of the time, Pallas kernels for 1%

profile of v11, /device:TPU:2, one launch (start us, length us, event | category | flops | bytes accessed | tf_op | source)
XLA Modules:
  0.0 163.7 jit_solution(4540812270880962354)
XLA Ops:
  0.6 2.6 %local_grads.1 = (bf16[1024,128]{1,0:T(8,128)(2,1)S(1)}, bf16[1024,128]{1,0:T(8,128)(2,1)S(1)}, bf16[1024,128]{1,0:T(8,128)(2,1)S(1)}, bf16[1024,128]{1,0:T(8,128)(2,1)S(1)}, f32[256,128]{1,0:T(8,128)S(1)}) custom-call(s32[1]{0:T(128)} %bitcast.place, bf16[256,4096]{1,0:T(8,128)(2,1)} %hidden_hbm.3, bf16[256,128]{1,0:T(8,128)(2,1)} %cot_hbm.3, f32[32,128]{1,0:T(8,128)} %bitcast.7), custom_call_target="tpu_custom_call" | custom-call | tf_op jit(solution)/shard_map/local_grads/pallas_call | solution.py:96
  3.3 6.5 %collective-permute-start = (bf16[1024,128]{1,0:T(8,128)(2,1)S(1)}, bf16[1024,128]{1,0:T(8,128)(2,1)S(1)}, u32[]{:S(2)}, u32[]{:S(2)}) collective-permute-start(bf16[1024,128]{1,0:T(8,128)(2,1)S(1)} %get-tuple-element.11), channel_id=1, source_target_pairs={{0,24},{8,16},{16,8},{24,0},{1,25},{9,17},{17,9},{25,1},{2,26},{10... | collective-permute-start | bytes 786440 | tf_op jit(solution)/shard_map/near_exchange/ppermute | solution.py:465
  9.8 1.9 %collective-permute-start.1 = (bf16[1024,128]{1,0:T(8,128)(2,1)S(1)}, bf16[1024,128]{1,0:T(8,128)(2,1)S(1)}, u32[]{:S(2)}, u32[]{:S(2)}) collective-permute-start(bf16[1024,128]{1,0:T(8,128)(2,1)S(1)} %get-tuple-element.12), channel_id=1, source_target_pairs={{0,16},{8,24},{16,0},{24,8},{1,17},{9,25},{17,1},{25,9},{2,18},{10... | collective-permute-start | bytes 786440 | tf_op jit(solution)/shard_map/near_exchange/ppermute | solution.py:465
  11.7 2.5 %collective-permute-start.2 = (bf16[1024,128]{1,0:T(8,128)(2,1)S(1)}, bf16[1024,128]{1,0:T(8,128)(2,1)S(1)}, u32[]{:S(2)}, u32[]{:S(2)}) collective-permute-start(bf16[1024,128]{1,0:T(8,128)(2,1)S(1)} %get-tuple-element.13), channel_id=1, source_target_pairs={{0,8},{8,0},{16,24},{24,16},{1,9},{9,1},{17,25},{25,17},{2,10},{10... | collective-permute-start | bytes 786440 | tf_op jit(solution)/shard_map/near_exchange/ppermute | solution.py:465
  14.2 2.4 %local_gains.1 = f32[32,128]{1,0:T(8,128)S(1)} custom-call(bf16[256,4096]{1,0:T(8,128)(2,1)} %hidden_hbm.3, bf16[256,128]{1,0:T(8,128)(2,1)} %cot_hbm.3, bf16[4096,128]{1,0:T(8,128)(2,1)} %weight_hbm.1, f32[256,128]{1,0:T(8,128)S(1)} %get-tuple-element.15.inv_wide), custom_call_target="tpu_custom_call" | custom-call | flops 268435456 | bytes 3145728 | tf_op jit(solution)/shard_map/gain_parts/local_gains/pallas_call | solution.py:153
  16.6 1.8 %all-gather = f32[64,128]{1,0:T(8,128)S(1)} all-gather(f32[32,128]{1,0:T(8,128)S(1)} %local_gains.1), channel_id=2, replica_groups=mesh['y'=4,'zh'=8,'zl'=4,'x'=4,'core'=2] {'core'}, dimensions={0}, use_global_device_ids=true | all-gather | bytes 49152 | tf_op jit(solution)/shard_map/gain_parts/all_gather | solution.py:481
  18.4 21.1 %all-gather.1.gain_parts = f32[8,32,128]{2,1,0:T(8,128)S(1)} all-gather(f32[2,32,128]{2,1,0:T(8,128)S(1)} %bitcast.6), channel_id=3, replica_groups=mesh['y'=4,'zh'=8,'zl'=4,'x'=4,'core'=2] {'x'}, dimensions={0}, use_global_device_ids=true | all-gather | bytes 163840 | tf_op jit(solution)/shard_map/gain_parts/all_gather | solution.py:481
  39.6 0.0 collective-permute-done.p3
  39.6 0.0 collective-permute-done.1.p2
  39.6 0.0 collective-permute-done.2.p1
  39.6 0.7 near_dots.1
  40.2 13.4 %all_to_all.20.messages = f32[32,8,128]{2,1,0:T(8,128)S(1)} all-to-all(f32[32,8,128]{2,1,0:T(8,128)S(1)} %near_dots.1), channel_id=1, replica_groups=mesh['y'=4,'zh'=8,'zl'=4,'x'=4,'core'=2] {'zl','x','core'}, dimensions={0} | all-to-all | bytes 262144 | tf_op jit(solution)/shard_map/near_dots_sum/all_to_all | solution.py:469
  53.7 0.5 near_merge.1
  54.2 59.9 %all_to_all.21.values = bf16[32,17,2,128]{3,2,1,0:T(2,128)(2,1)S(1)} all-to-all(bf16[32,17,2,128]{3,2,1,0:T(2,128)(2,1)S(1)} %near_merge.1), channel_id=1, replica_groups=mesh['y'=4,'zh'=8,'zl'=4,'x'=4,'core'=2] {'zh','y'}, dimensions={0} | all-to-all | bytes 557056 | tf_op jit(solution)/shard_map/far_exchange/all_to_all | solution.py:469
  114.1 0.5 far_dots.1
  114.6 9.0 %all_to_all.22.parts = f32[8,8,128]{2,1,0:T(8,128)S(1)} all-to-all(f32[8,8,128]{2,1,0:T(8,128)S(1)} %get-tuple-element.16), channel_id=1, replica_groups=mesh['y'=4,'zh'=8,'zl'=4,'x'=4,'core'=2] {'y','core'}, dimensions={0} | all-to-all | bytes 65536 | tf_op jit(solution)/shard_map/far_dots_sum/all_to_all | solution.py:469
  123.6 17.7 %all_to_all.23.parts = f32[16,8,128]{2,1,0:T(8,128)S(1)} all-to-all(f32[16,8,128]{2,1,0:T(8,128)S(1)} %total_of.2), channel_id=1, replica_groups=mesh['y'=4,'zh'=8,'zl'=4,'x'=4,'core'=2] {'zl','x'}, dimensions={0} | all-to-all | bytes 131072 | tf_op jit(solution)/shard_map/far_dots_sum/all_to_all | solution.py:469
  141.3 20.8 %psum.7.dots = f32[8,128]{1,0:T(8,128)S(1)} all-reduce(f32[8,128]{1,0:T(8,128)S(1)} %bitcast.5), channel_id=1, replica_groups=mesh['y'=4,'zh'=8,'zl'=4,'x'=4,'core'=2] {'zh'}, use_global_device_ids=true, to_apply=%region_0.0 | all-reduce | flops 1024 | bytes 8192 | tf_op jit(solution)/shard_map/far_dots_sum/psum | solution.py:494
  162.2 1.5 far_merge.1
  (2 shorter events, 0.0 us)
Async XLA Ops:
  3.3 36.3 %collective-permute-start = (bf16[1024,128]{1,0:T(8,128)(2,1)S(1)}, bf16[1024,128]{1,0:T(8,128)(2,1)S(1)}, u32[]{:S(2)}, u32[]{:S(2)}) collective-permute-start(bf16[1024,128]{1,0:T(8,128)(2,1)S(1)} %get-tuple-element.11), channel_id=1, source_target_pairs={{0,24},{8,16},{16,8},{24,0},{1,25},{9,17},{17,9},{25,1},{2,26},{10... | collective-permute-start | bytes 786440 | tf_op jit(solution)/shard_map/near_exchange/ppermute | solution.py:465
  9.8 29.8 %collective-permute-start.1 = (bf16[1024,128]{1,0:T(8,128)(2,1)S(1)}, bf16[1024,128]{1,0:T(8,128)(2,1)S(1)}, u32[]{:S(2)}, u32[]{:S(2)}) collective-permute-start(bf16[1024,128]{1,0:T(8,128)(2,1)S(1)} %get-tuple-element.12), channel_id=1, source_target_pairs={{0,16},{8,24},{16,0},{24,8},{1,17},{9,25},{17,1},{25,9},{2,18},{10... | collective-permute-start | bytes 786440 | tf_op jit(solution)/shard_map/near_exchange/ppermute | solution.py:465
  11.7 27.9 %collective-permute-start.2 = (bf16[1024,128]{1,0:T(8,128)(2,1)S(1)}, bf16[1024,128]{1,0:T(8,128)(2,1)S(1)}, u32[]{:S(2)}, u32[]{:S(2)}) collective-permute-start(bf16[1024,128]{1,0:T(8,128)(2,1)S(1)} %get-tuple-element.13), channel_id=1, source_target_pairs={{0,8},{8,0},{16,24},{24,16},{1,9},{9,1},{17,25},{25,17},{2,10},{10... | collective-permute-start | bytes 786440 | tf_op jit(solution)/shard_map/near_exchange/ppermute | solution.py:465
